TPU v7x, 512 devices: a whole 4x8x8 slice. The times are simulated.
512 devices in a mesh: ctx: 64 (over y, z), head: 8 (over x, core).
Axes of the slice: x: 4, y: 8, z: 8, core: 2. Of those that a mesh axis runs over, the one named last changes fastest.
Arguments:
- query_in: bfloat16 [12288, 1024], P('ctx', 'head'), may hold values from -18 to 18
- key_in: bfloat16 [12288, 128], P(('ctx', 'head')), may hold values from -4 to 4
- value_in: bfloat16 [12288, 128], P(('ctx', 'head')), may hold values from -6 to 6
- grad_out: bfloat16 [12288, 1024], P('ctx', 'head'), may hold values from -6 to 6
- span_of: int32 [128], replicated, may hold values from 0 to 127, as said below
Outputs:
- attn_out: bfloat16 [12288, 1024], P(('ctx', 'head'))
- grad_query: bfloat16 [12288, 1024], P(('ctx', 'head'))
- grad_key: bfloat16 [12288, 128], P(('ctx', 'head'))
- grad_value: bfloat16 [12288, 128], P(('ctx', 'head'))
Inputs may be any that keep to these rules, and one draw needn't show every extreme that they name: `span_of`: blocks 2c and 2c + 1 of 96 rows (those of context shard c) hold two spans whose numbers add up to 127; every span number occurs once.
All inputs are finite; a program needn't handle non-finite values.
Results may differ from a plain program's by a relative error of at most 0.018.
Values may be sent and summed in bfloat16 or wider, within the bound.
No kernel may reach another device: no remote copies, remote signals or barrier semaphores. Data moves between devices by JAX's collectives and lax.ppermute only.
A program may use at most 64 MiB of HBM per device.

v0:
```python
import math

import jax
import jax.numpy as jnp
from jax import lax
from jax.sharding import PartitionSpec as P


def masked_scores(queries, key_rows, key_pos, query_pos, scaling):
    scores = jnp.dot(queries, key_rows.T, preferred_element_type=jnp.float32) * scaling
    return jnp.where(key_pos[None, :] <= query_pos[:, None], scores, -jnp.inf)


def local(query_in, key_in, value_in, grad_out, span_of):
    head_dim = key_in.shape[1]
    scaling = 1.0 / math.sqrt(head_dim)
    local_rows = query_in.shape[0]
    span_len = local_rows // 2
    local_heads = query_in.shape[1] // head_dim
    key_shard, value_shard = (
        lax.all_gather(key_in, "head", axis=0, tiled=True),
        lax.all_gather(value_in, "head", axis=0, tiled=True),
    )
    keys_all, values_all = (
        lax.all_gather(key_shard, "ctx", axis=0, tiled=True),
        lax.all_gather(value_shard, "ctx", axis=0, tiled=True),
    )
    seq_len = keys_all.shape[0]
    spans = seq_len // span_len
    device = lax.axis_index("ctx")
    slot_pos = jnp.repeat(span_of, span_len) * span_len + jnp.tile(
        jnp.arange(span_len, dtype=jnp.int32), spans
    )
    first_row = device * local_rows
    own_keys = lax.dynamic_slice_in_dim(keys_all, first_row, local_rows, 0)
    own_values = lax.dynamic_slice_in_dim(values_all, first_row, local_rows, 0)
    own_pos = lax.dynamic_slice_in_dim(slot_pos, first_row, local_rows, 0)
    block_size = math.gcd(seq_len, 1024)
    block_count = seq_len // block_size
    flat_q = (
        query_in.reshape(local_rows, local_heads, head_dim).transpose(1, 0, 2).reshape(-1, head_dim)
    )
    flat_do = (
        grad_out.reshape(local_rows, local_heads, head_dim).transpose(1, 0, 2).reshape(-1, head_dim)
    )
    row_pos = jnp.tile(own_pos, local_heads)
    row_count = flat_q.shape[0]

    def block_scores(number):
        offset = number * block_size
        key_rows = lax.dynamic_slice_in_dim(keys_all, offset, block_size, 0)
        value_rows = lax.dynamic_slice_in_dim(values_all, offset, block_size, 0)
        block_pos = lax.dynamic_slice_in_dim(slot_pos, offset, block_size, 0)
        return (masked_scores(flat_q, key_rows, block_pos, row_pos, scaling), key_rows, value_rows)

    def stats_step(number, carried):
        running_max, running_sum = carried
        scores, key_rows, value_rows = block_scores(number)
        new_max = jnp.maximum(running_max, jnp.max(scores, axis=1))
        running_sum = running_sum * jnp.exp(running_max - new_max) + jnp.sum(
            jnp.exp(scores - new_max[:, None]), axis=1
        )
        return (new_max, running_sum)

    initial = (jnp.full((row_count,), -1e30, jnp.float32), jnp.zeros((row_count,), jnp.float32))
    running_max, running_sum = lax.fori_loop(0, block_count, stats_step, initial)
    log_total = running_max + jnp.log(running_sum)

    def output_step(number, carried):
        totals, delta_sum = carried
        scores, key_rows, value_rows = block_scores(number)
        probs = jnp.exp(scores - log_total[:, None]).astype(jnp.bfloat16)
        totals = totals + jnp.dot(probs, value_rows, preferred_element_type=jnp.float32)
        dprobs = jnp.dot(flat_do, value_rows.T, preferred_element_type=jnp.float32)
        delta_sum = delta_sum + jnp.sum(probs.astype(jnp.float32) * dprobs, axis=1)
        return (totals, delta_sum)

    initial = (jnp.zeros((row_count, head_dim), jnp.float32), jnp.zeros((row_count,), jnp.float32))
    totals, delta_sum = lax.fori_loop(0, block_count, output_step, initial)
    attn_flat = totals.astype(jnp.bfloat16)

    def query_grad_step(number, grad_rows):
        scores, key_rows, value_rows = block_scores(number)
        probs = jnp.exp(scores - log_total[:, None]).astype(jnp.bfloat16)
        dprobs = jnp.dot(flat_do, value_rows.T, preferred_element_type=jnp.float32)
        dscores = (probs.astype(jnp.float32) * (dprobs - delta_sum[:, None]) * scaling).astype(
            jnp.bfloat16
        )
        return grad_rows + jnp.dot(dscores, key_rows, preferred_element_type=jnp.float32)

    grad_rows = lax.fori_loop(
        0, block_count, query_grad_step, jnp.zeros((row_count, head_dim), jnp.float32)
    )
    dq_flat = grad_rows.astype(jnp.bfloat16)
    lse_rows = log_total.reshape(local_heads, local_rows).T
    delta_rows = delta_sum.reshape(local_heads, local_rows).T
    all_q, all_do = (
        lax.all_gather(query_in, "ctx", axis=0, tiled=True),
        lax.all_gather(grad_out, "ctx", axis=0, tiled=True),
    )
    all_lse, all_delta = (
        lax.all_gather(lse_rows, "ctx", axis=0, tiled=True),
        lax.all_gather(delta_rows, "ctx", axis=0, tiled=True),
    )
    lower_block = 0

    def key_grad_step(number, carried):
        grad_k, grad_v = carried
        offset = number * block_size
        queries = lax.dynamic_slice_in_dim(all_q, offset, block_size, 0).reshape(
            block_size, local_heads, head_dim
        )
        douts = lax.dynamic_slice_in_dim(all_do, offset, block_size, 0).reshape(
            block_size, local_heads, head_dim
        )
        lse_block = lax.dynamic_slice_in_dim(all_lse, offset, block_size, 0).T[:, :, None]
        delta_block = lax.dynamic_slice_in_dim(all_delta, offset, block_size, 0).T[:, :, None]
        query_pos = lax.dynamic_slice_in_dim(slot_pos, offset, block_size, 0)
        scores = (
            jnp.einsum("qhd,kd->hqk", queries, own_keys, preferred_element_type=jnp.float32)
            * scaling
        )
        scores = jnp.where(own_pos[None, None, :] <= query_pos[None, :, None], scores, -jnp.inf)
        probs = jnp.exp(scores - lse_block).astype(jnp.bfloat16)
        grad_v = grad_v + jnp.einsum(
            "hqk,qhd->kd", probs, douts, preferred_element_type=jnp.float32
        )
        dprobs = jnp.einsum("qhd,kd->hqk", douts, own_values, preferred_element_type=jnp.float32)
        dscores = (probs.astype(jnp.float32) * (dprobs - delta_block) * scaling).astype(
            jnp.bfloat16
        )
        grad_k = grad_k + jnp.einsum(
            "hqk,qhd->kd", dscores, queries, preferred_element_type=jnp.float32
        )
        return (grad_k, grad_v)

    initial = (
        jnp.zeros((local_rows, head_dim), jnp.float32),
        jnp.zeros((local_rows, head_dim), jnp.float32),
    )
    grad_k, grad_v = lax.fori_loop(lower_block, block_count, key_grad_step, initial)
    grad_k, grad_v = (
        lax.psum_scatter(grad_k, "head", scatter_dimension=0, tiled=True),
        lax.psum_scatter(grad_v, "head", scatter_dimension=0, tiled=True),
    )

    def restore(flat_rows):
        return (
            flat_rows.reshape(local_heads, local_rows, head_dim)
            .transpose(1, 0, 2)
            .reshape(local_rows, local_heads * head_dim)
        )

    attn_out, grad_query = (
        lax.all_to_all(restore(attn_flat), "head", split_axis=0, concat_axis=1, tiled=True),
        lax.all_to_all(restore(dq_flat), "head", split_axis=0, concat_axis=1, tiled=True),
    )
    return (attn_out, grad_query, grad_k.astype(jnp.bfloat16), grad_v.astype(jnp.bfloat16))


def solution(mesh):
    return jax.shard_map(
        local,
        mesh=mesh,
        in_specs=(
            P("ctx", "head"),
            P(("ctx", "head"), None),
            P(("ctx", "head"), None),
            P("ctx", "head"),
            P(),
        ),
        out_specs=(
            P(("ctx", "head"), None),
            P(("ctx", "head"), None),
            P(("ctx", "head"), None),
            P(("ctx", "head"), None),
        ),
        check_vma=False,
    )
```

profile of v0, /device:TPU:8, one launch (start us, length us, event | category | flops | bytes accessed | tf_op | source)
XLA Modules:
  0.0 653.4 jit_solution(15296140341715093202)
XLA Ops:
  7.2 14.4 %all_gather.24 = bf16[192,128]{1,0:T(8,128)(2,1)} all-gather(bf16[24,128]{1,0:T(8,128)(2,1)} %param.14), channel_id=1, replica_groups=mesh['ctx'=64,'head'=8] {'head'}, dimensions={0}, use_global_device_ids=true | all-gather | bytes 55296 | tf_op jit(solution)/shard_map/all_gather | solution.py:21
  21.6 14.0 %all_gather.26 = bf16[192,128]{1,0:T(8,128)(2,1)} all-gather(bf16[24,128]{1,0:T(8,128)(2,1)} %param.15), channel_id=1, replica_groups=mesh['ctx'=64,'head'=8] {'head'}, dimensions={0}, use_global_device_ids=true | all-gather | bytes 55296 | tf_op jit(solution)/shard_map/all_gather | solution.py:22
  40.0 70.8 %all-gather.7.cloned.1.call-done = bf16[12288,128]{1,0:T(8,128)(2,1)} async-done(((bf16[192,128]{1,0:T(8,128)(2,1)}), bf16[12288,128]{1,0:T(8,128)(2,1)}) %all-gather.7.cloned.1.call-update) | async-done | bytes 3145744 | tf_op jit(solution)/shard_map/all_gather | solution.py:25
  110.8 20.2 %while.62 = (s32[]{:T(128)}, f32[192]{0:T(256)S(1)}, f32[192]{0:T(256)S(1)}, s32[12288]{0:T(1024)S(1)}, s32[192]{0:T(256)S(1)}, /*index=5*/bf16[12288,128]{1,0:T...) while((s32[]{:T(128)}, f32[192]{0:T(256)S(1)}, ...), condition=%wide.region_3.4_spmd.clone, body=%wide.region_0.3_spmd.clone.sunk | while | flops 51512260 | bytes 1907382 | solution.py:66
  131.1 65.1 %all-gather.9.cloned.1.call-done = bf16[12288,128]{1,0:T(8,128)(2,1)} async-done(((bf16[192,128]{1,0:T(8,128)(2,1)}), bf16[12288,128]{1,0:T(8,128)(2,1)}) %all-gather.9.cloned.1.call-update) | async-done | bytes 3145744 | tf_op jit(solution)/shard_map/all_gather | solution.py:26
  196.2 46.9 %while.63 = (s32[]{:T(128)}, f32[192,128]{1,0:T(8,128)S(1)}, f32[192]{0:T(256)S(1)}, s32[12288]{0:T(1024)S(1)}, s32[192]{0:T(256)S(1)}, /*index=5*/bf16[12288,12...) while((s32[]{:T(128)}, f32[192,128]{1,0:T(8,128)S(1)}, ...), condition=%wide.region_6.7_spmd.clone, body=%wide.region_4.6_spmd.clone.sunk | while | flops 152617152 | bytes 2278102 | solution.py:79
  243.8 4.3 all-to-all-start
  248.1 33.4 %while.64 = (s32[]{:T(128)}, f32[192,128]{1,0:T(8,128)S(1)}, s32[12288]{0:T(1024)S(1)}, s32[192]{0:T(256)S(1)}, bf16[12288,128]{1,0:T(8,128)(2,1)}, /*index=5*/b...) while((s32[]{:T(128)}, f32[192,128]{1,0:T(8,128)S(1)}, ...), condition=%wide.region_8.9_spmd.clone, body=%wide.region_7.8_spmd.clone.sunk | while | flops 153010176 | bytes 2670540 | solution.py:91
  252.2 1.5 fusion.122
  257.8 1.5 fusion.122
  260.6 1.5 fusion.122
  263.4 1.5 fusion.122
  268.9 1.5 fusion.122
  271.7 1.5 fusion.122
  277.3 1.5 fusion.122
  284.7 82.4 %all-gather.13.cloned.1.call-done = bf16[12288,128]{1,0:T(8,128)(2,1)} async-done(((bf16[192,128]{1,0:T(8,128)(2,1)}), bf16[12288,128]{1,0:T(8,128)(2,1)}) %all-gather.13.cloned.1.call-update) | async-done | bytes 3145744 | tf_op jit(solution)/shard_map/all_gather | solution.py:99
  367.1 151.2 %all-reduce.7.cloned.1.call-done = (f32[12288]{0:T(1024)}, f32[12288]{0:T(1024)}) async-done(((f32[12288]{0:T(1024)}, f32[12288]{0:T(1024)}), (f32[12288]{0:T(1024)}, f32[12288]{0:T(1024)})) %all-reduce.7.cloned.1.call-update) | async-done | bytes 98320
  518.2 56.5 %while.65 = (s32[]{:T(128)}, f32[192,128]{1,0:T(8,128)S(1)}, f32[192,128]{1,0:T(8,128)S(1)}, s32[192]{0:T(256)S(1)}, s32[12288]{0:T(1024)S(1)}, /*index=5*/bf16[...) while((s32[]{:T(128)}, f32[192,128]{1,0:T(8,128)S(1)}, ...), condition=%wide.region_10.11_spmd.clone, body=%wide.region_9.10_spmd.clone.sunk | while | flops 203390976 | bytes 2759133 | solution.py:141
  534.3 1.5 convolution_add_fusion.7
  543.7 1.5 convolution_add_fusion.7
  575.4 4.3 all-to-all-start.1
  580.4 4.8 all-to-all-done.1
  585.8 22.1 %reduce-scatter.7.cloned.1.call-done = f32[24,128]{1,0:T(8,128)} async-done(((f32[192,128]{1,0:T(8,128)}), f32[24,128]{1,0:T(8,128)}) %reduce-scatter.7.cloned.1.call-update) | async-done | bytes 12304
  609.2 36.1 %reduce-scatter.9.cloned.1.call-done = f32[24,128]{1,0:T(8,128)} async-done(((f32[192,128]{1,0:T(8,128)}), f32[24,128]{1,0:T(8,128)}) %reduce-scatter.9.cloned.1.call-update) | async-done | bytes 12304
  (269 shorter events, 153.7 us)
Async XLA Ops:
  7.2 103.6 %all-gather.7.cloned.1.call-start = ((), (), s32[]{:S(2)}) async-start(), calls=%async_computation.4 | async-start | bytes 3194880 | tf_op jit(solution)/shard_map/all_gather | solution.py:25
  21.6 174.6 %all-gather.9.cloned.1.call-start = ((), (), s32[]{:S(2)}) async-start(), calls=%async_computation.5 | async-start | bytes 3194880 | tf_op jit(solution)/shard_map/all_gather | solution.py:26
  35.7 249.0 %all-gather.11.cloned.1.call-start = ((), (), s32[]{:S(2)}) async-start(), calls=%async_computation.6 | async-start | bytes 3194880 | tf_op jit(solution)/shard_map/all_gather | solution.py:98
  36.5 330.6 %all-gather.13.cloned.1.call-start = ((), (), s32[]{:S(2)}) async-start(), calls=%async_computation.7 | async-start | bytes 3194880 | tf_op jit(solution)/shard_map/all_gather | solution.py:99
  110.8 85.5 %copy-start.1 = (bf16[192,128]{1,0:T(8,128)(2,1)S(1)}, bf16[192,128]{1,0:T(8,128)(2,1)}, u32[]{:S(2)}) copy-start(bf16[192,128]{1,0:T(8,128)(2,1)} %param.16) | copy-start | bytes 147460
  131.1 65.2 %copy-start.2 = (f32[12288]{0:T(1024)}, f32[12288]{0:T(1024)S(1)}, u32[]{:S(2)}) copy-start(f32[12288]{0:T(1024)S(1)} %get-tuple-element.864) | copy-start | bytes 147460
  243.8 331.6 %all-to-all-start = ((bf16[8,24,128]{2,1,0:T(8,128)(2,1)}), bf16[8,24,128]{2,1,0:T(8,128)(2,1)S(1)}, u32[]{:S(2)}, u32[]{:S(2)}) async-start(bf16[8,24,128]{2,1,0:T(8,128)(2,1)} %bitcast), calls=%async_computation | async-start | bytes 98304 | tf_op jit(solution)/shard_map/all_to_all | solution.py:155
  248.1 270.2 %all-reduce.7.cloned.1.call-start = ((), (), s32[]{:S(2)}) async-start(), calls=%async_computation.10 | async-start | bytes 196608
  282.4 0.6 copy-start.3
  283.0 324.9 %reduce-scatter.7.cloned.1.call-start = ((), (), s32[]{:S(2)}) async-start(), calls=%async_computation.8 | async-start | bytes 110592
  574.7 0.6 copy-start.4
  574.7 5.6 copy-start
  575.4 9.8 %all-to-all-start.1 = ((bf16[8,24,128]{2,1,0:T(8,128)(2,1)}), bf16[8,24,128]{2,1,0:T(8,128)(2,1)S(1)}, u32[]{:S(2)}, u32[]{:S(2)}) async-start(bf16[8,24,128]{2,1,0:T(8,128)(2,1)} %bitcast.2), calls=%async_computation.1 | async-start | bytes 98304 | tf_op jit(solution)/shard_map/all_to_all | solution.py:156
  579.6 65.6 %reduce-scatter.9.cloned.1.call-start = ((), (), s32[]{:S(2)}) async-start(), calls=%async_computation.9 | async-start | bytes 110592
Sparse Core Ops, SparseCore 0:
  21.7 88.9 all-gather.6
  113.8 82.3 all-gather.8
  199.3 82.3 all-gather.10
  284.7 82.3 all-gather.12
  370.9 147.3 all-reduce.6
  575.5 32.3 reduce-scatter.6
  610.7 34.5 reduce-scatter.8
where the time goes:
time: 657 us; the launch traced here: 653 us
  waiting for transfers between devices  434 us (66%)
  matrix products  142 us (22%)
  blocking collectives  28.4 us (4%)
  between operations  14.9 us (2%)
  local copies, waits for them, and re-layouts  14.4 us (2%)
  starting transfers between devices  8.79 us (1%)
  other arithmetic  8.48 us (1%)
    unnamed x10, waiting for transfers between devices  211 us
    all_gather x1, waiting for transfers between devices, local(): lax.all_gather(grad_out, 'ctx', axis=0, tiled=True)  82.4 us
    all_gather x1, waiting for transfers between devices, local(): lax.all_gather(key_shard, 'ctx', axis=0, tiled=True)  70.8 us
    all_gather x1, waiting for transfers between devices, local(): lax.all_gather(value_shard, 'ctx', axis=0, tiled=True)  65.1 us
    dot_general x36, matrix products, masked_scores(): jnp.dot(queries, key_rows.T, preferred_element_type=jnp.float32) * scaling  46.6 us
    dot_general x12, matrix products, query_grad_step(): jnp.dot(dscores, key_rows, preferred_element_type=jnp.float32)  17.5 us
    dot_general x12, matrix products, key_grad_step(): jnp.einsum('hqk,qhd->kd', dscores, queries, preferred_element_type=jnp.fl...  17.4 us
    dot_general x12, matrix products, output_step(): dprobs = jnp.dot(flat_do, value_rows.T, preferred_element_type=jnp.float32)  15.8 us
  transfers between devices with their start and end apart: 9, of which 7 were waited for; matrix products, arithmetic and copies ran while one was open for 25% of the time, Pallas kernels for 0%

commit v1 on v0

v1 whole, which is shorter than its diff:
```python
import functools
import math

import jax
import jax.numpy as jnp
from jax import lax
from jax.experimental import pallas as pl
from jax.experimental.pallas import tpu as pltpu
from jax.sharding import PartitionSpec as P

F32 = jnp.float32
BF16 = jnp.bfloat16
LOG2E = 1.4426950408889634
LOW = -1e30
NT = (((1,), (1,)), ((), ()))


def stage_rows(src_ref, q_s, d_s, heads, span, hd):
    for half in range(2):
        for h in range(heads):
            rows = src_ref[h, half * span : (half + 1) * span, :]
            q_s[half, h * span : (h + 1) * span, :] = rows[:, :hd]
            d_s[half, h * span : (h + 1) * span, :] = rows[:, hd:]


def stats_kernel(
    dims, rank_ref, tiles_ref, kpos_ref, qpos_ref, qd_ref, kv_ref,
    stat_ref, kvs_ref, kvt_ref, q_s, d_s, sort_s,
):
    heads, span, hd, chunks, kc, tk, rc = dims
    factor = LOG2E / math.sqrt(hd)

    def place(c, _):
        start = pl.multiple_of(rank_ref[c] * kc, kc)
        sort_s[pl.ds(start, kc), :] = kv_ref[c].astype(F32)
        return 0

    lax.fori_loop(0, chunks, place, 0)
    n_keys = chunks * kc
    for t in range(n_keys // tk):
        block = sort_s[t * tk : (t + 1) * tk, :]
        kvs_ref[t * tk : (t + 1) * tk, :] = block.astype(BF16)
        kvt_ref[:, t * tk : (t + 1) * tk] = block.T.astype(BF16)
    stage_rows(qd_ref, q_s, d_s, heads, span, hd)
    half_rows = heads * span
    for half in range(2):
        for r in range(half_rows // rc):
            cols = slice(r * rc, (r + 1) * rc)
            q = q_s[half, cols, :]
            d = d_s[half, cols, :]
            qpos = qpos_ref[half : half + 1, cols]

            def tile(t, carried):
                m, l, ds = carried
                keys = pl.ds(pl.multiple_of(t * tk, tk), tk)
                k = kvs_ref[keys, :hd]
                v = kvs_ref[keys, hd:]
                s = lax.dot_general(k, q, NT, preferred_element_type=F32) * factor
                s = jnp.where(kpos_ref[keys, :] <= qpos, s, LOW)
                dp = lax.dot_general(v, d, NT, preferred_element_type=F32)
                s = s.reshape(tk // 8, 8, rc)
                dp = dp.reshape(tk // 8, 8, rc)
                m_new = jnp.maximum(m, jnp.max(s, axis=0))
                keep = jnp.exp2(m - m_new)
                p = jnp.exp2(s - m_new[None])
                l = l * keep + jnp.sum(p, axis=0)
                ds = ds * keep + jnp.sum(p * dp, axis=0)
                return (m_new, l, ds)

            zero = jnp.zeros((8, rc), F32)
            m, l, ds = lax.fori_loop(
                0, tiles_ref[half], tile, (jnp.full((8, rc), LOW, F32), zero, zero)
            )
            top = jnp.max(m, axis=0, keepdims=True)
            w = jnp.exp2(m - top)
            l = jnp.maximum(jnp.sum(l * w, axis=0, keepdims=True), 1e-30)
            ds = jnp.sum(ds * w, axis=0, keepdims=True)
            out = slice(half * half_rows + r * rc, half * half_rows + (r + 1) * rc)
            stat_ref[0:1, out] = top + jnp.log2(l)
            stat_ref[1:2, out] = ds / l


def grad_kernel(
    dims, rank_ref, tiles_ref, kpos_ref, qpos_ref, stat_ref, qd_ref, kvs_ref, kvt_ref,
    rows_ref, dkv_ref, q_s, d_s, acc_s, o_s, dq_s, lse_s, delta_s,
):
    heads, span, hd, chunks, kc, tk, rc = dims
    scaling = 1.0 / math.sqrt(hd)
    factor = LOG2E * scaling
    half_rows = heads * span
    stage_rows(qd_ref, q_s, d_s, heads, span, hd)
    acc_s[...] = jnp.zeros_like(acc_s)
    o_s[...] = jnp.zeros_like(o_s)
    dq_s[...] = jnp.zeros_like(dq_s)
    parts = [stat_ref[h] for h in range(stat_ref.shape[0])]
    top = functools.reduce(jnp.maximum, [p[0:1] for p in parts])
    weights = [jnp.exp2(p[0:1] - top) for p in parts]
    total = functools.reduce(jnp.add, weights)
    weighted = functools.reduce(jnp.add, [w * p[1:2] for w, p in zip(weights, parts)])
    lse_s[...] = top + jnp.log2(total)
    delta_s[...] = weighted / total
    for half in range(2):
        for r in range(half_rows // rc):
            cols = slice(r * rc, (r + 1) * rc)
            out = slice(half * half_rows + r * rc, half * half_rows + (r + 1) * rc)
            qpos = qpos_ref[half : half + 1, cols]
            lse = lse_s[:, out]
            delta = delta_s[:, out]

            def tile(t, _):
                keys = pl.ds(pl.multiple_of(t * tk, tk), tk)
                q = q_s[half, cols, :]
                d = d_s[half, cols, :]
                k = kvs_ref[keys, :hd]
                v = kvs_ref[keys, hd:]
                s = lax.dot_general(k, q, NT, preferred_element_type=F32) * factor
                p = jnp.where(kpos_ref[keys, :] <= qpos, jnp.exp2(s - lse), 0.0)
                dp = lax.dot_general(v, d, NT, preferred_element_type=F32)
                pb = p.astype(BF16)
                g = (p * (dp - delta) * scaling).astype(BF16)
                acc_s[keys, :hd] += jnp.dot(g, q, preferred_element_type=F32)
                acc_s[keys, hd:] += jnp.dot(pb, d, preferred_element_type=F32)
                dq_s[:, out] += jnp.dot(kvt_ref[:hd, keys], g, preferred_element_type=F32)
                o_s[:, out] += jnp.dot(kvt_ref[hd:, keys], pb, preferred_element_type=F32)
                return 0

            lax.fori_loop(0, tiles_ref[half], tile, 0)

    def place(c, _):
        start = pl.multiple_of(rank_ref[c] * kc, kc)
        dkv_ref[c] = acc_s[pl.ds(start, kc), :].astype(BF16)
        return 0

    lax.fori_loop(0, chunks, place, 0)
    blocks = span // kc
    for which, src in enumerate((o_s, dq_s)):
        whole = src[...].T
        for half in range(2):
            for h in range(heads):
                for i in range(blocks):
                    first = half * half_rows + h * span + i * kc
                    at = which * heads * hd + h * hd
                    rows_ref[half * blocks + i, :, at : at + hd] = whole[
                        first : first + kc
                    ].astype(BF16)


def exchange(x, axis):
    return lax.all_to_all(x, axis, split_axis=0, concat_axis=0, tiled=True)


def local(query_in, key_in, value_in, grad_out, span_of):
    hd = key_in.shape[1]
    kc = key_in.shape[0]
    heads = lax.axis_size("head")
    shards = lax.axis_size("ctx")
    local_rows = query_in.shape[0]
    span = local_rows // 2
    n_keys = shards * kc
    tk = math.gcd(n_keys, 256)
    rc = math.gcd(heads * span, 256)
    dims = (heads, span, hd, shards, kc, tk, rc)
    blocks = span // kc
    ctx = lax.axis_index("ctx")
    head = lax.axis_index("head")

    spans = span_of.reshape(shards, 2)
    key_span = lax.dynamic_index_in_dim(spans, head // blocks, 1, keepdims=False)
    own = lax.dynamic_index_in_dim(spans, ctx, 0, keepdims=False)
    rank = jnp.sum((key_span[None, :] < key_span[:, None]).astype(jnp.int32), axis=1)
    slot = jnp.arange(shards, dtype=jnp.int32)
    ordered = jnp.sum(jnp.where(rank[None, :] == slot[:, None], key_span[None, :], 0), axis=1)
    kpos = (
        ordered[:, None] * span
        + (head % blocks) * kc
        + jnp.arange(kc, dtype=jnp.int32)[None, :]
    ).reshape(n_keys, 1)
    qpos = own[:, None] * span + jnp.tile(jnp.arange(span, dtype=jnp.int32), heads)[None, :]
    seen = jnp.sum((key_span[None, :] <= own[:, None]).astype(jnp.int32), axis=1) * kc
    tiles = (seen + tk - 1) // tk

    kv = jnp.concatenate([key_in, value_in], axis=1)
    qd = jnp.concatenate([query_in, grad_out], axis=1)
    kv_all = exchange(jnp.broadcast_to(kv[None], (shards, kc, 2 * hd)), "ctx")
    qd_all = exchange(jnp.broadcast_to(qd[None], (heads, local_rows, 2 * hd)), "head")

    smem = pl.BlockSpec(memory_space=pltpu.SMEM)
    vmem = pl.BlockSpec(memory_space=pltpu.VMEM)
    params = pltpu.CompilerParams(vmem_limit_bytes=48 * 1024 * 1024)
    half_rows = heads * span
    rows = 2 * half_rows
    stat, kvs, kvt = pl.pallas_call(
        functools.partial(stats_kernel, dims),
        out_shape=(
            jax.ShapeDtypeStruct((2, rows), F32),
            jax.ShapeDtypeStruct((n_keys, 2 * hd), BF16),
            jax.ShapeDtypeStruct((2 * hd, n_keys), BF16),
        ),
        in_specs=[smem, smem] + [vmem] * 4,
        out_specs=(vmem, vmem, vmem),
        scratch_shapes=[
            pltpu.VMEM((2, half_rows, hd), BF16),
            pltpu.VMEM((2, half_rows, hd), BF16),
            pltpu.VMEM((n_keys, 2 * hd), F32),
        ],
        compiler_params=params,
        name="attention_stats",
    )(rank, tiles, kpos, qpos, qd_all, kv_all)

    stat_all = exchange(jnp.broadcast_to(stat[None], (heads, 2, rows)), "head")

    row_parts, key_parts = pl.pallas_call(
        functools.partial(grad_kernel, dims),
        out_shape=(
            jax.ShapeDtypeStruct((heads, kc, 2 * heads * hd), BF16),
            jax.ShapeDtypeStruct((shards, kc, 2 * hd), BF16),
        ),
        in_specs=[smem, smem] + [vmem] * 6,
        out_specs=(vmem, vmem),
        scratch_shapes=[
            pltpu.VMEM((2, half_rows, hd), BF16),
            pltpu.VMEM((2, half_rows, hd), BF16),
            pltpu.VMEM((n_keys, 2 * hd), F32),
            pltpu.VMEM((hd, rows), F32),
            pltpu.VMEM((hd, rows), F32),
            pltpu.VMEM((1, rows), F32),
            pltpu.VMEM((1, rows), F32),
        ],
        compiler_params=params,
        name="attention_grads",
    )(rank, tiles, kpos, qpos, stat_all, qd_all, kvs, kvt)

    key_parts = exchange(key_parts, "ctx")
    row_parts = exchange(row_parts, "head")
    key_sum = jnp.sum(key_parts.astype(F32), axis=0).astype(BF16)
    row_sum = jnp.sum(row_parts.astype(F32), axis=0).astype(BF16)
    width = heads * hd
    return (row_sum[:, :width], row_sum[:, width:], key_sum[:, :hd], key_sum[:, hd:])


def solution(mesh):
    return jax.shard_map(
        local,
        mesh=mesh,
        in_specs=(
            P("ctx", "head"),
            P(("ctx", "head"), None),
            P(("ctx", "head"), None),
            P("ctx", "head"),
            P(),
        ),
        out_specs=(P(("ctx", "head"), None),) * 4,
        check_vma=False,
    )
```

time: 657 us -> 138 us (0.21)
  the two profiles are of different devices: /device:TPU:8 before, /device:TPU:16 now
where the time goes in v1:
time: 138 us
  waiting for transfers between devices  59.7 us (43%)
  starting transfers between devices  28.5 us (21%)
  blocking collectives  23.8 us (17%)
  Pallas kernels  18.9 us (14%)
  local copies, waits for them, and re-layouts  4.37 us (3%)
  other arithmetic  1.75 us (1%)
    all_to_all x3, waiting for transfers between devices, exchange(): return lax.all_to_all(x, axis, split_axis=0, concat_axis=0, tiled=True)  59.7 us
    all_to_all x3, starting transfers between devices, exchange(): return lax.all_to_all(x, axis, split_axis=0, concat_axis=0, tiled=True)  28.5 us
    all_to_all x2, blocking collectives, exchange(): return lax.all_to_all(x, axis, split_axis=0, concat_axis=0, tiled=True)  23.8 us
    pallas_call x1, Pallas kernels, local(): pl.pallas_call(functools.partial(grad_kernel, dims), out_shape=(jax.Shape...  11.1 us
    pallas_call x1, Pallas kernels, local(): pl.pallas_call(functools.partial(stats_kernel, dims), out_shape=(jax.Shap...  7.79 us
  transfers between devices with their start and end apart: 3, of which 3 were waited for; matrix products, arithmetic and copies ran while one was open for 2% of the time, Pallas kernels for 0%

profile of v1, /device:TPU:16, one launch (start us, length us, event | category | flops | bytes accessed | tf_op | source)
XLA Modules:
  0.0 137.8 jit_solution(5018793535850051225)
XLA Ops:
  0.6 0.8 pad_maximum_fusion
  1.5 0.9 broadcast_in_dim.17
  2.4 4.4 %all-to-all-start = ((bf16[8,192,256]{2,1,0:T(8,128)(2,1)}), bf16[8,192,256]{2,1,0:T(8,128)(2,1)S(1)}, u32[]{:S(2)}, u32[]{:S(2)}) async-start(bf16[8,192,256]{2,1,0:T(8,128)(2,1)} %broadcast_in_dim.17), calls=%async_computation | async-start | bytes 1572864 | tf_op jit(solution)/shard_map/all_to_all | solution.py:149
  6.9 13.1 %all-to-all-done.qd_ref = bf16[8,192,256]{2,1,0:T(8,128)(2,1)S(1)} async-done(((bf16[8,192,256]{2,1,0:T(8,128)(2,1)}), bf16[8,192,256]{2,1,0:T(8,128)(2,1)S(1)}, u32[]{:S(2)}, u32[]{:S(2)}) %all-to-all-start) | async-done | bytes 786464 | tf_op jit(solution)/shard_map/all_to_all | solution.py:149
  20.0 0.9 broadcast_in_dim.18
  20.9 16.5 %all-to-all-start.1 = ((bf16[64,24,256]{2,1,0:T(8,128)(2,1)}), bf16[64,24,256]{2,1,0:T(8,128)(2,1)S(1)}, u32[]{:S(2)}, u32[]{:S(2)}) async-start(bf16[64,24,256]{2,1,0:T(8,128)(2,1)} %broadcast_in_dim.18), calls=%async_computation.1 | async-start | bytes 1572864 | tf_op jit(solution)/shard_map/all_to_all | solution.py:149
  37.5 0.6 copy-done.2
  38.1 0.1 reshape.56
  38.2 0.2 dynamic-slice_reduce_fusion
  38.4 0.2 convert_reduce_fusion.rank_ref
  38.6 0.1 select_reduce_fusion
  38.8 0.3 add.80.kpos_ref
  39.1 0.2 fusion
  39.4 22.7 %all-to-all-done.1.kv_ref = bf16[64,24,256]{2,1,0:T(8,128)(2,1)S(1)} async-done(((bf16[64,24,256]{2,1,0:T(8,128)(2,1)}), bf16[64,24,256]{2,1,0:T(8,128)(2,1)S(1)}, u32[]{:S(2)}, u32[]{:S(2)}) %all-to-all-start.1) | async-done | bytes 786464 | tf_op jit(solution)/shard_map/all_to_all | solution.py:149
  62.1 7.8 %attention_stats.1 = (f32[2,1536]{1,0:T(2,128)S(1)}, bf16[1536,256]{1,0:T(8,128)(2,1)S(1)}, bf16[256,1536]{1,0:T(8,128)(2,1)S(1)}) custom-call(s32[64]{0:T(128)S(1)} %convert_reduce_fusion.rank_ref, s32[2]{0:T(128)S(1)} %and_select_fusion.tiles_ref, s32[1536,1]{1,0:T(8,128)S(1)} %add.80.kpos_ref, s32[2,768]{1,0:T(2,128)S(1)} %broadcast_add_fusion.qpos_ref, ...), custom_call_target="tpu_custom_call" | custom-call | tf_op jit(solution)/shard_map/attention_stats/pallas_call | solution.py:192
  69.9 8.2 %all_to_all.25.stat_ref = f32[8,2,1536]{2,1,0:T(2,128)S(1)} all-to-all(f32[8,2,1536]{2,1,0:T(2,128)S(1)} %broadcast_in_dim.19), channel_id=1, replica_groups=mesh['ctx'=64,'head'=8] {'head'}, dimensions={0} | all-to-all | bytes 196608 | tf_op jit(solution)/shard_map/all_to_all | solution.py:149
  78.1 11.1 %attention_grads.1 = (bf16[8,24,2048]{2,1,0:T(8,128)(2,1)S(1)}, bf16[64,24,256]{2,1,0:T(8,128)(2,1)}) custom-call(s32[64]{0:T(128)S(1)} %convert_reduce_fusion.rank_ref, s32[2]{0:T(128)S(1)} %and_select_fusion.tiles_ref, s32[1536,1]{1,0:T(8,128)S(1)} %add.80.kpos_ref, s32[2,768]{1,0:T(2,128)S(1)} %broadcast_add_fusion.qpos_ref, ...), custom_call_target="tpu_custom_call" | custom-call | tf_op jit(solution)/shard_map/attention_grads/pallas_call | solution.py:212
  89.2 15.6 %all_to_all.26 = bf16[8,24,2048]{2,1,0:T(8,128)(2,1)S(1)} all-to-all(bf16[8,24,2048]{2,1,0:T(8,128)(2,1)S(1)} %get-tuple-element.12), channel_id=1, replica_groups=mesh['ctx'=64,'head'=8] {'head'}, dimensions={0} | all-to-all | bytes 1572864 | tf_op jit(solution)/shard_map/all_to_all | solution.py:149
  104.8 7.6 %all-to-all-start.4 = ((bf16[64,24,256]{2,1,0:T(8,128)(2,1)}), bf16[64,24,256]{2,1,0:T(8,128)(2,1)S(1)}, u32[]{:S(2)}, u32[]{:S(2)}) async-start(bf16[64,24,256]{2,1,0:T(8,128)(2,1)} %get-tuple-element.13), calls=%async_computation.4 | async-start | bytes 1572864 | tf_op jit(solution)/shard_map/all_to_all | solution.py:149
  112.4 0.1 reduce_sum.54
  112.5 0.6 fusion.1
  113.2 23.8 %all-to-all-done.4 = bf16[64,24,256]{2,1,0:T(8,128)(2,1)S(1)} async-done(((bf16[64,24,256]{2,1,0:T(8,128)(2,1)}), bf16[64,24,256]{2,1,0:T(8,128)(2,1)S(1)}, u32[]{:S(2)}, u32[]{:S(2)}) %all-to-all-start.4) | async-done | bytes 786464 | tf_op jit(solution)/shard_map/all_to_all | solution.py:149
  137.0 0.1 reduce_sum.55
  137.1 0.6 fusion.2
  (14 shorter events, 0.3 us)
Async XLA Ops:
  2.4 4.4 %copy-start = (bf16[24,128]{1,0:T(8,128)(2,1)S(1)}, bf16[24,128]{1,0:T(8,128)(2,1)}, u32[]{:S(2)}) copy-start(bf16[24,128]{1,0:T(8,128)(2,1)} %param.7) | copy-start | bytes 18436
  2.4 4.4 %copy-start.1 = (bf16[24,128]{1,0:T(8,128)(2,1)S(1)}, bf16[24,128]{1,0:T(8,128)(2,1)}, u32[]{:S(2)}) copy-start(bf16[24,128]{1,0:T(8,128)(2,1)} %param.6) | copy-start | bytes 18436
  2.4 17.6 %all-to-all-start = ((bf16[8,192,256]{2,1,0:T(8,128)(2,1)}), bf16[8,192,256]{2,1,0:T(8,128)(2,1)S(1)}, u32[]{:S(2)}, u32[]{:S(2)}) async-start(bf16[8,192,256]{2,1,0:T(8,128)(2,1)} %broadcast_in_dim.17), calls=%async_computation | async-start | bytes 1572864 | tf_op jit(solution)/shard_map/all_to_all | solution.py:149
  20.9 41.2 %all-to-all-start.1 = ((bf16[64,24,256]{2,1,0:T(8,128)(2,1)}), bf16[64,24,256]{2,1,0:T(8,128)(2,1)S(1)}, u32[]{:S(2)}, u32[]{:S(2)}) async-start(bf16[64,24,256]{2,1,0:T(8,128)(2,1)} %broadcast_in_dim.18), calls=%async_computation.1 | async-start | bytes 1572864 | tf_op jit(solution)/shard_map/all_to_all | solution.py:149
  37.4 0.7 copy-start.2
  104.8 32.2 %all-to-all-start.4 = ((bf16[64,24,256]{2,1,0:T(8,128)(2,1)}), bf16[64,24,256]{2,1,0:T(8,128)(2,1)S(1)}, u32[]{:S(2)}, u32[]{:S(2)}) async-start(bf16[64,24,256]{2,1,0:T(8,128)(2,1)} %get-tuple-element.13), calls=%async_computation.4 | async-start | bytes 1572864 | tf_op jit(solution)/shard_map/all_to_all | solution.py:149

commit v2 on v1

--- a/solution.py
+++ b/solution.py
@@ -15,17 +15,21 @@
 NT = (((1,), (1,)), ((), ()))
 
 
-def stage_rows(src_ref, q_s, d_s, heads, span, hd):
-    for half in range(2):
-        for h in range(heads):
-            rows = src_ref[h, half * span : (half + 1) * span, :]
-            q_s[half, h * span : (h + 1) * span, :] = rows[:, :hd]
-            d_s[half, h * span : (h + 1) * span, :] = rows[:, hd:]
+def stage_rows(order_ref, sources, q_s, d_s, span, hd):
+    number = 0
+    for src_ref in sources:
+        for piece in range(src_ref.shape[0]):
+            at = pl.ds(pl.multiple_of(order_ref[number] * span, span), span)
+            for half in range(2):
+                rows = src_ref[piece, half * span : (half + 1) * span, :]
+                q_s[half, at, :] = rows[:, :hd]
+                d_s[half, at, :] = rows[:, hd:]
+            number += 1
 
 
 def stats_kernel(
-    dims, rank_ref, tiles_ref, kpos_ref, qpos_ref, qd_ref, kv_ref,
-    stat_ref, kvs_ref, kvt_ref, q_s, d_s, sort_s,
+    dims, rank_ref, tiles_ref, order_ref, kpos_ref, qpos_ref, near_ref, far_ref, kv_ref,
+    stat_ref, kvs_ref, q_s, d_s, sort_s,
 ):
     heads, span, hd, chunks, kc, tk, rc = dims
     factor = LOG2E / math.sqrt(hd)
@@ -38,10 +42,8 @@
     lax.fori_loop(0, chunks, place, 0)
     n_keys = chunks * kc
     for t in range(n_keys // tk):
-        block = sort_s[t * tk : (t + 1) * tk, :]
-        kvs_ref[t * tk : (t + 1) * tk, :] = block.astype(BF16)
-        kvt_ref[:, t * tk : (t + 1) * tk] = block.T.astype(BF16)
-    stage_rows(qd_ref, q_s, d_s, heads, span, hd)
+        kvs_ref[t * tk : (t + 1) * tk, :] = sort_s[t * tk : (t + 1) * tk, :].astype(BF16)
+    stage_rows(order_ref, (near_ref, far_ref), q_s, d_s, span, hd)
     half_rows = heads * span
     for half in range(2):
         for r in range(half_rows // rc):
@@ -81,14 +83,18 @@
 
 
 def grad_kernel(
-    dims, rank_ref, tiles_ref, kpos_ref, qpos_ref, stat_ref, qd_ref, kvs_ref, kvt_ref,
-    rows_ref, dkv_ref, q_s, d_s, acc_s, o_s, dq_s, lse_s, delta_s,
+    dims, rank_ref, tiles_ref, order_ref, kpos_ref, qpos_ref, stat_ref, near_ref, far_ref,
+    kvs_ref, keep_ref, send_ref, dkv_ref,
+    q_s, d_s, acc_s, o_s, dq_s, lse_s, delta_s, kvt_s, flat_s,
 ):
     heads, span, hd, chunks, kc, tk, rc = dims
     scaling = 1.0 / math.sqrt(hd)
     factor = LOG2E * scaling
     half_rows = heads * span
-    stage_rows(qd_ref, q_s, d_s, heads, span, hd)
+    stage_rows(order_ref, (near_ref, far_ref), q_s, d_s, span, hd)
+    n_keys = chunks * kc
+    for t in range(n_keys // tk):
+        kvt_s[:, t * tk : (t + 1) * tk] = kvs_ref[t * tk : (t + 1) * tk, :].T
     acc_s[...] = jnp.zeros_like(acc_s)
     o_s[...] = jnp.zeros_like(o_s)
     dq_s[...] = jnp.zeros_like(dq_s)
@@ -120,8 +126,8 @@
                 g = (p * (dp - delta) * scaling).astype(BF16)
                 acc_s[keys, :hd] += jnp.dot(g, q, preferred_element_type=F32)
                 acc_s[keys, hd:] += jnp.dot(pb, d, preferred_element_type=F32)
-                dq_s[:, out] += jnp.dot(kvt_ref[:hd, keys], g, preferred_element_type=F32)
-                o_s[:, out] += jnp.dot(kvt_ref[hd:, keys], pb, preferred_element_type=F32)
+                dq_s[:, out] += jnp.dot(kvt_s[:hd, keys], g, preferred_element_type=F32)
+                o_s[:, out] += jnp.dot(kvt_s[hd:, keys], pb, preferred_element_type=F32)
                 return 0
 
             lax.fori_loop(0, tiles_ref[half], tile, 0)
@@ -133,20 +139,46 @@
 
     lax.fori_loop(0, chunks, place, 0)
     blocks = span // kc
+    per_core = heads // 2
     for which, src in enumerate((o_s, dq_s)):
-        whole = src[...].T
-        for half in range(2):
+        flat_s[...] = src[...].T
+        for number in range(heads):
+            target = order_ref[number]
+            half, block = target // blocks, target % blocks
+            out_ref = keep_ref if number < per_core else send_ref
             for h in range(heads):
-                for i in range(blocks):
-                    first = half * half_rows + h * span + i * kc
-                    at = which * heads * hd + h * hd
-                    rows_ref[half * blocks + i, :, at : at + hd] = whole[
-                        first : first + kc
-                    ].astype(BF16)
-
-
-def exchange(x, axis):
-    return lax.all_to_all(x, axis, split_axis=0, concat_axis=0, tiled=True)
+                first = pl.multiple_of(half * half_rows + h * span + block * kc, kc)
+                at = which * heads * hd + h * hd
+                out_ref[number % per_core, :, at : at + hd] = flat_s[
+                    pl.ds(first, kc), :
+                ].astype(BF16)
+
+
+def grouped(x, groups):
+    return lax.all_to_all(
+        x, ("ctx", "head"), split_axis=0, concat_axis=0, axis_index_groups=groups, tiled=True
+    )
+
+
+def line_groups(side, heads):
+    first, second = [], []
+    for head in range(heads):
+        for fixed in range(side):
+            along_z = [(fixed * side + moving) * heads + head for moving in range(side)]
+            along_y = [(moving * side + fixed) * heads + head for moving in range(side)]
+            first.append(along_y if head % 2 else along_z)
+            second.append(along_z if head % 2 else along_y)
+    return first, second
+
+
+def flip_x(x, mesh_x, mask):
+    pairs = [(2 * a + c, 2 * (a ^ mask) + c) for a in range(mesh_x) for c in range(2)]
+    return lax.ppermute(x, "head", pairs)
+
+
+def swap_cores(x, mesh_x):
+    pairs = [(2 * a + c, 2 * a + 1 - c) for a in range(mesh_x) for c in range(2)]
+    return lax.ppermute(x, "head", pairs)
 
 
 def local(query_in, key_in, value_in, grad_out, span_of):
@@ -164,12 +196,25 @@
     ctx = lax.axis_index("ctx")
     head = lax.axis_index("head")
 
+    mesh_x = heads // 2
+    at_x, core = head // 2, head % 2
+    masks = [2 ** (bit + 1) - 1 for bit in range(mesh_x.bit_length() - 1)]
+    offsets = [0]
+    for mask in masks:
+        offsets = offsets + [mask ^ offset for offset in offsets]
+    origin = jnp.bitwise_xor(at_x, jnp.array(offsets, jnp.int32)) * 2
+    order = jnp.concatenate([origin + core, origin + 1 - core]).astype(jnp.int32)
+    side = math.isqrt(shards)
+    first, second = line_groups(side, heads)
+
     spans = span_of.reshape(shards, 2)
     key_span = lax.dynamic_index_in_dim(spans, head // blocks, 1, keepdims=False)
     own = lax.dynamic_index_in_dim(spans, ctx, 0, keepdims=False)
     rank = jnp.sum((key_span[None, :] < key_span[:, None]).astype(jnp.int32), axis=1)
-    slot = jnp.arange(shards, dtype=jnp.int32)
-    ordered = jnp.sum(jnp.where(rank[None, :] == slot[:, None], key_span[None, :], 0), axis=1)
+    place = jnp.arange(shards, dtype=jnp.int32)
+    crossed = rank.reshape(side, side).T.reshape(shards)
+    slots = jnp.where(core == 0, rank, crossed)
+    ordered = jnp.sum(jnp.where(rank[None, :] == place[:, None], key_span[None, :], 0), axis=1)
     kpos = (
         ordered[:, None] * span
         + (head % blocks) * kc
@@ -181,23 +226,27 @@
 
     kv = jnp.concatenate([key_in, value_in], axis=1)
     qd = jnp.concatenate([query_in, grad_out], axis=1)
-    kv_all = exchange(jnp.broadcast_to(kv[None], (shards, kc, 2 * hd)), "ctx")
-    qd_all = exchange(jnp.broadcast_to(qd[None], (heads, local_rows, 2 * hd)), "head")
+    kv_line = grouped(jnp.broadcast_to(kv[None], (side, kc, 2 * hd)), first)
+    kv_all = grouped(jnp.broadcast_to(kv_line[None], (side, side, kc, 2 * hd)), second)
+    kv_all = kv_all.reshape(shards, kc, 2 * hd)
+    near = qd[None]
+    for mask in masks:
+        near = jnp.concatenate([near, flip_x(near, mesh_x, mask)])
+    far = swap_cores(near, mesh_x)
 
     smem = pl.BlockSpec(memory_space=pltpu.SMEM)
     vmem = pl.BlockSpec(memory_space=pltpu.VMEM)
     params = pltpu.CompilerParams(vmem_limit_bytes=48 * 1024 * 1024)
     half_rows = heads * span
     rows = 2 * half_rows
-    stat, kvs, kvt = pl.pallas_call(
+    stat, kvs = pl.pallas_call(
         functools.partial(stats_kernel, dims),
         out_shape=(
             jax.ShapeDtypeStruct((2, rows), F32),
             jax.ShapeDtypeStruct((n_keys, 2 * hd), BF16),
-            jax.ShapeDtypeStruct((2 * hd, n_keys), BF16),
         ),
-        in_specs=[smem, smem] + [vmem] * 4,
-        out_specs=(vmem, vmem, vmem),
+        in_specs=[smem] * 3 + [vmem] * 5,
+        out_specs=(vmem, vmem),
         scratch_shapes=[
             pltpu.VMEM((2, half_rows, hd), BF16),
             pltpu.VMEM((2, half_rows, hd), BF16),
@@ -205,18 +254,21 @@
         ],
         compiler_params=params,
         name="attention_stats",
-    )(rank, tiles, kpos, qpos, qd_all, kv_all)
-
-    stat_all = exchange(jnp.broadcast_to(stat[None], (heads, 2, rows)), "head")
-
-    row_parts, key_parts = pl.pallas_call(
+    )(slots, tiles, order, kpos, qpos, near, far, kv_all)
+
+    stat_all = lax.all_to_all(
+        jnp.broadcast_to(stat[None], (heads, 2, rows)), "head", 0, 0, tiled=True
+    )
+
+    keep, send, key_parts = pl.pallas_call(
         functools.partial(grad_kernel, dims),
         out_shape=(
-            jax.ShapeDtypeStruct((heads, kc, 2 * heads * hd), BF16),
+            jax.ShapeDtypeStruct((mesh_x, kc, 2 * heads * hd), BF16),
+            jax.ShapeDtypeStruct((mesh_x, kc, 2 * heads * hd), BF16),
             jax.ShapeDtypeStruct((shards, kc, 2 * hd), BF16),
         ),
-        in_specs=[smem, smem] + [vmem] * 6,
-        out_specs=(vmem, vmem),
+        in_specs=[smem] * 3 + [vmem] * 6,
+        out_specs=(vmem, vmem, vmem),
         scratch_shapes=[
             pltpu.VMEM((2, half_rows, hd), BF16),
             pltpu.VMEM((2, half_rows, hd), BF16),
@@ -225,15 +277,23 @@
             pltpu.VMEM((hd, rows), F32),
             pltpu.VMEM((1, rows), F32),
             pltpu.VMEM((1, rows), F32),
+            pltpu.VMEM((2 * hd, n_keys), BF16),
+            pltpu.VMEM((rows, hd), F32),
         ],
         compiler_params=params,
         name="attention_grads",
-    )(rank, tiles, kpos, qpos, stat_all, qd_all, kvs, kvt)
-
-    key_parts = exchange(key_parts, "ctx")
-    row_parts = exchange(row_parts, "head")
-    key_sum = jnp.sum(key_parts.astype(F32), axis=0).astype(BF16)
-    row_sum = jnp.sum(row_parts.astype(F32), axis=0).astype(BF16)
+    )(slots, tiles, order, kpos, qpos, stat_all, near, far, kvs)
+
+    key_line = grouped(key_parts.reshape(side, side, kc, 2 * hd), second)
+    key_line = jnp.sum(key_line.astype(F32), axis=0).astype(BF16)
+    key_sum = jnp.sum(grouped(key_line, first).astype(F32), axis=0).astype(BF16)
+
+    row_sum = keep.astype(F32) + swap_cores(send, mesh_x).astype(F32)
+    for mask in reversed(masks):
+        half = row_sum.shape[0] // 2
+        moved = flip_x(row_sum[half:].astype(BF16), mesh_x, mask)
+        row_sum = row_sum[:half] + moved.astype(F32)
+    row_sum = row_sum[0].astype(BF16)
     width = heads * hd
     return (row_sum[:, :width], row_sum[:, width:], key_sum[:, :hd], key_sum[:, hd:])
 

time: 138 us -> 113 us (0.82)
  the two profiles are of different devices: /device:TPU:16 before, /device:TPU:24 now
where the time goes in v2:
time: 113 us; the launch traced here: 112 us
  starting transfers between devices  48.1 us (43%)
  waiting for transfers between devices  26.7 us (24%)
  Pallas kernels  19.4 us (17%)
  blocking collectives  9.63 us (9%)
  local copies, waits for them, and re-layouts  4.91 us (4%)
  other arithmetic  2.44 us (2%)
    all_to_all x4, starting transfers between devices, grouped(): lax.all_to_all(x, ('ctx', 'head'), split_axis=0, concat_axis=0, axis_inde...  29.9 us
    ppermute x4, starting transfers between devices, flip_x(): return lax.ppermute(x, 'head', pairs)  14.3 us
    ppermute x4, waiting for transfers between devices, flip_x(): return lax.ppermute(x, 'head', pairs)  13.1 us
    all_to_all x4, waiting for transfers between devices, grouped(): lax.all_to_all(x, ('ctx', 'head'), split_axis=0, concat_axis=0, axis_inde...  12 us
    pallas_call x1, Pallas kernels, local(): pl.pallas_call(functools.partial(grad_kernel, dims), out_shape=(jax.Shape...  11.7 us
    all_to_all x1, blocking collectives, local(): lax.all_to_all(jnp.broadcast_to(stat[None], (heads, 2, rows)), 'head', 0,...  9.63 us
    pallas_call x1, Pallas kernels, local(): pl.pallas_call(functools.partial(stats_kernel, dims), out_shape=(jax.Shap...  7.66 us
    ppermute x2, starting transfers between devices, swap_cores(): return lax.ppermute(x, 'head', pairs)  3.83 us
  transfers between devices with their start and end apart: 10, of which 6 were waited for; matrix products, arithmetic and copies ran while one was open for 3% of the time, Pallas kernels for 0%

profile of v2, /device:TPU:24, one launch (start us, length us, event | category | flops | bytes accessed | tf_op | source)
XLA Modules:
  0.0 112.0 jit_solution(14642933605341753674)
XLA Ops:
  0.6 0.7 pad_maximum_fusion.2
  1.3 0.6 broadcast_in_dim.20
  2.0 10.4 %all-to-all-start = ((bf16[8,24,256]{2,1,0:T(8,128)(2,1)}), bf16[8,24,256]{2,1,0:T(8,128)(2,1)S(1)}, u32[]{:S(2)}, u32[]{:S(2)}) async-start(bf16[8,24,256]{2,1,0:T(8,128)(2,1)} %broadcast_in_dim.20), calls=%async_computation | async-start | bytes 196608 | tf_op jit(solution)/shard_map/all_to_all | solution.py:158
  12.5 3.4 %collective-permute-start = (bf16[1,192,256]{2,1,0:T(8,128)(2,1)S(1)}, bf16[1,192,256]{2,1,0:T(8,128)(2,1)S(1)}, u32[]{:S(2)}, u32[]{:S(2)}) collective-permute-start(bf16[1,192,256]{2,1,0:T(8,128)(2,1)S(1)} %maximum_bitcast_fusion), channel_id=1, source_target_pairs={{0,2},{1,3},{2,0},{3,1},{4,6},{5,7},{6,4},{7,5},{8,10},{9,11},{10,... | collective-permute-start | bytes 294920 | tf_op jit(solution)/shard_map/ppermute | solution.py:176
  15.9 0.6 copy-done.2
  17.3 3.9 %all-to-all-done = bf16[8,24,256]{2,1,0:T(8,128)(2,1)S(1)} async-done(((bf16[8,24,256]{2,1,0:T(8,128)(2,1)}), bf16[8,24,256]{2,1,0:T(8,128)(2,1)S(1)}, u32[]{:S(2)}, u32[]{:S(2)}) %all-to-all-start) | async-done | bytes 98336 | tf_op jit(solution)/shard_map/all_to_all | solution.py:158
  21.2 0.9 broadcast_in_dim.21
  22.1 7.3 %all-to-all-start.1 = ((bf16[8,8,24,256]{3,2,1,0:T(8,128)(2,1)}), bf16[8,8,24,256]{3,2,1,0:T(8,128)(2,1)S(1)}, u32[]{:S(2)}, u32[]{:S(2)}) async-start(bf16[8,8,24,256]{3,2,1,0:T(8,128)(2,1)} %broadcast_in_dim.21), calls=%async_computation.1 | async-start | bytes 1572864 | tf_op jit(solution)/shard_map/all_to_all | solution.py:158
  30.8 4.7 %collective-permute-start.1 = (bf16[2,192,256]{2,1,0:T(8,128)(2,1)S(1)}, bf16[2,192,256]{2,1,0:T(8,128)(2,1)S(1)}, u32[]{:S(2)}, u32[]{:S(2)}) collective-permute-start(bf16[2,192,256]{2,1,0:T(8,128)(2,1)S(1)} %pad_maximum_fusion.1), channel_id=1, source_target_pairs={{0,6},{1,7},{2,4},{3,5},{4,2},{5,3},{6,0},{7,1},{8,14},{9,15},{10,... | collective-permute-start | bytes 589832 | tf_op jit(solution)/shard_map/ppermute | solution.py:176
  35.5 4.1 %collective-permute-done.1 = bf16[2,192,256]{2,1,0:T(8,128)(2,1)S(1)} collective-permute-done((bf16[2,192,256]{2,1,0:T(8,128)(2,1)S(1)}, bf16[2,192,256]{2,1,0:T(8,128)(2,1)S(1)}, u32[]{:S(2)}, u32[]{:S(2)}) %collective-permute-start.1) | collective-permute-done | bytes 196640 | tf_op jit(solution)/shard_map/ppermute | solution.py:176
  39.6 1.9 %collective-permute-start.2 = (bf16[4,192,256]{2,1,0:T(8,128)(2,1)S(1)}, bf16[4,192,256]{2,1,0:T(8,128)(2,1)S(1)}, u32[]{:S(2)}, u32[]{:S(2)}) collective-permute-start(bf16[4,192,256]{2,1,0:T(8,128)(2,1)S(1)} %pad_maximum_fusion.near_ref), channel_id=1, source_target_pairs={{0,1},{1,0},{2,3},{3,2},{4,5},{5,4},{6,7},{7,6},{8,9},{9,8},{10,11... | collective-permute-start | bytes 1179656 | tf_op jit(solution)/shard_map/ppermute | solution.py:181
  41.7 1.6 %collective-permute-done.2.far_ref = bf16[4,192,256]{2,1,0:T(8,128)(2,1)S(1)} collective-permute-done((bf16[4,192,256]{2,1,0:T(8,128)(2,1)S(1)}, bf16[4,192,256]{2,1,0:T(8,128)(2,1)S(1)}, u32[]{:S(2)}, u32[]{:S(2)}) %collective-permute-start.2) | collective-permute-done | bytes 393248 | tf_op jit(solution)/shard_map/ppermute | solution.py:181
  43.3 7.7 %attention_stats.1 = (f32[2,1536]{1,0:T(2,128)S(1)}, bf16[1536,256]{1,0:T(8,128)(2,1)S(1)}) custom-call(s32[64]{0:T(128)S(1)} %broadcast_select_fusion.rank_ref, s32[2]{0:T(128)S(1)} %and_select_fusion.tiles_ref, s32[8]{0:T(128)S(1)} %pad_add_fusion.order_ref, s32[1536,1]{1,0:T(8,128)S(1)} %add.109.kpos_ref, s32[2,768]{1,0:T(2,128)S(1)} %broadcast_add_fusion.qpos_ref, ...), custom_call_target="tpu_custom_call" | custom-call | tf_op jit(solution)/shard_map/attention_stats/pallas_call | solution.py:242
  51.0 9.6 %all_to_all.25.stat_ref = f32[8,2,1536]{2,1,0:T(2,128)S(1)} all-to-all(f32[8,2,1536]{2,1,0:T(2,128)S(1)} %broadcast_in_dim.22), channel_id=1, replica_groups=mesh['ctx'=64,'head'=8] {'head'}, dimensions={0} | all-to-all | bytes 196608 | tf_op jit(solution)/shard_map/all_to_all | solution.py:259
  60.6 11.7 %attention_grads.1 = (bf16[4,24,2048]{2,1,0:T(8,128)(2,1)S(1)}, bf16[4,24,2048]{2,1,0:T(8,128)(2,1)S(1)}, bf16[64,24,256]{2,1,0:T(8,128)(2,1)}) custom-call(s32[64]{0:T(128)S(1)} %broadcast_select_fusion.rank_ref, s32[2]{0:T(128)S(1)} %and_select_fusion.tiles_ref, s32[8]{0:T(128)S(1)} %pad_add_fusion.order_ref, s32[1536,1]{1,0:T(8,128)S(1)} %add.109.kpos_ref, ...), custom_call_target="tpu_custom_call" | custom-call | tf_op jit(solution)/shard_map/attention_grads/pallas_call | solution.py:263
  72.3 1.9 %collective-permute-start.3 = (bf16[4,24,2048]{2,1,0:T(8,128)(2,1)S(1)}, bf16[4,24,2048]{2,1,0:T(8,128)(2,1)S(1)}, u32[]{:S(2)}, u32[]{:S(2)}) collective-permute-start(bf16[4,24,2048]{2,1,0:T(8,128)(2,1)S(1)} %get-tuple-element.12), channel_id=1, source_target_pairs={{0,1},{1,0},{2,3},{3,2},{4,5},{5,4},{6,7},{7,6},{8,9},{9,8},{10,11... | collective-permute-start | bytes 1179656 | tf_op jit(solution)/shard_map/ppermute | solution.py:181
  74.2 7.2 %all-to-all-start.3 = ((bf16[8,8,24,256]{3,2,1,0:T(8,128)(2,1)}), bf16[8,8,24,256]{3,2,1,0:T(8,128)(2,1)S(1)}, u32[]{:S(2)}, u32[]{:S(2)}) async-start(bf16[8,8,24,256]{3,2,1,0:T(8,128)(2,1)} %bitcast.5), calls=%async_computation.3 | async-start | bytes 1572864 | tf_op jit(solution)/shard_map/all_to_all | solution.py:158
  81.6 4.3 %collective-permute-start.4 = (bf16[2,24,2048]{2,1,0:T(8,128)(2,1)S(1)}, bf16[2,24,2048]{2,1,0:T(8,128)(2,1)S(1)}, u32[]{:S(2)}, u32[]{:S(2)}) collective-permute-start(bf16[2,24,2048]{2,1,0:T(8,128)(2,1)S(1)} %slice.50), channel_id=1, source_target_pairs={{0,6},{1,7},{2,4},{3,5},{4,2},{5,3},{6,0},{7,1},{8,14},{9,15},{10,... | collective-permute-start | bytes 589832 | tf_op jit(solution)/shard_map/ppermute | solution.py:176
  85.9 4.4 %collective-permute-done.4 = bf16[2,24,2048]{2,1,0:T(8,128)(2,1)S(1)} collective-permute-done((bf16[2,24,2048]{2,1,0:T(8,128)(2,1)S(1)}, bf16[2,24,2048]{2,1,0:T(8,128)(2,1)S(1)}, u32[]{:S(2)}, u32[]{:S(2)}) %collective-permute-start.4) | collective-permute-done | bytes 196640 | tf_op jit(solution)/shard_map/ppermute | solution.py:176
  90.4 1.9 %collective-permute-start.5 = (bf16[1,24,2048]{2,1,0:T(8,128)(2,1)S(1)}, bf16[1,24,2048]{2,1,0:T(8,128)(2,1)S(1)}, u32[]{:S(2)}, u32[]{:S(2)}) collective-permute-start(bf16[1,24,2048]{2,1,0:T(8,128)(2,1)S(1)} %slice.51), channel_id=1, source_target_pairs={{0,2},{1,3},{2,0},{3,1},{4,6},{5,7},{6,4},{7,5},{8,10},{9,11},{10,... | collective-permute-start | bytes 294920 | tf_op jit(solution)/shard_map/ppermute | solution.py:176
  92.3 4.6 %collective-permute-done.5 = bf16[1,24,2048]{2,1,0:T(8,128)(2,1)S(1)} collective-permute-done((bf16[1,24,2048]{2,1,0:T(8,128)(2,1)S(1)}, bf16[1,24,2048]{2,1,0:T(8,128)(2,1)S(1)}, u32[]{:S(2)}, u32[]{:S(2)}) %collective-permute-start.5) | collective-permute-done | bytes 98336 | tf_op jit(solution)/shard_map/ppermute | solution.py:176
  96.9 0.8 reduce_sum.54
  97.7 5.0 %all-to-all-start.4 = ((bf16[8,24,256]{2,1,0:T(8,128)(2,1)}), bf16[8,24,256]{2,1,0:T(8,128)(2,1)S(1)}, u32[]{:S(2)}, u32[]{:S(2)}) async-start(bf16[8,24,256]{2,1,0:T(8,128)(2,1)} %reduce_sum.54), calls=%async_computation.4 | async-start | bytes 196608 | tf_op jit(solution)/shard_map/all_to_all | solution.py:158
  103.3 8.1 %all-to-all-done.4 = bf16[8,24,256]{2,1,0:T(8,128)(2,1)S(1)} async-done(((bf16[8,24,256]{2,1,0:T(8,128)(2,1)}), bf16[8,24,256]{2,1,0:T(8,128)(2,1)S(1)}, u32[]{:S(2)}, u32[]{:S(2)}) %all-to-all-start.4) | async-done | bytes 98336 | tf_op jit(solution)/shard_map/all_to_all | solution.py:158
  (42 shorter events, 3.7 us)
Async XLA Ops:
  2.0 10.5 %copy-start = (bf16[192,128]{1,0:T(8,128)(2,1)S(1)}, bf16[192,128]{1,0:T(8,128)(2,1)}, u32[]{:S(2)}) copy-start(bf16[192,128]{1,0:T(8,128)(2,1)} %param.9) | copy-start | bytes 147460
  2.0 10.5 %copy-start.1 = (bf16[192,128]{1,0:T(8,128)(2,1)S(1)}, bf16[192,128]{1,0:T(8,128)(2,1)}, u32[]{:S(2)}) copy-start(bf16[192,128]{1,0:T(8,128)(2,1)} %param.6) | copy-start | bytes 147460
  2.0 19.2 %all-to-all-start = ((bf16[8,24,256]{2,1,0:T(8,128)(2,1)}), bf16[8,24,256]{2,1,0:T(8,128)(2,1)S(1)}, u32[]{:S(2)}, u32[]{:S(2)}) async-start(bf16[8,24,256]{2,1,0:T(8,128)(2,1)} %broadcast_in_dim.20), calls=%async_computation | async-start | bytes 196608 | tf_op jit(solution)/shard_map/all_to_all | solution.py:158
  12.5 18.3 %collective-permute-start = (bf16[1,192,256]{2,1,0:T(8,128)(2,1)S(1)}, bf16[1,192,256]{2,1,0:T(8,128)(2,1)S(1)}, u32[]{:S(2)}, u32[]{:S(2)}) collective-permute-start(bf16[1,192,256]{2,1,0:T(8,128)(2,1)S(1)} %maximum_bitcast_fusion), channel_id=1, source_target_pairs={{0,2},{1,3},{2,0},{3,1},{4,6},{5,7},{6,4},{7,5},{8,10},{9,11},{10,... | collective-permute-start | bytes 294920 | tf_op jit(solution)/shard_map/ppermute | solution.py:176
  15.9 0.7 copy-start.2
  22.1 21.1 %all-to-all-start.1 = ((bf16[8,8,24,256]{3,2,1,0:T(8,128)(2,1)}), bf16[8,8,24,256]{3,2,1,0:T(8,128)(2,1)S(1)}, u32[]{:S(2)}, u32[]{:S(2)}) async-start(bf16[8,8,24,256]{3,2,1,0:T(8,128)(2,1)} %broadcast_in_dim.21), calls=%async_computation.1 | async-start | bytes 1572864 | tf_op jit(solution)/shard_map/all_to_all | solution.py:158
  30.1 0.7 copy-start.3
  30.8 8.8 %collective-permute-start.1 = (bf16[2,192,256]{2,1,0:T(8,128)(2,1)S(1)}, bf16[2,192,256]{2,1,0:T(8,128)(2,1)S(1)}, u32[]{:S(2)}, u32[]{:S(2)}) collective-permute-start(bf16[2,192,256]{2,1,0:T(8,128)(2,1)S(1)} %pad_maximum_fusion.1), channel_id=1, source_target_pairs={{0,6},{1,7},{2,4},{3,5},{4,2},{5,3},{6,0},{7,1},{8,14},{9,15},{10,... | collective-permute-start | bytes 589832 | tf_op jit(solution)/shard_map/ppermute | solution.py:176
  39.6 3.6 %collective-permute-start.2 = (bf16[4,192,256]{2,1,0:T(8,128)(2,1)S(1)}, bf16[4,192,256]{2,1,0:T(8,128)(2,1)S(1)}, u32[]{:S(2)}, u32[]{:S(2)}) collective-permute-start(bf16[4,192,256]{2,1,0:T(8,128)(2,1)S(1)} %pad_maximum_fusion.near_ref), channel_id=1, source_target_pairs={{0,1},{1,0},{2,3},{3,2},{4,5},{5,4},{6,7},{7,6},{8,9},{9,8},{10,11... | collective-permute-start | bytes 1179656 | tf_op jit(solution)/shard_map/ppermute | solution.py:181
  72.3 9.1 %collective-permute-start.3 = (bf16[4,24,2048]{2,1,0:T(8,128)(2,1)S(1)}, bf16[4,24,2048]{2,1,0:T(8,128)(2,1)S(1)}, u32[]{:S(2)}, u32[]{:S(2)}) collective-permute-start(bf16[4,24,2048]{2,1,0:T(8,128)(2,1)S(1)} %get-tuple-element.12), channel_id=1, source_target_pairs={{0,1},{1,0},{2,3},{3,2},{4,5},{5,4},{6,7},{7,6},{8,9},{9,8},{10,11... | collective-permute-start | bytes 1179656 | tf_op jit(solution)/shard_map/ppermute | solution.py:181
  74.2 22.7 %all-to-all-start.3 = ((bf16[8,8,24,256]{3,2,1,0:T(8,128)(2,1)}), bf16[8,8,24,256]{3,2,1,0:T(8,128)(2,1)S(1)}, u32[]{:S(2)}, u32[]{:S(2)}) async-start(bf16[8,8,24,256]{3,2,1,0:T(8,128)(2,1)} %bitcast.5), calls=%async_computation.3 | async-start | bytes 1572864 | tf_op jit(solution)/shard_map/all_to_all | solution.py:158
  81.6 8.8 %collective-permute-start.4 = (bf16[2,24,2048]{2,1,0:T(8,128)(2,1)S(1)}, bf16[2,24,2048]{2,1,0:T(8,128)(2,1)S(1)}, u32[]{:S(2)}, u32[]{:S(2)}) collective-permute-start(bf16[2,24,2048]{2,1,0:T(8,128)(2,1)S(1)} %slice.50), channel_id=1, source_target_pairs={{0,6},{1,7},{2,4},{3,5},{4,2},{5,3},{6,0},{7,1},{8,14},{9,15},{10,... | collective-permute-start | bytes 589832 | tf_op jit(solution)/shard_map/ppermute | solution.py:176
  90.4 6.5 %collective-permute-start.5 = (bf16[1,24,2048]{2,1,0:T(8,128)(2,1)S(1)}, bf16[1,24,2048]{2,1,0:T(8,128)(2,1)S(1)}, u32[]{:S(2)}, u32[]{:S(2)}) collective-permute-start(bf16[1,24,2048]{2,1,0:T(8,128)(2,1)S(1)} %slice.51), channel_id=1, source_target_pairs={{0,2},{1,3},{2,0},{3,1},{4,6},{5,7},{6,4},{7,5},{8,10},{9,11},{10,... | collective-permute-start | bytes 294920 | tf_op jit(solution)/shard_map/ppermute | solution.py:176
  97.7 13.7 %all-to-all-start.4 = ((bf16[8,24,256]{2,1,0:T(8,128)(2,1)}), bf16[8,24,256]{2,1,0:T(8,128)(2,1)S(1)}, u32[]{:S(2)}, u32[]{:S(2)}) async-start(bf16[8,24,256]{2,1,0:T(8,128)(2,1)} %reduce_sum.54), calls=%async_computation.4 | async-start | bytes 196608 | tf_op jit(solution)/shard_map/all_to_all | solution.py:158

commit v3 on v2

v3 whole, which is shorter than its diff:
```python
import functools
import math

import jax
import jax.numpy as jnp
from jax import lax
from jax.experimental import pallas as pl
from jax.experimental.pallas import tpu as pltpu
from jax.sharding import PartitionSpec as P

F32 = jnp.float32
BF16 = jnp.bfloat16
LOG2E = 1.4426950408889634
LOW = -1e30
NT = (((1,), (1,)), ((), ()))


def stage_rows(order_ref, sources, q_ref, d_ref, span, hd):
    number = 0
    for src_ref in sources:
        for piece in range(src_ref.shape[0]):
            at = pl.ds(pl.multiple_of(order_ref[number] * span, span), span)
            for half in range(2):
                rows = src_ref[piece, half * span : (half + 1) * span, :]
                q_ref[half, at, :] = rows[:, :hd]
                d_ref[half, at, :] = rows[:, hd:]
            number += 1


def columns(half, half_rows, r, rc):
    first = half * half_rows + r * rc
    return slice(first, first + rc)


def stats_kernel(
    dims, slots_ref, tiles_ref, order_ref, kpos_ref, qpos_ref, near_ref, far_ref, kv_ref,
    stat_ref, kvs_ref, q_ref, d_ref, p_ref, s_s, sort_s,
):
    heads, span, hd, chunks, kc, tk, rc = dims
    factor = LOG2E / math.sqrt(hd)
    half_rows = heads * span
    parts = range(half_rows // rc)

    def place(c, _):
        start = pl.multiple_of(slots_ref[c] * kc, kc)
        sort_s[pl.ds(start, kc), :] = kv_ref[c].astype(F32)
        return 0

    lax.fori_loop(0, chunks, place, 0, unroll=4)
    for t in range(chunks * kc // tk):
        kvs_ref[t * tk : (t + 1) * tk, :] = sort_s[t * tk : (t + 1) * tk, :].astype(BF16)
    stage_rows(order_ref, (near_ref, far_ref), q_ref, d_ref, span, hd)

    for half in range(2):

        def score(masked, t, tops):
            keys = pl.ds(pl.multiple_of(t * tk, tk), tk)
            k = kvs_ref[keys, :hd]
            new = []
            for r in parts:
                cols = slice(r * rc, (r + 1) * rc)
                s = lax.dot_general(k, q_ref[half, cols, :], NT, preferred_element_type=F32)
                s = s * factor
                if masked:
                    s = jnp.where(kpos_ref[keys, :] <= qpos_ref[half : half + 1, cols], s, LOW)
                s_s[keys, cols] = s
                new.append(jnp.maximum(tops[r], jnp.max(s.reshape(tk // 8, 8, rc), axis=0)))
            return tuple(new)

        full, count = tiles_ref[2 * half], tiles_ref[2 * half + 1]
        tops = tuple(jnp.full((8, rc), LOW, F32) for _ in parts)
        tops = lax.fori_loop(0, full, functools.partial(score, False), tops)
        tops = lax.fori_loop(full, count, functools.partial(score, True), tops)
        tops = [jnp.max(top, axis=0, keepdims=True) for top in tops]

        def weigh(t, carried):
            keys = pl.ds(pl.multiple_of(t * tk, tk), tk)
            v = kvs_ref[keys, hd:]
            new = []
            for r in parts:
                cols = slice(r * rc, (r + 1) * rc)
                l, ds = carried[r]
                dp = lax.dot_general(v, d_ref[half, cols, :], NT, preferred_element_type=F32)
                p = jnp.exp2(s_s[keys, cols] - tops[r])
                p_ref[keys, columns(half, half_rows, r, rc)] = p.astype(BF16)
                l = l + jnp.sum(p.reshape(tk // 8, 8, rc), axis=0)
                ds = ds + jnp.sum((p * dp).reshape(tk // 8, 8, rc), axis=0)
                new.append((l, ds))
            return tuple(new)

        zero = jnp.zeros((8, rc), F32)
        sums = lax.fori_loop(0, count, weigh, tuple((zero, zero) for _ in parts))
        for r in parts:
            l = jnp.maximum(jnp.sum(sums[r][0], axis=0, keepdims=True), 1e-30)
            ds = jnp.sum(sums[r][1], axis=0, keepdims=True)
            out = columns(half, half_rows, r, rc)
            stat_ref[0:1, out] = tops[r] + jnp.log2(l)
            stat_ref[1:2, out] = ds / l
            stat_ref[2:3, out] = tops[r]


def grad_kernel(
    dims, slots_ref, tiles_ref, order_ref, stat_ref, all_ref, q_ref, d_ref, kvs_ref, p_ref,
    keep_ref, send_ref, dkv_ref, acc_s, o_s, dq_s, kvt_s, w_s, delta_s, flat_s,
):
    heads, span, hd, chunks, kc, tk, rc = dims
    scaling = 1.0 / math.sqrt(hd)
    half_rows = heads * span
    parts = range(half_rows // rc)
    for t in range(chunks * kc // tk):
        kvt_s[:, t * tk : (t + 1) * tk] = kvs_ref[t * tk : (t + 1) * tk, :].T
    acc_s[...] = jnp.zeros_like(acc_s)
    o_s[...] = jnp.zeros_like(o_s)
    dq_s[...] = jnp.zeros_like(dq_s)
    every = [all_ref[h] for h in range(all_ref.shape[0])]
    top = functools.reduce(jnp.maximum, [e[0:1] for e in every])
    weights = [jnp.exp2(e[0:1] - top) for e in every]
    total = functools.reduce(jnp.add, weights)
    weighted = functools.reduce(jnp.add, [w * e[1:2] for w, e in zip(weights, every)])
    w_s[...] = jnp.exp2(stat_ref[2:3, :] - top - jnp.log2(total))
    delta_s[...] = weighted / total
    for half in range(2):

        def tile(t, _):
            keys = pl.ds(pl.multiple_of(t * tk, tk), tk)
            v = kvs_ref[keys, hd:]
            dk = dv = None
            for r in parts:
                cols = slice(r * rc, (r + 1) * rc)
                out = columns(half, half_rows, r, rc)
                q, d = q_ref[half, cols, :], d_ref[half, cols, :]
                p = p_ref[keys, out].astype(F32) * w_s[:, out]
                dp = lax.dot_general(v, d, NT, preferred_element_type=F32)
                pb = p.astype(BF16)
                g = (p * (dp - delta_s[:, out])).astype(BF16)
                one = jnp.dot(g, q, preferred_element_type=F32)
                two = jnp.dot(pb, d, preferred_element_type=F32)
                dk, dv = (one, two) if dk is None else (dk + one, dv + two)
                dq_s[:, out] += jnp.dot(kvt_s[:hd, keys], g, preferred_element_type=F32)
                o_s[:, out] += jnp.dot(kvt_s[hd:, keys], pb, preferred_element_type=F32)
            acc_s[keys, :hd] += dk
            acc_s[keys, hd:] += dv
            return 0

        lax.fori_loop(0, tiles_ref[2 * half + 1], tile, 0)

    def place(c, _):
        start = pl.multiple_of(slots_ref[c] * kc, kc)
        rows = acc_s[pl.ds(start, kc), :]
        dkv_ref[c, :, :hd] = (rows[:, :hd] * scaling).astype(BF16)
        dkv_ref[c, :, hd:] = rows[:, hd:].astype(BF16)
        return 0

    lax.fori_loop(0, chunks, place, 0, unroll=4)
    blocks = span // kc
    per_core = heads // 2
    for which, (src, scale) in enumerate(((o_s, 1.0), (dq_s, scaling))):
        flat_s[...] = (src[...] * scale).T
        for number in range(heads):
            target = order_ref[number]
            half, block = target // blocks, target % blocks
            out_ref = keep_ref if number < per_core else send_ref
            for h in range(heads):
                first = pl.multiple_of(half * half_rows + h * span + block * kc, kc)
                at = which * heads * hd + h * hd
                out_ref[number % per_core, :, at : at + hd] = flat_s[
                    pl.ds(first, kc), :
                ].astype(BF16)


def run_stats(dims, slots, tiles, order, kpos, qpos, near, far, kv_all):
    heads, span, hd, chunks, kc, _, _ = dims
    half_rows, n_keys = heads * span, chunks * kc
    smem = pl.BlockSpec(memory_space=pltpu.SMEM)
    vmem = pl.BlockSpec(memory_space=pltpu.VMEM)
    return pl.pallas_call(
        functools.partial(stats_kernel, dims),
        out_shape=(
            jax.ShapeDtypeStruct((3, 2 * half_rows), F32),
            jax.ShapeDtypeStruct((n_keys, 2 * hd), BF16),
            jax.ShapeDtypeStruct((2, half_rows, hd), BF16),
            jax.ShapeDtypeStruct((2, half_rows, hd), BF16),
            jax.ShapeDtypeStruct((n_keys, 2 * half_rows), BF16),
        ),
        in_specs=[smem] * 3 + [vmem] * 5,
        out_specs=(vmem,) * 5,
        scratch_shapes=[
            pltpu.VMEM((n_keys, half_rows), F32),
            pltpu.VMEM((n_keys, 2 * hd), F32),
        ],
        compiler_params=pltpu.CompilerParams(vmem_limit_bytes=32 * 1024 * 1024),
        name="attention_stats",
    )(slots, tiles, order, kpos, qpos, near, far, kv_all)


def run_grads(dims, slots, tiles, order, stat, stat_all, q, d, kvs, probs):
    heads, span, hd, chunks, kc, _, _ = dims
    rows, n_keys = 2 * heads * span, chunks * kc
    smem = pl.BlockSpec(memory_space=pltpu.SMEM)
    vmem = pl.BlockSpec(memory_space=pltpu.VMEM)
    return pl.pallas_call(
        functools.partial(grad_kernel, dims),
        out_shape=(
            jax.ShapeDtypeStruct((heads // 2, kc, 2 * heads * hd), BF16),
            jax.ShapeDtypeStruct((heads // 2, kc, 2 * heads * hd), BF16),
            jax.ShapeDtypeStruct((chunks, kc, 2 * hd), BF16),
        ),
        in_specs=[smem] * 3 + [vmem] * 6,
        out_specs=(vmem,) * 3,
        scratch_shapes=[
            pltpu.VMEM((n_keys, 2 * hd), F32),
            pltpu.VMEM((hd, rows), F32),
            pltpu.VMEM((hd, rows), F32),
            pltpu.VMEM((2 * hd, n_keys), BF16),
            pltpu.VMEM((1, rows), F32),
            pltpu.VMEM((1, rows), F32),
            pltpu.VMEM((rows, hd), F32),
        ],
        compiler_params=pltpu.CompilerParams(vmem_limit_bytes=32 * 1024 * 1024),
        name="attention_grads",
    )(slots, tiles, order, stat, stat_all, q, d, kvs, probs)


def grouped(x, groups):
    return lax.all_to_all(
        x, ("ctx", "head"), split_axis=0, concat_axis=0, axis_index_groups=groups, tiled=True
    )


def line_groups(side, heads):
    first, second = [], []
    for head in range(heads):
        for fixed in range(side):
            along_z = [(fixed * side + moving) * heads + head for moving in range(side)]
            along_y = [(moving * side + fixed) * heads + head for moving in range(side)]
            first.append(along_y if head % 2 else along_z)
            second.append(along_z if head % 2 else along_y)
    return first, second


def flip_x(x, mesh_x, mask):
    pairs = [(2 * a + c, 2 * (a ^ mask) + c) for a in range(mesh_x) for c in range(2)]
    return lax.ppermute(x, "head", pairs)


def swap_cores(x, mesh_x):
    pairs = [(2 * a + c, 2 * a + 1 - c) for a in range(mesh_x) for c in range(2)]
    return lax.ppermute(x, "head", pairs)


def local(query_in, key_in, value_in, grad_out, span_of):
    hd = key_in.shape[1]
    kc = key_in.shape[0]
    heads = lax.axis_size("head")
    shards = lax.axis_size("ctx")
    local_rows = query_in.shape[0]
    span = local_rows // 2
    n_keys = shards * kc
    tk = math.gcd(n_keys, 256)
    rc = heads * span
    dims = (heads, span, hd, shards, kc, tk, rc)
    blocks = span // kc
    ctx = lax.axis_index("ctx")
    head = lax.axis_index("head")

    mesh_x = heads // 2
    at_x, core = head // 2, head % 2
    masks = [2 ** (bit + 1) - 1 for bit in range(mesh_x.bit_length() - 1)]
    offsets = [0]
    for mask in masks:
        offsets = offsets + [mask ^ offset for offset in offsets]
    origin = jnp.bitwise_xor(at_x, jnp.array(offsets, jnp.int32)) * 2
    order = jnp.concatenate([origin + core, origin + 1 - core]).astype(jnp.int32)
    side = math.isqrt(shards)
    first, second = line_groups(side, heads)

    spans = span_of.reshape(shards, 2)
    key_span = lax.dynamic_index_in_dim(spans, head // blocks, 1, keepdims=False)
    own = lax.dynamic_index_in_dim(spans, ctx, 0, keepdims=False)
    rank = jnp.sum((key_span[None, :] < key_span[:, None]).astype(jnp.int32), axis=1)
    place = jnp.arange(shards, dtype=jnp.int32)
    crossed = rank.reshape(side, side).T.reshape(shards)
    slots = jnp.where(core == 0, rank, crossed)
    ordered = jnp.sum(jnp.where(rank[None, :] == place[:, None], key_span[None, :], 0), axis=1)
    kpos = (
        ordered[:, None] * span
        + (head % blocks) * kc
        + jnp.arange(kc, dtype=jnp.int32)[None, :]
    ).reshape(n_keys, 1)
    qpos = own[:, None] * span + jnp.tile(jnp.arange(span, dtype=jnp.int32), heads)[None, :]
    before = jnp.sum((key_span[None, :] < own[:, None]).astype(jnp.int32), axis=1) * kc
    seen = jnp.sum((key_span[None, :] <= own[:, None]).astype(jnp.int32), axis=1) * kc
    tiles = jnp.stack([before // tk, (seen + tk - 1) // tk], axis=1).reshape(4)

    kv = jnp.concatenate([key_in, value_in], axis=1)
    qd = jnp.concatenate([query_in, grad_out], axis=1)
    near = qd[None]
    near = jnp.concatenate([near, flip_x(near, mesh_x, masks[0])])
    kv_line = grouped(jnp.broadcast_to(kv[None], (side, kc, 2 * hd)), first)
    kv_line, near = lax.optimization_barrier((kv_line, near))
    kv_all = grouped(jnp.broadcast_to(kv_line[None], (side, side, kc, 2 * hd)), second)
    kv_all = kv_all.reshape(shards, kc, 2 * hd)
    for mask in masks[1:]:
        near = jnp.concatenate([near, flip_x(near, mesh_x, mask)])
    far = swap_cores(near, mesh_x)

    stat, kvs, q, d, probs = run_stats(dims, slots, tiles, order, kpos, qpos, near, far, kv_all)
    rows = 2 * heads * span
    stat_all = lax.all_to_all(
        jnp.broadcast_to(stat[None, :2], (heads, 2, rows)), "head", 0, 0, tiled=True
    )
    keep, send, key_parts = run_grads(
        dims, slots, tiles, order, stat, stat_all, q, d, kvs, probs
    )

    key_line = grouped(key_parts.reshape(side, side, kc, 2 * hd), second)
    key_line = jnp.sum(key_line.astype(F32), axis=0).astype(BF16)

    row_sum = keep.astype(F32) + swap_cores(send, mesh_x).astype(F32)
    for mask in reversed(masks):
        if mask == masks[0]:
            key_line, row_sum = lax.optimization_barrier((key_line, row_sum))
            key_sum = jnp.sum(grouped(key_line, first).astype(F32), axis=0).astype(BF16)
        half = row_sum.shape[0] // 2
        moved = flip_x(row_sum[half:].astype(BF16), mesh_x, mask)
        row_sum = row_sum[:half] + moved.astype(F32)
    row_sum = row_sum[0].astype(BF16)
    width = heads * hd
    return (row_sum[:, :width], row_sum[:, width:], key_sum[:, :hd], key_sum[:, hd:])


def solution(mesh):
    return jax.shard_map(
        local,
        mesh=mesh,
        in_specs=(
            P("ctx", "head"),
            P(("ctx", "head"), None),
            P(("ctx", "head"), None),
            P("ctx", "head"),
            P(),
        ),
        out_specs=(P(("ctx", "head"), None),) * 4,
        check_vma=False,
    )
```

time: 113 us -> 109 us (0.965)
  the two profiles are of different devices: /device:TPU:24 before, /device:TPU:2 now
where the time goes in v3:
time: 109 us; the launch traced here: 108 us
  starting transfers between devices  42.8 us (39%)
  waiting for transfers between devices  34.8 us (32%)
  Pallas kernels  12 us (11%)
  blocking collectives  8.96 us (8%)
  local copies, waits for them, and re-layouts  4.62 us (4%)
  other arithmetic  3.89 us (4%)
    all_to_all x4, starting transfers between devices, grouped(): lax.all_to_all(x, ('ctx', 'head'), split_axis=0, concat_axis=0, axis_inde...  27.5 us
    all_to_all x4, waiting for transfers between devices, grouped(): lax.all_to_all(x, ('ctx', 'head'), split_axis=0, concat_axis=0, axis_inde...  20.5 us
    ppermute x4, waiting for transfers between devices, flip_x(): return lax.ppermute(x, 'head', pairs)  12.7 us
    ppermute x4, starting transfers between devices, flip_x(): return lax.ppermute(x, 'head', pairs)  11.4 us
    all_to_all x1, blocking collectives, local(): lax.all_to_all(jnp.broadcast_to(stat[None, :2], (heads, 2, rows)), 'head'...  8.96 us
    pallas_call x1, Pallas kernels, run_grads(): pl.pallas_call(functools.partial(grad_kernel, dims), out_shape=(jax.Shape...  7.06 us
    pallas_call x1, Pallas kernels, run_stats(): pl.pallas_call(functools.partial(stats_kernel, dims), out_shape=(jax.Shap...  4.96 us
    ppermute x2, starting transfers between devices, swap_cores(): return lax.ppermute(x, 'head', pairs)  3.83 us
  transfers between devices with their start and end apart: 10, of which 8 were waited for; matrix products, arithmetic and copies ran while one was open for 4% of the time, Pallas kernels for 0%

profile of v3, /device:TPU:2, one launch (start us, length us, event | category | flops | bytes accessed | tf_op | source)
XLA Modules:
  0.0 107.9 jit_solution(15444068690783201208)
XLA Ops:
  2.0 10.3 %all-to-all-start = ((bf16[8,24,256]{2,1,0:T(8,128)(2,1)}), bf16[8,24,256]{2,1,0:T(8,128)(2,1)S(1)}, u32[]{:S(2)}, u32[]{:S(2)}) async-start(bf16[8,24,256]{2,1,0:T(8,128)(2,1)} %broadcast_in_dim.19), calls=%async_computation | async-start | bytes 196608 | tf_op jit(solution)/shard_map/all_to_all | solution.py:225
  12.3 0.8 maximum_bitcast_fusion
  13.1 2.4 %collective-permute-start = (bf16[1,192,256]{2,1,0:T(8,128)(2,1)S(1)}, bf16[1,192,256]{2,1,0:T(8,128)(2,1)S(1)}, u32[]{:S(2)}, u32[]{:S(2)}) collective-permute-start(bf16[1,192,256]{2,1,0:T(8,128)(2,1)S(1)} %maximum_bitcast_fusion), channel_id=1, source_target_pairs={{0,2},{1,3},{2,0},{3,1},{4,6},{5,7},{6,4},{7,5},{8,10},{9,11},{10,... | collective-permute-start | bytes 294920 | tf_op jit(solution)/shard_map/ppermute | solution.py:243
  15.6 0.8 reshape.185
  17.6 2.0 %collective-permute-done = bf16[1,192,256]{2,1,0:T(8,128)(2,1)S(1)} collective-permute-done((bf16[1,192,256]{2,1,0:T(8,128)(2,1)S(1)}, bf16[1,192,256]{2,1,0:T(8,128)(2,1)S(1)}, u32[]{:S(2)}, u32[]{:S(2)}) %collective-permute-start) | collective-permute-done | bytes 98336 | tf_op jit(solution)/shard_map/ppermute | solution.py:243
  19.7 1.4 %all-to-all-done = bf16[8,24,256]{2,1,0:T(8,128)(2,1)S(1)} async-done(((bf16[8,24,256]{2,1,0:T(8,128)(2,1)}), bf16[8,24,256]{2,1,0:T(8,128)(2,1)S(1)}, u32[]{:S(2)}, u32[]{:S(2)}) %all-to-all-start) | async-done | bytes 98336 | tf_op jit(solution)/shard_map/all_to_all | solution.py:225
  21.0 0.9 broadcast_in_dim.21
  22.0 7.1 %all-to-all-start.1 = ((bf16[8,8,24,256]{3,2,1,0:T(8,128)(2,1)}), bf16[8,8,24,256]{3,2,1,0:T(8,128)(2,1)S(1)}, u32[]{:S(2)}, u32[]{:S(2)}) async-start(bf16[8,8,24,256]{3,2,1,0:T(8,128)(2,1)} %broadcast_in_dim.21), calls=%async_computation.1 | async-start | bytes 1572864 | tf_op jit(solution)/shard_map/all_to_all | solution.py:225
  30.1 3.4 %collective-permute-start.1 = (bf16[2,192,256]{2,1,0:T(8,128)(2,1)S(1)}, bf16[2,192,256]{2,1,0:T(8,128)(2,1)S(1)}, u32[]{:S(2)}, u32[]{:S(2)}) collective-permute-start(bf16[2,192,256]{2,1,0:T(8,128)(2,1)S(1)} %pad_maximum_fusion), channel_id=1, source_target_pairs={{0,6},{1,7},{2,4},{3,5},{4,2},{5,3},{6,0},{7,1},{8,14},{9,15},{10,... | collective-permute-start | bytes 589832 | tf_op jit(solution)/shard_map/ppermute | solution.py:243
  33.6 4.1 %collective-permute-done.1 = bf16[2,192,256]{2,1,0:T(8,128)(2,1)S(1)} collective-permute-done((bf16[2,192,256]{2,1,0:T(8,128)(2,1)S(1)}, bf16[2,192,256]{2,1,0:T(8,128)(2,1)S(1)}, u32[]{:S(2)}, u32[]{:S(2)}) %collective-permute-start.1) | collective-permute-done | bytes 196640 | tf_op jit(solution)/shard_map/ppermute | solution.py:243
  37.7 1.9 %collective-permute-start.2 = (bf16[4,192,256]{2,1,0:T(8,128)(2,1)S(1)}, bf16[4,192,256]{2,1,0:T(8,128)(2,1)S(1)}, u32[]{:S(2)}, u32[]{:S(2)}) collective-permute-start(bf16[4,192,256]{2,1,0:T(8,128)(2,1)S(1)} %constant_dynamic-update-slice_fusion.near_ref), channel_id=1, source_target_pairs={{0,1},{1,0},{2,3},{3,2},{4,5},{5,4},{6,7},{7,6},{8,9},{9,8},{10,11... | collective-permute-start | bytes 1179656 | tf_op jit(solution)/shard_map/ppermute | solution.py:248
  39.7 1.6 %collective-permute-done.2.far_ref = bf16[4,192,256]{2,1,0:T(8,128)(2,1)S(1)} collective-permute-done((bf16[4,192,256]{2,1,0:T(8,128)(2,1)S(1)}, bf16[4,192,256]{2,1,0:T(8,128)(2,1)S(1)}, u32[]{:S(2)}, u32[]{:S(2)}) %collective-permute-start.2) | collective-permute-done | bytes 393248 | tf_op jit(solution)/shard_map/ppermute | solution.py:248
  41.3 3.9 %all-to-all-done.1 = bf16[8,8,24,256]{3,2,1,0:T(8,128)(2,1)S(1)} async-done(((bf16[8,8,24,256]{3,2,1,0:T(8,128)(2,1)}), bf16[8,8,24,256]{3,2,1,0:T(8,128)(2,1)S(1)}, u32[]{:S(2)}, u32[]{:S(2)}) %all-to-all-start.1) | async-done | bytes 786464 | tf_op jit(solution)/shard_map/all_to_all | solution.py:225
  45.2 5.0 %attention_stats.1 = (f32[3,1536]{1,0:T(4,128)S(1)}, bf16[1536,256]{1,0:T(8,128)(2,1)S(1)}, bf16[2,768,128]{2,1,0:T(8,128)(2,1)S(1)}, bf16[2,768,128]{2,1,0:T(8,128)(2,1)S(1)}, bf16[1536,1536]{1,0:T(8,128)(2,1)S(1)}) custom-call(s32[64]{0:T(128)S(1)} %broadcast_select_fusion.slots_ref, s32[4]{0:T(128)S(1)} %reshape.188.tiles_ref, ...), custom_call_target="tpu_custom_call" | custom-call | tf_op jit(solution)/shard_map/attention_stats/pallas_call | solution.py:176
  50.2 9.0 %all_to_all.25.all_ref = f32[8,2,1536]{2,1,0:T(2,128)S(1)} all-to-all(f32[8,2,1536]{2,1,0:T(2,128)S(1)} %broadcast_in_dim.22), channel_id=1, replica_groups=mesh['ctx'=64,'head'=8] {'head'}, dimensions={0} | all-to-all | bytes 196608 | tf_op jit(solution)/shard_map/all_to_all | solution.py:309
  59.2 7.1 %attention_grads.1 = (bf16[4,24,2048]{2,1,0:T(8,128)(2,1)S(1)}, bf16[4,24,2048]{2,1,0:T(8,128)(2,1)S(1)}, bf16[64,24,256]{2,1,0:T(8,128)(2,1)}) custom-call(s32[64]{0:T(128)S(1)} %broadcast_select_fusion.slots_ref, s32[4]{0:T(128)S(1)} %reshape.188.tiles_ref, s32[8]{0:T(128)S(1)} %pad_add_fusion.1.order_ref, f32[3,1536]{1,0:T(4,128)S(1)} %get-tuple-element.18.stat_ref, ...), custom_call_target="tpu_custom_call" | custom-call | tf_op jit(solution)/shard_map/attention_grads/pallas_call | solution.py:201
  66.2 1.9 %collective-permute-start.3 = (bf16[4,24,2048]{2,1,0:T(8,128)(2,1)S(1)}, bf16[4,24,2048]{2,1,0:T(8,128)(2,1)S(1)}, u32[]{:S(2)}, u32[]{:S(2)}) collective-permute-start(bf16[4,24,2048]{2,1,0:T(8,128)(2,1)S(1)} %get-tuple-element.25), channel_id=1, source_target_pairs={{0,1},{1,0},{2,3},{3,2},{4,5},{5,4},{6,7},{7,6},{8,9},{9,8},{10,11... | collective-permute-start | bytes 1179656 | tf_op jit(solution)/shard_map/ppermute | solution.py:248
  68.2 4.2 %all-to-all-start.3 = ((bf16[8,8,24,256]{3,2,1,0:T(8,128)(2,1)}), bf16[8,8,24,256]{3,2,1,0:T(8,128)(2,1)S(1)}, u32[]{:S(2)}, u32[]{:S(2)}) async-start(bf16[8,8,24,256]{3,2,1,0:T(8,128)(2,1)} %bitcast.6), calls=%async_computation.3 | async-start | bytes 1572864 | tf_op jit(solution)/shard_map/all_to_all | solution.py:225
  72.5 2.2 %collective-permute-start.4 = (bf16[2,24,2048]{2,1,0:T(8,128)(2,1)S(1)}, bf16[2,24,2048]{2,1,0:T(8,128)(2,1)S(1)}, u32[]{:S(2)}, u32[]{:S(2)}) collective-permute-start(bf16[2,24,2048]{2,1,0:T(8,128)(2,1)S(1)} %slice.51), channel_id=1, source_target_pairs={{0,6},{1,7},{2,4},{3,5},{4,2},{5,3},{6,0},{7,1},{8,14},{9,15},{10,... | collective-permute-start | bytes 589832 | tf_op jit(solution)/shard_map/ppermute | solution.py:243
  74.8 6.6 %collective-permute-done.4 = bf16[2,24,2048]{2,1,0:T(8,128)(2,1)S(1)} collective-permute-done((bf16[2,24,2048]{2,1,0:T(8,128)(2,1)S(1)}, bf16[2,24,2048]{2,1,0:T(8,128)(2,1)S(1)}, u32[]{:S(2)}, u32[]{:S(2)}) %collective-permute-start.4) | collective-permute-done | bytes 196640 | tf_op jit(solution)/shard_map/ppermute | solution.py:243
  81.4 7.1 %all-to-all-done.3 = bf16[8,8,24,256]{3,2,1,0:T(8,128)(2,1)S(1)} async-done(((bf16[8,8,24,256]{3,2,1,0:T(8,128)(2,1)}), bf16[8,8,24,256]{3,2,1,0:T(8,128)(2,1)S(1)}, u32[]{:S(2)}, u32[]{:S(2)}) %all-to-all-start.3) | async-done | bytes 786464 | tf_op jit(solution)/shard_map/all_to_all | solution.py:225
  89.3 3.4 %collective-permute-start.5 = (bf16[1,24,2048]{2,1,0:T(8,128)(2,1)S(1)}, bf16[1,24,2048]{2,1,0:T(8,128)(2,1)S(1)}, u32[]{:S(2)}, u32[]{:S(2)}) collective-permute-start(bf16[1,24,2048]{2,1,0:T(8,128)(2,1)S(1)} %slice.52), channel_id=1, source_target_pairs={{0,2},{1,3},{2,0},{3,1},{4,6},{5,7},{6,4},{7,5},{8,10},{9,11},{10,... | collective-permute-start | bytes 294920 | tf_op jit(solution)/shard_map/ppermute | solution.py:243
  92.7 5.9 %all-to-all-start.4 = ((bf16[8,24,256]{2,1,0:T(8,128)(2,1)}), bf16[8,24,256]{2,1,0:T(8,128)(2,1)S(1)}, u32[]{:S(2)}, u32[]{:S(2)}) async-start(bf16[8,24,256]{2,1,0:T(8,128)(2,1)} %reduce_sum.64), calls=%async_computation.4 | async-start | bytes 196608 | tf_op jit(solution)/shard_map/all_to_all | solution.py:225
  99.2 8.1 %all-to-all-done.4 = bf16[8,24,256]{2,1,0:T(8,128)(2,1)S(1)} async-done(((bf16[8,24,256]{2,1,0:T(8,128)(2,1)}), bf16[8,24,256]{2,1,0:T(8,128)(2,1)S(1)}, u32[]{:S(2)}, u32[]{:S(2)}) %all-to-all-start.4) | async-done | bytes 98336 | tf_op jit(solution)/shard_map/all_to_all | solution.py:225
  (39 shorter events, 6.0 us)
Async XLA Ops:
  2.0 19.0 %all-to-all-start = ((bf16[8,24,256]{2,1,0:T(8,128)(2,1)}), bf16[8,24,256]{2,1,0:T(8,128)(2,1)S(1)}, u32[]{:S(2)}, u32[]{:S(2)}) async-start(bf16[8,24,256]{2,1,0:T(8,128)(2,1)} %broadcast_in_dim.19), calls=%async_computation | async-start | bytes 196608 | tf_op jit(solution)/shard_map/all_to_all | solution.py:225
  13.1 6.5 %collective-permute-start = (bf16[1,192,256]{2,1,0:T(8,128)(2,1)S(1)}, bf16[1,192,256]{2,1,0:T(8,128)(2,1)S(1)}, u32[]{:S(2)}, u32[]{:S(2)}) collective-permute-start(bf16[1,192,256]{2,1,0:T(8,128)(2,1)S(1)} %maximum_bitcast_fusion), channel_id=1, source_target_pairs={{0,2},{1,3},{2,0},{3,1},{4,6},{5,7},{6,4},{7,5},{8,10},{9,11},{10,... | collective-permute-start | bytes 294920 | tf_op jit(solution)/shard_map/ppermute | solution.py:243
  22.0 23.2 %all-to-all-start.1 = ((bf16[8,8,24,256]{3,2,1,0:T(8,128)(2,1)}), bf16[8,8,24,256]{3,2,1,0:T(8,128)(2,1)S(1)}, u32[]{:S(2)}, u32[]{:S(2)}) async-start(bf16[8,8,24,256]{3,2,1,0:T(8,128)(2,1)} %broadcast_in_dim.21), calls=%async_computation.1 | async-start | bytes 1572864 | tf_op jit(solution)/shard_map/all_to_all | solution.py:225
  30.1 7.6 %collective-permute-start.1 = (bf16[2,192,256]{2,1,0:T(8,128)(2,1)S(1)}, bf16[2,192,256]{2,1,0:T(8,128)(2,1)S(1)}, u32[]{:S(2)}, u32[]{:S(2)}) collective-permute-start(bf16[2,192,256]{2,1,0:T(8,128)(2,1)S(1)} %pad_maximum_fusion), channel_id=1, source_target_pairs={{0,6},{1,7},{2,4},{3,5},{4,2},{5,3},{6,0},{7,1},{8,14},{9,15},{10,... | collective-permute-start | bytes 589832 | tf_op jit(solution)/shard_map/ppermute | solution.py:243
  37.7 3.6 %collective-permute-start.2 = (bf16[4,192,256]{2,1,0:T(8,128)(2,1)S(1)}, bf16[4,192,256]{2,1,0:T(8,128)(2,1)S(1)}, u32[]{:S(2)}, u32[]{:S(2)}) collective-permute-start(bf16[4,192,256]{2,1,0:T(8,128)(2,1)S(1)} %constant_dynamic-update-slice_fusion.near_ref), channel_id=1, source_target_pairs={{0,1},{1,0},{2,3},{3,2},{4,5},{5,4},{6,7},{7,6},{8,9},{9,8},{10,11... | collective-permute-start | bytes 1179656 | tf_op jit(solution)/shard_map/ppermute | solution.py:248
  66.2 6.2 %collective-permute-start.3 = (bf16[4,24,2048]{2,1,0:T(8,128)(2,1)S(1)}, bf16[4,24,2048]{2,1,0:T(8,128)(2,1)S(1)}, u32[]{:S(2)}, u32[]{:S(2)}) collective-permute-start(bf16[4,24,2048]{2,1,0:T(8,128)(2,1)S(1)} %get-tuple-element.25), channel_id=1, source_target_pairs={{0,1},{1,0},{2,3},{3,2},{4,5},{5,4},{6,7},{7,6},{8,9},{9,8},{10,11... | collective-permute-start | bytes 1179656 | tf_op jit(solution)/shard_map/ppermute | solution.py:248
  68.2 20.4 %all-to-all-start.3 = ((bf16[8,8,24,256]{3,2,1,0:T(8,128)(2,1)}), bf16[8,8,24,256]{3,2,1,0:T(8,128)(2,1)S(1)}, u32[]{:S(2)}, u32[]{:S(2)}) async-start(bf16[8,8,24,256]{3,2,1,0:T(8,128)(2,1)} %bitcast.6), calls=%async_computation.3 | async-start | bytes 1572864 | tf_op jit(solution)/shard_map/all_to_all | solution.py:225
  72.5 8.8 %collective-permute-start.4 = (bf16[2,24,2048]{2,1,0:T(8,128)(2,1)S(1)}, bf16[2,24,2048]{2,1,0:T(8,128)(2,1)S(1)}, u32[]{:S(2)}, u32[]{:S(2)}) collective-permute-start(bf16[2,24,2048]{2,1,0:T(8,128)(2,1)S(1)} %slice.51), channel_id=1, source_target_pairs={{0,6},{1,7},{2,4},{3,5},{4,2},{5,3},{6,0},{7,1},{8,14},{9,15},{10,... | collective-permute-start | bytes 589832 | tf_op jit(solution)/shard_map/ppermute | solution.py:243
  89.3 9.3 %collective-permute-start.5 = (bf16[1,24,2048]{2,1,0:T(8,128)(2,1)S(1)}, bf16[1,24,2048]{2,1,0:T(8,128)(2,1)S(1)}, u32[]{:S(2)}, u32[]{:S(2)}) collective-permute-start(bf16[1,24,2048]{2,1,0:T(8,128)(2,1)S(1)} %slice.52), channel_id=1, source_target_pairs={{0,2},{1,3},{2,0},{3,1},{4,6},{5,7},{6,4},{7,5},{8,10},{9,11},{10,... | collective-permute-start | bytes 294920 | tf_op jit(solution)/shard_map/ppermute | solution.py:243
  92.7 14.6 %all-to-all-start.4 = ((bf16[8,24,256]{2,1,0:T(8,128)(2,1)}), bf16[8,24,256]{2,1,0:T(8,128)(2,1)S(1)}, u32[]{:S(2)}, u32[]{:S(2)}) async-start(bf16[8,24,256]{2,1,0:T(8,128)(2,1)} %reduce_sum.64), calls=%async_computation.4 | async-start | bytes 196608 | tf_op jit(solution)/shard_map/all_to_all | solution.py:225

commit v4 on v3

v4 whole, which is shorter than its diff:
```python
import functools
import math

import jax
import jax.numpy as jnp
from jax import lax
from jax.experimental import pallas as pl
from jax.experimental.pallas import tpu as pltpu
from jax.sharding import PartitionSpec as P

F32 = jnp.float32
BF16 = jnp.bfloat16
LOG2E = 1.4426950408889634
LOW = -1e30
NT = (((1,), (1,)), ((), ()))


def stage_rows(order_ref, sources, q_ref, d_ref, span, hd):
    for number, src_ref in enumerate(sources):
        at = pl.ds(pl.multiple_of(order_ref[number] * span, span), span)
        for half in range(2):
            rows = src_ref[half * span : (half + 1) * span, :]
            q_ref[half, at, :] = rows[:, :hd]
            d_ref[half, at, :] = rows[:, hd:]


def tile_copies(pairs, sems, half, t, tk):
    at = (half, pl.ds(pl.multiple_of(t * tk, tk), tk))
    return [
        pltpu.make_async_copy(src.at[at], dst.at[at], sems.at[which, half, t])
        for which, (src, dst) in enumerate(pairs)
    ]


def start_all(tiles_ref, pairs, sems, tk):
    for half in range(2):

        def step(t, _):
            for copy in tile_copies(pairs, sems, half, t, tk):
                copy.start()
            return 0

        lax.fori_loop(0, tiles_ref[2 * half + 1], step, 0)


def wait_all(tiles_ref, pairs, sems, tk):
    for half in range(2):

        def step(t, _):
            for copy in tile_copies(pairs, sems, half, t, tk):
                copy.wait()
            return 0

        lax.fori_loop(0, tiles_ref[2 * half + 1], step, 0)


def columns(half, half_rows, r, rc):
    first = half * half_rows + r * rc
    return slice(first, first + rc)


def stats_kernel(
    dims, slots_ref, tiles_ref, order_ref, kpos_ref, qpos_ref, kv_ref, *refs
):
    heads, span, hd, chunks, kc, tk, rc = dims
    row_refs = refs[:heads]
    stat_ref, kvs_ref, q_ref, d_ref, probs_ref, s_s, sort_s, p_s, sems = refs[heads:]
    pairs = ((p_s, probs_ref),)
    factor = LOG2E / math.sqrt(hd)
    half_rows = heads * span
    parts = range(half_rows // rc)

    def place(c, _):
        start = pl.multiple_of(slots_ref[c] * kc, kc)
        sort_s[pl.ds(start, kc), :] = kv_ref[c].astype(F32)
        return 0

    lax.fori_loop(0, chunks, place, 0, unroll=4)
    for t in range(chunks * kc // tk):
        kvs_ref[t * tk : (t + 1) * tk, :] = sort_s[t * tk : (t + 1) * tk, :].astype(BF16)
    stage_rows(order_ref, row_refs, q_ref, d_ref, span, hd)

    for half in range(2):

        def score(masked, t, tops):
            keys = pl.ds(pl.multiple_of(t * tk, tk), tk)
            k = kvs_ref[keys, :hd]
            new = []
            for r in parts:
                cols = slice(r * rc, (r + 1) * rc)
                s = lax.dot_general(k, q_ref[half, cols, :], NT, preferred_element_type=F32)
                s = s * factor
                if masked:
                    s = jnp.where(kpos_ref[keys, :] <= qpos_ref[half : half + 1, cols], s, LOW)
                s_s[keys, cols] = s
                new.append(jnp.maximum(tops[r], jnp.max(s.reshape(tk // 8, 8, rc), axis=0)))
            return tuple(new)

        full, count = tiles_ref[2 * half], tiles_ref[2 * half + 1]
        tops = tuple(jnp.full((8, rc), LOW, F32) for _ in parts)
        tops = lax.fori_loop(0, full, functools.partial(score, False), tops)
        tops = lax.fori_loop(full, count, functools.partial(score, True), tops)
        tops = [jnp.max(top, axis=0, keepdims=True) for top in tops]

        def weigh(t, carried):
            keys = pl.ds(pl.multiple_of(t * tk, tk), tk)
            v = kvs_ref[keys, hd:]
            new = []
            for r in parts:
                cols = slice(r * rc, (r + 1) * rc)
                l, ds = carried[r]
                dp = lax.dot_general(v, d_ref[half, cols, :], NT, preferred_element_type=F32)
                p = jnp.exp2(s_s[keys, cols] - tops[r])
                p_s[half, keys, cols] = p.astype(BF16)
                l = l + jnp.sum(p.reshape(tk // 8, 8, rc), axis=0)
                ds = ds + jnp.sum((p * dp).reshape(tk // 8, 8, rc), axis=0)
                new.append((l, ds))
            for copy in tile_copies(pairs, sems, half, t, tk):
                copy.start()
            return tuple(new)

        zero = jnp.zeros((8, rc), F32)
        sums = lax.fori_loop(0, count, weigh, tuple((zero, zero) for _ in parts))
        for r in parts:
            l = jnp.maximum(jnp.sum(sums[r][0], axis=0, keepdims=True), 1e-30)
            ds = jnp.sum(sums[r][1], axis=0, keepdims=True)
            out = columns(half, half_rows, r, rc)
            stat_ref[0:1, out] = tops[r] + jnp.log2(l)
            stat_ref[1:2, out] = ds / l
            stat_ref[2:3, out] = tops[r]
    wait_all(tiles_ref, pairs, sems, tk)


def key_kernel(
    dims, slots_ref, tiles_ref, stat_ref, all_ref, q_ref, d_ref, kvs_ref, probs_ref,
    grads_ref, w_ref, dkv_ref, acc_s, delta_s, p_s, g_s, load_sems, store_sems,
):
    heads, span, hd, chunks, kc, tk, rc = dims
    loads, stores = ((probs_ref, p_s),), ((g_s, grads_ref),)
    start_all(tiles_ref, loads, load_sems, tk)
    scaling = 1.0 / math.sqrt(hd)
    half_rows = heads * span
    parts = range(half_rows // rc)
    acc_s[...] = jnp.zeros_like(acc_s)
    every = [all_ref[h] for h in range(all_ref.shape[0])]
    top = functools.reduce(jnp.maximum, [e[0:1] for e in every])
    weights = [jnp.exp2(e[0:1] - top) for e in every]
    total = functools.reduce(jnp.add, weights)
    weighted = functools.reduce(jnp.add, [w * e[1:2] for w, e in zip(weights, every)])
    w_ref[...] = jnp.exp2(stat_ref[2:3, :] - top - jnp.log2(total))
    delta_s[...] = weighted / total

    for half in range(2):

        def tile(t, _):
            keys = pl.ds(pl.multiple_of(t * tk, tk), tk)
            v = kvs_ref[keys, hd:]
            for copy in tile_copies(loads, load_sems, half, t, tk):
                copy.wait()
            dk = dv = None
            for r in parts:
                cols = slice(r * rc, (r + 1) * rc)
                out = columns(half, half_rows, r, rc)
                q, d = q_ref[half, cols, :], d_ref[half, cols, :]
                p = p_s[half, keys, cols].astype(F32) * w_ref[:, out]
                dp = lax.dot_general(v, d, NT, preferred_element_type=F32)
                g = (p * (dp - delta_s[:, out])).astype(BF16)
                g_s[half, keys, cols] = g
                one = jnp.dot(g, q, preferred_element_type=F32)
                two = jnp.dot(p.astype(BF16), d, preferred_element_type=F32)
                dk, dv = (one, two) if dk is None else (dk + one, dv + two)
            acc_s[keys, :hd] += dk
            acc_s[keys, hd:] += dv
            for copy in tile_copies(stores, store_sems, half, t, tk):
                copy.start()
            return 0

        lax.fori_loop(0, tiles_ref[2 * half + 1], tile, 0)

    def place(c, _):
        start = pl.multiple_of(slots_ref[c] * kc, kc)
        rows = acc_s[pl.ds(start, kc), :]
        dkv_ref[c, :, :hd] = (rows[:, :hd] * scaling).astype(BF16)
        dkv_ref[c, :, hd:] = rows[:, hd:].astype(BF16)
        return 0

    lax.fori_loop(0, chunks, place, 0, unroll=4)
    wait_all(tiles_ref, stores, store_sems, tk)


def row_kernel(dims, tiles_ref, target_ref, w_ref, kvs_ref, probs_ref, grads_ref, *refs):
    heads, span, hd, chunks, kc, tk, rc = dims
    out_refs = refs[:heads]
    o_s, dq_s, kvt_s, flat_s, p_s, g_s, sems = refs[heads:]
    scaling = 1.0 / math.sqrt(hd)
    half_rows = heads * span

    loads = ((probs_ref, p_s), (grads_ref, g_s))
    start_all(tiles_ref, loads, sems, tk)
    for t in range(chunks * kc // tk):
        kvt_s[:, t * tk : (t + 1) * tk] = kvs_ref[t * tk : (t + 1) * tk, :].T
    o_s[...] = jnp.zeros_like(o_s)
    dq_s[...] = jnp.zeros_like(dq_s)
    for half in range(2):

        def tile(t, _):
            keys = pl.ds(pl.multiple_of(t * tk, tk), tk)
            for copy in tile_copies(loads, sems, half, t, tk):
                copy.wait()
            for r in range(half_rows // rc):
                cols = slice(r * rc, (r + 1) * rc)
                out = columns(half, half_rows, r, rc)
                dq_s[:, out] += jnp.dot(
                    kvt_s[:hd, keys], g_s[half, keys, cols], preferred_element_type=F32
                )
                o_s[:, out] += jnp.dot(
                    kvt_s[hd:, keys], p_s[half, keys, cols], preferred_element_type=F32
                )
            return 0

        lax.fori_loop(0, tiles_ref[2 * half + 1], tile, 0)

    blocks = span // kc
    for which, (src, scale) in enumerate(((o_s, w_ref[...]), (dq_s, scaling))):
        flat_s[...] = (src[...] * scale).T
        for number in range(heads):
            target = target_ref[number]
            half, block = target // blocks, target % blocks
            for h in range(heads):
                first = pl.multiple_of(half * half_rows + h * span + block * kc, kc)
                at = which * heads * hd + h * hd
                out_refs[number][:, at : at + hd] = flat_s[pl.ds(first, kc), :].astype(BF16)


def run_stats(dims, slots, tiles, order, kpos, qpos, kv_all, row_parts):
    heads, span, hd, chunks, kc, tk, _ = dims
    half_rows, n_keys = heads * span, chunks * kc
    smem = pl.BlockSpec(memory_space=pltpu.SMEM)
    vmem = pl.BlockSpec(memory_space=pltpu.VMEM)
    hbm = pl.BlockSpec(memory_space=pltpu.HBM)
    return pl.pallas_call(
        functools.partial(stats_kernel, dims),
        out_shape=(
            jax.ShapeDtypeStruct((3, 2 * half_rows), F32),
            jax.ShapeDtypeStruct((n_keys, 2 * hd), BF16),
            jax.ShapeDtypeStruct((2, half_rows, hd), BF16),
            jax.ShapeDtypeStruct((2, half_rows, hd), BF16),
            jax.ShapeDtypeStruct((2, n_keys, half_rows), BF16),
        ),
        in_specs=[smem] * 3 + [vmem] * (3 + heads),
        out_specs=(vmem,) * 4 + (hbm,),
        scratch_shapes=[
            pltpu.VMEM((n_keys, half_rows), F32),
            pltpu.VMEM((n_keys, 2 * hd), F32),
            pltpu.VMEM((2, n_keys, half_rows), BF16),
            pltpu.SemaphoreType.DMA((1, 2, n_keys // tk)),
        ],
        compiler_params=pltpu.CompilerParams(vmem_limit_bytes=48 * 1024 * 1024),
        name="attention_stats",
    )(slots, tiles, order, kpos, qpos, kv_all, *row_parts)


def run_keys(dims, slots, tiles, stat, stat_all, q, d, kvs, probs):
    heads, span, hd, chunks, kc, tk, _ = dims
    rows, n_keys = 2 * heads * span, chunks * kc
    smem = pl.BlockSpec(memory_space=pltpu.SMEM)
    vmem = pl.BlockSpec(memory_space=pltpu.VMEM)
    hbm = pl.BlockSpec(memory_space=pltpu.HBM)
    return pl.pallas_call(
        functools.partial(key_kernel, dims),
        out_shape=(
            jax.ShapeDtypeStruct((2, n_keys, rows // 2), BF16),
            jax.ShapeDtypeStruct((1, rows), F32),
            jax.ShapeDtypeStruct((chunks, kc, 2 * hd), BF16),
        ),
        in_specs=[smem] * 2 + [vmem] * 5 + [hbm],
        out_specs=(hbm, vmem, vmem),
        scratch_shapes=[
            pltpu.VMEM((n_keys, 2 * hd), F32),
            pltpu.VMEM((1, rows), F32),
            pltpu.VMEM((2, n_keys, rows // 2), BF16),
            pltpu.VMEM((2, n_keys, rows // 2), BF16),
            pltpu.SemaphoreType.DMA((1, 2, n_keys // tk)),
            pltpu.SemaphoreType.DMA((1, 2, n_keys // tk)),
        ],
        compiler_params=pltpu.CompilerParams(vmem_limit_bytes=48 * 1024 * 1024),
        cost_estimate=pl.CostEstimate(
            flops=3 * n_keys * rows * hd, bytes_accessed=8 * n_keys * rows, transcendentals=0
        ),
        name="attention_keys",
    )(slots, tiles, stat, stat_all, q, d, kvs, probs)


def run_rows(dims, tiles, targets, weights, kvs, probs, grads):
    heads, span, hd, chunks, kc, tk, _ = dims
    rows, n_keys = 2 * heads * span, chunks * kc
    smem = pl.BlockSpec(memory_space=pltpu.SMEM)
    vmem = pl.BlockSpec(memory_space=pltpu.VMEM)
    hbm = pl.BlockSpec(memory_space=pltpu.HBM)
    return pl.pallas_call(
        functools.partial(row_kernel, dims),
        out_shape=(jax.ShapeDtypeStruct((kc, 2 * heads * hd), BF16),) * heads,
        in_specs=[smem] * 2 + [vmem] * 2 + [hbm] * 2,
        out_specs=(vmem,) * heads,
        scratch_shapes=[
            pltpu.VMEM((hd, rows), F32),
            pltpu.VMEM((hd, rows), F32),
            pltpu.VMEM((2 * hd, n_keys), BF16),
            pltpu.VMEM((rows, hd), F32),
            pltpu.VMEM((2, n_keys, rows // 2), BF16),
            pltpu.VMEM((2, n_keys, rows // 2), BF16),
            pltpu.SemaphoreType.DMA((2, 2, n_keys // tk)),
        ],
        compiler_params=pltpu.CompilerParams(vmem_limit_bytes=48 * 1024 * 1024),
        cost_estimate=pl.CostEstimate(
            flops=n_keys * rows * hd, bytes_accessed=2 * n_keys * rows, transcendentals=0
        ),
        name="attention_rows",
    )(tiles, targets, weights, kvs, probs, grads)


def exchange(x, axis):
    return lax.all_to_all(x, axis, split_axis=0, concat_axis=0, tiled=True)


def send(x, mesh_x, step, cross):
    pairs = [
        (2 * a + c, 2 * ((a + step) % mesh_x) + (c ^ cross))
        for a in range(mesh_x)
        for c in range(2)
    ]
    return lax.ppermute(x, "head", pairs)


def local(query_in, key_in, value_in, grad_out, span_of):
    hd = key_in.shape[1]
    kc = key_in.shape[0]
    heads = lax.axis_size("head")
    shards = lax.axis_size("ctx")
    local_rows = query_in.shape[0]
    span = local_rows // 2
    n_keys = shards * kc
    tk = math.gcd(n_keys, 256)
    rc = heads * span
    dims = (heads, span, hd, shards, kc, tk, rc)
    blocks = span // kc
    ctx = lax.axis_index("ctx")
    head = lax.axis_index("head")

    mesh_x = heads // 2
    at_x, core = head // 2, head % 2
    moves = [(step, cross) for step in range(mesh_x) for cross in range(2)]
    order = jnp.stack(
        [lax.rem(at_x - step + mesh_x, mesh_x) * 2 + (core ^ cross) for step, cross in moves]
    )
    targets = jnp.stack(
        [lax.rem(at_x + step, mesh_x) * 2 + (core ^ cross) for step, cross in moves]
    )

    spans = span_of.reshape(shards, 2)
    key_span = lax.dynamic_index_in_dim(spans, head // blocks, 1, keepdims=False)
    own = lax.dynamic_index_in_dim(spans, ctx, 0, keepdims=False)
    rank = jnp.sum((key_span[None, :] < key_span[:, None]).astype(jnp.int32), axis=1)
    place = jnp.arange(shards, dtype=jnp.int32)
    ordered = jnp.sum(jnp.where(rank[None, :] == place[:, None], key_span[None, :], 0), axis=1)
    kpos = (
        ordered[:, None] * span
        + (head % blocks) * kc
        + jnp.arange(kc, dtype=jnp.int32)[None, :]
    ).reshape(n_keys, 1)
    qpos = own[:, None] * span + jnp.tile(jnp.arange(span, dtype=jnp.int32), heads)[None, :]
    before = jnp.sum((key_span[None, :] < own[:, None]).astype(jnp.int32), axis=1) * kc
    seen = jnp.sum((key_span[None, :] <= own[:, None]).astype(jnp.int32), axis=1) * kc
    tiles = jnp.stack([before // tk, (seen + tk - 1) // tk], axis=1).reshape(4)

    kv = jnp.concatenate([key_in, value_in], axis=1)
    qd = jnp.concatenate([query_in, grad_out], axis=1)
    kv_all = exchange(jnp.broadcast_to(kv[None], (shards, kc, 2 * hd)), "ctx")
    row_parts = [qd] + [send(qd, mesh_x, step, cross) for step, cross in moves[1:]]

    stat, kvs, q, d, probs = run_stats(dims, rank, tiles, order, kpos, qpos, kv_all, row_parts)
    rows = 2 * heads * span
    stat_all = exchange(jnp.broadcast_to(stat[None, :2], (heads, 2, rows)), "head")
    grads, weights, key_parts = run_keys(dims, rank, tiles, stat, stat_all, q, d, kvs, probs)
    key_parts = exchange(key_parts, "ctx")
    row_parts = run_rows(dims, tiles, targets, weights, kvs, probs, grads)
    row_sum = row_parts[0].astype(F32)
    for (step, cross), part in zip(moves[1:], row_parts[1:]):
        row_sum = row_sum + send(part, mesh_x, step, cross).astype(F32)
    row_sum = row_sum.astype(BF16)
    key_sum = jnp.sum(key_parts.astype(F32), axis=0).astype(BF16)
    width = heads * hd
    return (row_sum[:, :width], row_sum[:, width:], key_sum[:, :hd], key_sum[:, hd:])


def solution(mesh):
    return jax.shard_map(
        local,
        mesh=mesh,
        in_specs=(
            P("ctx", "head"),
            P(("ctx", "head"), None),
            P(("ctx", "head"), None),
            P("ctx", "head"),
            P(),
        ),
        out_specs=(P(("ctx", "head"), None),) * 4,
        check_vma=False,
    )
```

time: 109 us -> 114 us (1.046)
  the two profiles are of different devices: /device:TPU:2 before, /device:TPU:1 now
where the time goes in v4:
time: 114 us; the launch traced here: 113 us
  starting transfers between devices  73.5 us (64%)
  Pallas kernels  17.2 us (15%)
  blocking collectives  7.74 us (7%)
  waiting for transfers between devices  6.39 us (6%)
  local copies, waits for them, and re-layouts  5.5 us (5%)
  other arithmetic  1.61 us (1%)
    ppermute x14, starting transfers between devices, send(): return lax.ppermute(x, 'head', pairs)  44.4 us
    all_to_all x2, starting transfers between devices, exchange(): return lax.all_to_all(x, axis, split_axis=0, concat_axis=0, tiled=True)  29.1 us
    all_to_all x1, blocking collectives, exchange(): return lax.all_to_all(x, axis, split_axis=0, concat_axis=0, tiled=True)  7.74 us
    pallas_call x1, Pallas kernels, run_keys(): pl.pallas_call(functools.partial(key_kernel, dims), out_shape=(jax.ShapeD...  7.05 us
    ppermute x14, waiting for transfers between devices, send(): return lax.ppermute(x, 'head', pairs)  6.38 us
    pallas_call x1, Pallas kernels, run_stats(): pl.pallas_call(functools.partial(stats_kernel, dims), out_shape=(jax.Shap...  5.79 us
    pallas_call x1, Pallas kernels, run_rows(): pl.pallas_call(functools.partial(row_kernel, dims), out_shape=(jax.ShapeD...  4.37 us
  transfers between devices with their start and end apart: 16, of which 2 were waited for; matrix products, arithmetic and copies ran while one was open for 4% of the time, Pallas kernels for 4%

profile of v4, /device:TPU:1, one launch (start us, length us, event | category | flops | bytes accessed | tf_op | source)
XLA Modules:
  0.0 113.0 jit_solution(3638615084770623476)
XLA Ops:
  1.3 0.9 broadcast_in_dim.15
  2.3 17.1 %all-to-all-start = ((bf16[64,24,256]{2,1,0:T(8,128)(2,1)}), bf16[64,24,256]{2,1,0:T(8,128)(2,1)S(1)}, u32[]{:S(2)}, u32[]{:S(2)}) async-start(bf16[64,24,256]{2,1,0:T(8,128)(2,1)} %broadcast_in_dim.15), calls=%async_computation | async-start | bytes 1572864 | tf_op jit(solution)/shard_map/all_to_all | solution.py:323
  20.2 0.8 constant_dynamic-update-slice_fusion.refs_0_
  21.1 5.2 %collective-permute-start.6 = (bf16[192,256]{1,0:T(8,128)(2,1)S(1)}, bf16[192,256]{1,0:T(8,128)(2,1)S(1)}, u32[]{:S(2)}, u32[]{:S(2)}) collective-permute-start(bf16[192,256]{1,0:T(8,128)(2,1)S(1)} %constant_dynamic-update-slice_fusion.refs_0_), channel_id=1, source_target_pairs={{0,7},{1,6},{2,1},{3,0},{4,3},{5,2},{6,5},{7,4},{8,15},{9,14},{10,... | collective-permute-start | bytes 294920 | tf_op jit(solution)/shard_map/ppermute | solution.py:332
  26.3 2.5 %collective-permute-start.5 = (bf16[192,256]{1,0:T(8,128)(2,1)S(1)}, bf16[192,256]{1,0:T(8,128)(2,1)S(1)}, u32[]{:S(2)}, u32[]{:S(2)}) collective-permute-start(bf16[192,256]{1,0:T(8,128)(2,1)S(1)} %constant_dynamic-update-slice_fusion.refs_0_), channel_id=1, source_target_pairs={{0,6},{1,7},{2,0},{3,1},{4,2},{5,3},{6,4},{7,5},{8,14},{9,15},{10,... | collective-permute-start | bytes 294920 | tf_op jit(solution)/shard_map/ppermute | solution.py:332
  28.8 2.2 %collective-permute-start.4 = (bf16[192,256]{1,0:T(8,128)(2,1)S(1)}, bf16[192,256]{1,0:T(8,128)(2,1)S(1)}, u32[]{:S(2)}, u32[]{:S(2)}) collective-permute-start(bf16[192,256]{1,0:T(8,128)(2,1)S(1)} %constant_dynamic-update-slice_fusion.refs_0_), channel_id=1, source_target_pairs={{0,5},{1,4},{2,7},{3,6},{4,1},{5,0},{6,3},{7,2},{8,13},{9,12},{10,... | collective-permute-start | bytes 294920 | tf_op jit(solution)/shard_map/ppermute | solution.py:332
  31.0 4.3 %collective-permute-start.3 = (bf16[192,256]{1,0:T(8,128)(2,1)S(1)}, bf16[192,256]{1,0:T(8,128)(2,1)S(1)}, u32[]{:S(2)}, u32[]{:S(2)}) collective-permute-start(bf16[192,256]{1,0:T(8,128)(2,1)S(1)} %constant_dynamic-update-slice_fusion.refs_0_), channel_id=1, source_target_pairs={{0,4},{1,5},{2,6},{3,7},{4,0},{5,1},{6,2},{7,3},{8,12},{9,13},{10,... | collective-permute-start | bytes 294920 | tf_op jit(solution)/shard_map/ppermute | solution.py:332
  35.3 3.6 %collective-permute-start.2 = (bf16[192,256]{1,0:T(8,128)(2,1)S(1)}, bf16[192,256]{1,0:T(8,128)(2,1)S(1)}, u32[]{:S(2)}, u32[]{:S(2)}) collective-permute-start(bf16[192,256]{1,0:T(8,128)(2,1)S(1)} %constant_dynamic-update-slice_fusion.refs_0_), channel_id=1, source_target_pairs={{0,3},{1,2},{2,5},{3,4},{4,7},{5,6},{6,1},{7,0},{8,11},{9,10},{10,... | collective-permute-start | bytes 294920 | tf_op jit(solution)/shard_map/ppermute | solution.py:332
  40.8 1.9 %collective-permute-start.1 = (bf16[192,256]{1,0:T(8,128)(2,1)S(1)}, bf16[192,256]{1,0:T(8,128)(2,1)S(1)}, u32[]{:S(2)}, u32[]{:S(2)}) collective-permute-start(bf16[192,256]{1,0:T(8,128)(2,1)S(1)} %constant_dynamic-update-slice_fusion.refs_0_), channel_id=1, source_target_pairs={{0,2},{1,3},{2,4},{3,5},{4,6},{5,7},{6,0},{7,1},{8,10},{9,11},{10,... | collective-permute-start | bytes 294920 | tf_op jit(solution)/shard_map/ppermute | solution.py:332
  42.7 2.3 %collective-permute-start = (bf16[192,256]{1,0:T(8,128)(2,1)S(1)}, bf16[192,256]{1,0:T(8,128)(2,1)S(1)}, u32[]{:S(2)}, u32[]{:S(2)}) collective-permute-start(bf16[192,256]{1,0:T(8,128)(2,1)S(1)} %constant_dynamic-update-slice_fusion.refs_0_), channel_id=1, source_target_pairs={{0,1},{1,0},{2,3},{3,2},{4,5},{5,4},{6,7},{7,6},{8,9},{9,8},{10,11... | collective-permute-start | bytes 294920 | tf_op jit(solution)/shard_map/ppermute | solution.py:332
  45.6 3.1 %collective-permute-done.1.refs_2_ = bf16[192,256]{1,0:T(8,128)(2,1)S(1)} collective-permute-done((bf16[192,256]{1,0:T(8,128)(2,1)S(1)}, bf16[192,256]{1,0:T(8,128)(2,1)S(1)}, u32[]{:S(2)}, u32[]{:S(2)}) %collective-permute-start.1) | collective-permute-done | bytes 98336 | tf_op jit(solution)/shard_map/ppermute | solution.py:332
  48.7 5.8 %attention_stats.1 = (f32[3,1536]{1,0:T(4,128)S(1)}, bf16[1536,256]{1,0:T(8,128)(2,1)S(1)}, bf16[2,768,128]{2,1,0:T(8,128)(2,1)S(1)}, bf16[2,768,128]{2,1,0:T(8,128)(2,1)S(1)}, bf16[2,1536,768]{2,1,0:T(8,128)(2,1)}) custom-call(s32[64]{0:T(128)S(1)} %convert_reduce_fusion.slots_ref, s32[4]{0:T(128)S(1)} %reshape.172.tiles_ref, s32[8]{0:T(128)S(1)} %stack.59.order_ref, ...), custom_call_target="tpu_custom_call" | custom-call | tf_op jit(solution)/shard_map/attention_stats/pallas_call | solution.py:241
  54.6 7.7 %all_to_all.15.all_ref = f32[8,2,1536]{2,1,0:T(2,128)S(1)} all-to-all(f32[8,2,1536]{2,1,0:T(2,128)S(1)} %broadcast_in_dim.16), channel_id=1, replica_groups=mesh['ctx'=64,'head'=8] {'head'}, dimensions={0} | all-to-all | bytes 196608 | tf_op jit(solution)/shard_map/all_to_all | solution.py:323
  62.3 7.0 %attention_keys.1 = (bf16[2,1536,768]{2,1,0:T(8,128)(2,1)}, f32[1,1536]{1,0:T(1,128)S(1)}, bf16[64,24,256]{2,1,0:T(8,128)(2,1)}) custom-call(s32[64]{0:T(128)S(1)} %convert_reduce_fusion.slots_ref, s32[4]{0:T(128)S(1)} %reshape.172.tiles_ref, f32[3,1536]{1,0:T(4,128)S(1)} %get-tuple-element.20.stat_ref, f32[8,2,1536]{2,1,0:T(2,128)S(1)} %all_to_all.15.all_ref, ...), custom_call_target="tpu_custom_call" | custom-call | flops 905969664 | bytes 18874368 | tf_op jit(solution)/shard_map/attention_keys/pallas_call | solution.py:269
  69.4 12.0 %all-to-all-start.2 = ((bf16[64,24,256]{2,1,0:T(8,128)(2,1)}), bf16[64,24,256]{2,1,0:T(8,128)(2,1)S(1)}, u32[]{:S(2)}, u32[]{:S(2)}) async-start(bf16[64,24,256]{2,1,0:T(8,128)(2,1)} %get-tuple-element.35), calls=%async_computation.2 | async-start | bytes 1572864 | tf_op jit(solution)/shard_map/all_to_all | solution.py:323
  81.4 4.4 %attention_rows.1 = (bf16[24,2048]{1,0:T(8,128)(2,1)S(1)}, bf16[24,2048]{1,0:T(8,128)(2,1)S(1)}, bf16[24,2048]{1,0:T(8,128)(2,1)S(1)}, bf16[24,2048]{1,0:T(8,128...) custom-call(s32[4]{0:T(128)S(1)} %reshape.172.tiles_ref, ...), custom_call_target="tpu_custom_call" | custom-call | flops 301989888 | bytes 4718592 | tf_op jit(solution)/shard_map/attention_rows/pallas_call | solution.py:300
  85.8 3.0 %collective-permute-start.7 = (bf16[24,2048]{1,0:T(8,128)(2,1)S(1)}, bf16[24,2048]{1,0:T(8,128)(2,1)S(1)}, u32[]{:S(2)}, u32[]{:S(2)}) collective-permute-start(bf16[24,2048]{1,0:T(8,128)(2,1)S(1)} %get-tuple-element.28), channel_id=1, source_target_pairs={{0,1},{1,0},{2,3},{3,2},{4,5},{5,4},{6,7},{7,6},{8,9},{9,8},{10,11... | collective-permute-start | bytes 294920 | tf_op jit(solution)/shard_map/ppermute | solution.py:332
  88.8 2.2 %collective-permute-start.8 = (bf16[24,2048]{1,0:T(8,128)(2,1)S(1)}, bf16[24,2048]{1,0:T(8,128)(2,1)S(1)}, u32[]{:S(2)}, u32[]{:S(2)}) collective-permute-start(bf16[24,2048]{1,0:T(8,128)(2,1)S(1)} %get-tuple-element.29), channel_id=1, source_target_pairs={{0,2},{1,3},{2,4},{3,5},{4,6},{5,7},{6,0},{7,1},{8,10},{9,11},{10,... | collective-permute-start | bytes 294920 | tf_op jit(solution)/shard_map/ppermute | solution.py:332
  91.0 2.4 %collective-permute-start.9 = (bf16[24,2048]{1,0:T(8,128)(2,1)S(1)}, bf16[24,2048]{1,0:T(8,128)(2,1)S(1)}, u32[]{:S(2)}, u32[]{:S(2)}) collective-permute-start(bf16[24,2048]{1,0:T(8,128)(2,1)S(1)} %get-tuple-element.30), channel_id=1, source_target_pairs={{0,3},{1,2},{2,5},{3,4},{4,7},{5,6},{6,1},{7,0},{8,11},{9,10},{10,... | collective-permute-start | bytes 294920 | tf_op jit(solution)/shard_map/ppermute | solution.py:332
  93.4 5.2 %collective-permute-start.10 = (bf16[24,2048]{1,0:T(8,128)(2,1)S(1)}, bf16[24,2048]{1,0:T(8,128)(2,1)S(1)}, u32[]{:S(2)}, u32[]{:S(2)}) collective-permute-start(bf16[24,2048]{1,0:T(8,128)(2,1)S(1)} %get-tuple-element.31), channel_id=1, source_target_pairs={{0,4},{1,5},{2,6},{3,7},{4,0},{5,1},{6,2},{7,3},{8,12},{9,13},{10,... | collective-permute-start | bytes 294920 | tf_op jit(solution)/shard_map/ppermute | solution.py:332
  98.6 2.0 %collective-permute-start.11 = (bf16[24,2048]{1,0:T(8,128)(2,1)S(1)}, bf16[24,2048]{1,0:T(8,128)(2,1)S(1)}, u32[]{:S(2)}, u32[]{:S(2)}) collective-permute-start(bf16[24,2048]{1,0:T(8,128)(2,1)S(1)} %get-tuple-element.32), channel_id=1, source_target_pairs={{0,5},{1,4},{2,7},{3,6},{4,1},{5,0},{6,3},{7,2},{8,13},{9,12},{10,... | collective-permute-start | bytes 294920 | tf_op jit(solution)/shard_map/ppermute | solution.py:332
  100.7 4.3 %collective-permute-start.12 = (bf16[24,2048]{1,0:T(8,128)(2,1)S(1)}, bf16[24,2048]{1,0:T(8,128)(2,1)S(1)}, u32[]{:S(2)}, u32[]{:S(2)}) collective-permute-start(bf16[24,2048]{1,0:T(8,128)(2,1)S(1)} %get-tuple-element.33), channel_id=1, source_target_pairs={{0,6},{1,7},{2,0},{3,1},{4,2},{5,3},{6,4},{7,5},{8,14},{9,15},{10,... | collective-permute-start | bytes 294920 | tf_op jit(solution)/shard_map/ppermute | solution.py:332
  104.9 3.3 %collective-permute-start.13 = (bf16[24,2048]{1,0:T(8,128)(2,1)S(1)}, bf16[24,2048]{1,0:T(8,128)(2,1)S(1)}, u32[]{:S(2)}, u32[]{:S(2)}) collective-permute-start(bf16[24,2048]{1,0:T(8,128)(2,1)S(1)} %get-tuple-element.34), channel_id=1, source_target_pairs={{0,7},{1,6},{2,1},{3,0},{4,3},{5,2},{6,5},{7,4},{8,15},{9,14},{10,... | collective-permute-start | bytes 294920 | tf_op jit(solution)/shard_map/ppermute | solution.py:332
  108.2 3.3 %collective-permute-done.13 = bf16[24,2048]{1,0:T(8,128)(2,1)S(1)} collective-permute-done((bf16[24,2048]{1,0:T(8,128)(2,1)S(1)}, bf16[24,2048]{1,0:T(8,128)(2,1)S(1)}, u32[]{:S(2)}, u32[]{:S(2)}) %collective-permute-start.13) | collective-permute-done | bytes 98336 | tf_op jit(solution)/shard_map/ppermute | solution.py:332
  (40 shorter events, 5.4 us)
Async XLA Ops:
  2.3 46.4 %all-to-all-start = ((bf16[64,24,256]{2,1,0:T(8,128)(2,1)}), bf16[64,24,256]{2,1,0:T(8,128)(2,1)S(1)}, u32[]{:S(2)}, u32[]{:S(2)}) async-start(bf16[64,24,256]{2,1,0:T(8,128)(2,1)} %broadcast_in_dim.15), calls=%async_computation | async-start | bytes 1572864 | tf_op jit(solution)/shard_map/all_to_all | solution.py:323
  21.1 19.7 %collective-permute-start.6 = (bf16[192,256]{1,0:T(8,128)(2,1)S(1)}, bf16[192,256]{1,0:T(8,128)(2,1)S(1)}, u32[]{:S(2)}, u32[]{:S(2)}) collective-permute-start(bf16[192,256]{1,0:T(8,128)(2,1)S(1)} %constant_dynamic-update-slice_fusion.refs_0_), channel_id=1, source_target_pairs={{0,7},{1,6},{2,1},{3,0},{4,3},{5,2},{6,5},{7,4},{8,15},{9,14},{10,... | collective-permute-start | bytes 294920 | tf_op jit(solution)/shard_map/ppermute | solution.py:332
  26.3 16.4 %collective-permute-start.5 = (bf16[192,256]{1,0:T(8,128)(2,1)S(1)}, bf16[192,256]{1,0:T(8,128)(2,1)S(1)}, u32[]{:S(2)}, u32[]{:S(2)}) collective-permute-start(bf16[192,256]{1,0:T(8,128)(2,1)S(1)} %constant_dynamic-update-slice_fusion.refs_0_), channel_id=1, source_target_pairs={{0,6},{1,7},{2,0},{3,1},{4,2},{5,3},{6,4},{7,5},{8,14},{9,15},{10,... | collective-permute-start | bytes 294920 | tf_op jit(solution)/shard_map/ppermute | solution.py:332
  28.8 16.9 %collective-permute-start.4 = (bf16[192,256]{1,0:T(8,128)(2,1)S(1)}, bf16[192,256]{1,0:T(8,128)(2,1)S(1)}, u32[]{:S(2)}, u32[]{:S(2)}) collective-permute-start(bf16[192,256]{1,0:T(8,128)(2,1)S(1)} %constant_dynamic-update-slice_fusion.refs_0_), channel_id=1, source_target_pairs={{0,5},{1,4},{2,7},{3,6},{4,1},{5,0},{6,3},{7,2},{8,13},{9,12},{10,... | collective-permute-start | bytes 294920 | tf_op jit(solution)/shard_map/ppermute | solution.py:332
  31.0 14.7 %collective-permute-start.3 = (bf16[192,256]{1,0:T(8,128)(2,1)S(1)}, bf16[192,256]{1,0:T(8,128)(2,1)S(1)}, u32[]{:S(2)}, u32[]{:S(2)}) collective-permute-start(bf16[192,256]{1,0:T(8,128)(2,1)S(1)} %constant_dynamic-update-slice_fusion.refs_0_), channel_id=1, source_target_pairs={{0,4},{1,5},{2,6},{3,7},{4,0},{5,1},{6,2},{7,3},{8,12},{9,13},{10,... | collective-permute-start | bytes 294920 | tf_op jit(solution)/shard_map/ppermute | solution.py:332
  35.3 10.3 %collective-permute-start.2 = (bf16[192,256]{1,0:T(8,128)(2,1)S(1)}, bf16[192,256]{1,0:T(8,128)(2,1)S(1)}, u32[]{:S(2)}, u32[]{:S(2)}) collective-permute-start(bf16[192,256]{1,0:T(8,128)(2,1)S(1)} %constant_dynamic-update-slice_fusion.refs_0_), channel_id=1, source_target_pairs={{0,3},{1,2},{2,5},{3,4},{4,7},{5,6},{6,1},{7,0},{8,11},{9,10},{10,... | collective-permute-start | bytes 294920 | tf_op jit(solution)/shard_map/ppermute | solution.py:332
  40.8 7.9 %collective-permute-start.1 = (bf16[192,256]{1,0:T(8,128)(2,1)S(1)}, bf16[192,256]{1,0:T(8,128)(2,1)S(1)}, u32[]{:S(2)}, u32[]{:S(2)}) collective-permute-start(bf16[192,256]{1,0:T(8,128)(2,1)S(1)} %constant_dynamic-update-slice_fusion.refs_0_), channel_id=1, source_target_pairs={{0,2},{1,3},{2,4},{3,5},{4,6},{5,7},{6,0},{7,1},{8,10},{9,11},{10,... | collective-permute-start | bytes 294920 | tf_op jit(solution)/shard_map/ppermute | solution.py:332
  42.7 6.0 %collective-permute-start = (bf16[192,256]{1,0:T(8,128)(2,1)S(1)}, bf16[192,256]{1,0:T(8,128)(2,1)S(1)}, u32[]{:S(2)}, u32[]{:S(2)}) collective-permute-start(bf16[192,256]{1,0:T(8,128)(2,1)S(1)} %constant_dynamic-update-slice_fusion.refs_0_), channel_id=1, source_target_pairs={{0,1},{1,0},{2,3},{3,2},{4,5},{5,4},{6,7},{7,6},{8,9},{9,8},{10,11... | collective-permute-start | bytes 294920 | tf_op jit(solution)/shard_map/ppermute | solution.py:332
  69.4 42.9 %all-to-all-start.2 = ((bf16[64,24,256]{2,1,0:T(8,128)(2,1)}), bf16[64,24,256]{2,1,0:T(8,128)(2,1)S(1)}, u32[]{:S(2)}, u32[]{:S(2)}) async-start(bf16[64,24,256]{2,1,0:T(8,128)(2,1)} %get-tuple-element.35), calls=%async_computation.2 | async-start | bytes 1572864 | tf_op jit(solution)/shard_map/all_to_all | solution.py:323
  85.8 14.8 %collective-permute-start.7 = (bf16[24,2048]{1,0:T(8,128)(2,1)S(1)}, bf16[24,2048]{1,0:T(8,128)(2,1)S(1)}, u32[]{:S(2)}, u32[]{:S(2)}) collective-permute-start(bf16[24,2048]{1,0:T(8,128)(2,1)S(1)} %get-tuple-element.28), channel_id=1, source_target_pairs={{0,1},{1,0},{2,3},{3,2},{4,5},{5,4},{6,7},{7,6},{8,9},{9,8},{10,11... | collective-permute-start | bytes 294920 | tf_op jit(solution)/shard_map/ppermute | solution.py:332
  88.8 16.1 %collective-permute-start.8 = (bf16[24,2048]{1,0:T(8,128)(2,1)S(1)}, bf16[24,2048]{1,0:T(8,128)(2,1)S(1)}, u32[]{:S(2)}, u32[]{:S(2)}) collective-permute-start(bf16[24,2048]{1,0:T(8,128)(2,1)S(1)} %get-tuple-element.29), channel_id=1, source_target_pairs={{0,2},{1,3},{2,4},{3,5},{4,6},{5,7},{6,0},{7,1},{8,10},{9,11},{10,... | collective-permute-start | bytes 294920 | tf_op jit(solution)/shard_map/ppermute | solution.py:332
  91.0 17.2 %collective-permute-start.9 = (bf16[24,2048]{1,0:T(8,128)(2,1)S(1)}, bf16[24,2048]{1,0:T(8,128)(2,1)S(1)}, u32[]{:S(2)}, u32[]{:S(2)}) collective-permute-start(bf16[24,2048]{1,0:T(8,128)(2,1)S(1)} %get-tuple-element.30), channel_id=1, source_target_pairs={{0,3},{1,2},{2,5},{3,4},{4,7},{5,6},{6,1},{7,0},{8,11},{9,10},{10,... | collective-permute-start | bytes 294920 | tf_op jit(solution)/shard_map/ppermute | solution.py:332
  93.4 14.8 %collective-permute-start.10 = (bf16[24,2048]{1,0:T(8,128)(2,1)S(1)}, bf16[24,2048]{1,0:T(8,128)(2,1)S(1)}, u32[]{:S(2)}, u32[]{:S(2)}) collective-permute-start(bf16[24,2048]{1,0:T(8,128)(2,1)S(1)} %get-tuple-element.31), channel_id=1, source_target_pairs={{0,4},{1,5},{2,6},{3,7},{4,0},{5,1},{6,2},{7,3},{8,12},{9,13},{10,... | collective-permute-start | bytes 294920 | tf_op jit(solution)/shard_map/ppermute | solution.py:332
  98.6 9.6 %collective-permute-start.11 = (bf16[24,2048]{1,0:T(8,128)(2,1)S(1)}, bf16[24,2048]{1,0:T(8,128)(2,1)S(1)}, u32[]{:S(2)}, u32[]{:S(2)}) collective-permute-start(bf16[24,2048]{1,0:T(8,128)(2,1)S(1)} %get-tuple-element.32), channel_id=1, source_target_pairs={{0,5},{1,4},{2,7},{3,6},{4,1},{5,0},{6,3},{7,2},{8,13},{9,12},{10,... | collective-permute-start | bytes 294920 | tf_op jit(solution)/shard_map/ppermute | solution.py:332
  100.7 7.6 %collective-permute-start.12 = (bf16[24,2048]{1,0:T(8,128)(2,1)S(1)}, bf16[24,2048]{1,0:T(8,128)(2,1)S(1)}, u32[]{:S(2)}, u32[]{:S(2)}) collective-permute-start(bf16[24,2048]{1,0:T(8,128)(2,1)S(1)} %get-tuple-element.33), channel_id=1, source_target_pairs={{0,6},{1,7},{2,0},{3,1},{4,2},{5,3},{6,4},{7,5},{8,14},{9,15},{10,... | collective-permute-start | bytes 294920 | tf_op jit(solution)/shard_map/ppermute | solution.py:332
  104.9 6.6 %collective-permute-start.13 = (bf16[24,2048]{1,0:T(8,128)(2,1)S(1)}, bf16[24,2048]{1,0:T(8,128)(2,1)S(1)}, u32[]{:S(2)}, u32[]{:S(2)}) collective-permute-start(bf16[24,2048]{1,0:T(8,128)(2,1)S(1)} %get-tuple-element.34), channel_id=1, source_target_pairs={{0,7},{1,6},{2,1},{3,0},{4,3},{5,2},{6,5},{7,4},{8,15},{9,14},{10,... | collective-permute-start | bytes 294920 | tf_op jit(solution)/shard_map/ppermute | solution.py:332

commit v5 on v3

--- a/solution.py
+++ b/solution.py
@@ -166,6 +166,34 @@
                 out_ref[number % per_core, :, at : at + hd] = flat_s[
                     pl.ds(first, kc), :
                 ].astype(BF16)
+
+
+def pack_kernel(hd, q_ref, d_ref, k_ref, v_ref, qd_ref, kv_ref, sems):
+    pairs = ((q_ref, qd_ref.at[0, :, :hd]), (d_ref, qd_ref.at[0, :, hd:]))
+    copies = [pltpu.make_async_copy(a, b, sems.at[n]) for n, (a, b) in enumerate(pairs)]
+    for copy in copies:
+        copy.start()
+    shape = kv_ref.shape[:2] + (hd,)
+    kv_ref[:, :, :hd] = jnp.broadcast_to(k_ref[...][None], shape)
+    kv_ref[:, :, hd:] = jnp.broadcast_to(v_ref[...][None], shape)
+    for copy in copies:
+        copy.wait()
+
+
+def run_pack(shards, query, dout, key, value):
+    (rows, hd), kc = query.shape, key.shape[0]
+    return pl.pallas_call(
+        functools.partial(pack_kernel, hd),
+        out_shape=(
+            jax.ShapeDtypeStruct((1, rows, 2 * hd), BF16),
+            jax.ShapeDtypeStruct((shards, kc, 2 * hd), BF16),
+        ),
+        in_specs=[pl.BlockSpec(memory_space=pltpu.HBM)] * 2
+        + [pl.BlockSpec(memory_space=pltpu.VMEM)] * 2,
+        scratch_shapes=[pltpu.SemaphoreType.DMA((2,))],
+        compiler_params=pltpu.CompilerParams(vmem_limit_bytes=63 * 1024 * 1024),
+        name="attention_pack",
+    )(query, dout, key, value)
 
 
 def run_stats(dims, slots, tiles, order, kpos, qpos, near, far, kv_all):
@@ -221,21 +249,8 @@
     )(slots, tiles, order, stat, stat_all, q, d, kvs, probs)
 
 
-def grouped(x, groups):
-    return lax.all_to_all(
-        x, ("ctx", "head"), split_axis=0, concat_axis=0, axis_index_groups=groups, tiled=True
-    )
-
-
-def line_groups(side, heads):
-    first, second = [], []
-    for head in range(heads):
-        for fixed in range(side):
-            along_z = [(fixed * side + moving) * heads + head for moving in range(side)]
-            along_y = [(moving * side + fixed) * heads + head for moving in range(side)]
-            first.append(along_y if head % 2 else along_z)
-            second.append(along_z if head % 2 else along_y)
-    return first, second
+def exchange(x, axis):
+    return lax.all_to_all(x, axis, split_axis=0, concat_axis=0, tiled=True)
 
 
 def flip_x(x, mesh_x, mask):
@@ -271,16 +286,12 @@
         offsets = offsets + [mask ^ offset for offset in offsets]
     origin = jnp.bitwise_xor(at_x, jnp.array(offsets, jnp.int32)) * 2
     order = jnp.concatenate([origin + core, origin + 1 - core]).astype(jnp.int32)
-    side = math.isqrt(shards)
-    first, second = line_groups(side, heads)
 
     spans = span_of.reshape(shards, 2)
     key_span = lax.dynamic_index_in_dim(spans, head // blocks, 1, keepdims=False)
     own = lax.dynamic_index_in_dim(spans, ctx, 0, keepdims=False)
     rank = jnp.sum((key_span[None, :] < key_span[:, None]).astype(jnp.int32), axis=1)
     place = jnp.arange(shards, dtype=jnp.int32)
-    crossed = rank.reshape(side, side).T.reshape(shards)
-    slots = jnp.where(core == 0, rank, crossed)
     ordered = jnp.sum(jnp.where(rank[None, :] == place[:, None], key_span[None, :], 0), axis=1)
     kpos = (
         ordered[:, None] * span
@@ -292,39 +303,27 @@
     seen = jnp.sum((key_span[None, :] <= own[:, None]).astype(jnp.int32), axis=1) * kc
     tiles = jnp.stack([before // tk, (seen + tk - 1) // tk], axis=1).reshape(4)
 
-    kv = jnp.concatenate([key_in, value_in], axis=1)
-    qd = jnp.concatenate([query_in, grad_out], axis=1)
-    near = qd[None]
-    near = jnp.concatenate([near, flip_x(near, mesh_x, masks[0])])
-    kv_line = grouped(jnp.broadcast_to(kv[None], (side, kc, 2 * hd)), first)
-    kv_line, near = lax.optimization_barrier((kv_line, near))
-    kv_all = grouped(jnp.broadcast_to(kv_line[None], (side, side, kc, 2 * hd)), second)
-    kv_all = kv_all.reshape(shards, kc, 2 * hd)
-    for mask in masks[1:]:
+    near, kv_all = run_pack(shards, query_in, grad_out, key_in, value_in)
+    kv_all = exchange(kv_all, "ctx")
+    for mask in masks:
         near = jnp.concatenate([near, flip_x(near, mesh_x, mask)])
     far = swap_cores(near, mesh_x)
 
-    stat, kvs, q, d, probs = run_stats(dims, slots, tiles, order, kpos, qpos, near, far, kv_all)
+    stat, kvs, q, d, probs = run_stats(dims, rank, tiles, order, kpos, qpos, near, far, kv_all)
     rows = 2 * heads * span
-    stat_all = lax.all_to_all(
-        jnp.broadcast_to(stat[None, :2], (heads, 2, rows)), "head", 0, 0, tiled=True
+    stat_all = exchange(jnp.broadcast_to(stat[None, :2], (heads, 2, rows)), "head")
+    keep, send, key_parts = run_grads(
+        dims, rank, tiles, order, stat, stat_all, q, d, kvs, probs
     )
-    keep, send, key_parts = run_grads(
-        dims, slots, tiles, order, stat, stat_all, q, d, kvs, probs
-    )
-
-    key_line = grouped(key_parts.reshape(side, side, kc, 2 * hd), second)
-    key_line = jnp.sum(key_line.astype(F32), axis=0).astype(BF16)
+    key_parts = exchange(key_parts, "ctx")
 
     row_sum = keep.astype(F32) + swap_cores(send, mesh_x).astype(F32)
     for mask in reversed(masks):
-        if mask == masks[0]:
-            key_line, row_sum = lax.optimization_barrier((key_line, row_sum))
-            key_sum = jnp.sum(grouped(key_line, first).astype(F32), axis=0).astype(BF16)
         half = row_sum.shape[0] // 2
         moved = flip_x(row_sum[half:].astype(BF16), mesh_x, mask)
         row_sum = row_sum[:half] + moved.astype(F32)
     row_sum = row_sum[0].astype(BF16)
+    key_sum = jnp.sum(key_parts.astype(F32), axis=0).astype(BF16)
     width = heads * hd
     return (row_sum[:, :width], row_sum[:, width:], key_sum[:, :hd], key_sum[:, hd:])
 

time: 109 us -> 103 us (0.945)
  the two profiles are of different devices: /device:TPU:2 before, /device:TPU:16 now
where the time goes in v5:
time: 103 us; the launch traced here: 102 us
  starting transfers between devices  39.6 us (38%)
  waiting for transfers between devices  30.3 us (29%)
  Pallas kernels  16.7 us (16%)
  blocking collectives  8.37 us (8%)
  local copies, waits for them, and re-layouts  3.72 us (4%)
  other arithmetic  2.6 us (3%)
    all_to_all x2, starting transfers between devices, exchange(): return lax.all_to_all(x, axis, split_axis=0, concat_axis=0, tiled=True)  23.4 us
    ppermute x4, waiting for transfers between devices, flip_x(): return lax.ppermute(x, 'head', pairs)  16.1 us
    all_to_all x2, waiting for transfers between devices, exchange(): return lax.all_to_all(x, axis, split_axis=0, concat_axis=0, tiled=True)  13.2 us
    ppermute x4, starting transfers between devices, flip_x(): return lax.ppermute(x, 'head', pairs)  12.4 us
    all_to_all x1, blocking collectives, exchange(): return lax.all_to_all(x, axis, split_axis=0, concat_axis=0, tiled=True)  8.37 us
    pallas_call x1, Pallas kernels, run_grads(): pl.pallas_call(functools.partial(grad_kernel, dims), out_shape=(jax.Shape...  8.24 us
    pallas_call x1, Pallas kernels, run_stats(): pl.pallas_call(functools.partial(stats_kernel, dims), out_shape=(jax.Shap...  6 us
    ppermute x2, starting transfers between devices, swap_cores(): return lax.ppermute(x, 'head', pairs)  3.83 us
  transfers between devices with their start and end apart: 8, of which 7 were waited for; matrix products, arithmetic and copies ran while one was open for 5% of the time, Pallas kernels for 0%

profile of v5, /device:TPU:16, one launch (start us, length us, event | category | flops | bytes accessed | tf_op | source)
XLA Modules:
  0.0 102.3 jit_solution(2657521029207346520)
XLA Ops:
  0.6 2.5 %attention_pack.1 = (bf16[1,192,256]{2,1,0:T(8,128)(2,1)}, bf16[64,24,256]{2,1,0:T(8,128)(2,1)}) custom-call(bf16[192,128]{1,0:T(8,128)(2,1)} %q_ref.1, bf16[192,128]{1,0:T(8,128)(2,1)} %d_ref.1, bf16[24,128]{1,0:T(8,128)(2,1)} %k_ref.1, bf16[24,128]{1,0:T(8,128)(2,1)} %v_ref.1), custom_call_target="tpu_custom_call" | custom-call | tf_op jit(solution)/shard_map/attention_pack/pallas_call | solution.py:185
  3.1 16.5 %all-to-all-start = ((bf16[64,24,256]{2,1,0:T(8,128)(2,1)}), bf16[64,24,256]{2,1,0:T(8,128)(2,1)S(1)}, u32[]{:S(2)}, u32[]{:S(2)}) async-start(bf16[64,24,256]{2,1,0:T(8,128)(2,1)} %get-tuple-element.15), calls=%async_computation | async-start | bytes 1572864 | tf_op jit(solution)/shard_map/all_to_all | solution.py:253
  19.6 3.4 %collective-permute-start = (bf16[1,192,256]{2,1,0:T(8,128)(2,1)}, bf16[1,192,256]{2,1,0:T(8,128)(2,1)S(1)}, u32[]{:S(2)}, u32[]{:S(2)}) collective-permute-start(bf16[1,192,256]{2,1,0:T(8,128)(2,1)} %get-tuple-element.14), channel_id=1, source_target_pairs={{0,2},{1,3},{2,0},{3,1},{4,6},{5,7},{6,4},{7,5},{8,10},{9,11},{10,... | collective-permute-start | bytes 294920 | tf_op jit(solution)/shard_map/ppermute | solution.py:258
  23.0 0.8 reshape.171
  24.6 0.7 fusion.4
  25.4 0.9 collective-permute-done
  26.3 0.9 pad_maximum_fusion
  27.2 4.7 %collective-permute-start.1 = (bf16[2,192,256]{2,1,0:T(8,128)(2,1)S(1)}, bf16[2,192,256]{2,1,0:T(8,128)(2,1)S(1)}, u32[]{:S(2)}, u32[]{:S(2)}) collective-permute-start(bf16[2,192,256]{2,1,0:T(8,128)(2,1)S(1)} %pad_maximum_fusion), channel_id=1, source_target_pairs={{0,6},{1,7},{2,4},{3,5},{4,2},{5,3},{6,0},{7,1},{8,14},{9,15},{10,... | collective-permute-start | bytes 589832 | tf_op jit(solution)/shard_map/ppermute | solution.py:258
  31.9 0.9 constant_dynamic-update-slice_fusion.2
  32.8 3.2 %collective-permute-done.1 = bf16[2,192,256]{2,1,0:T(8,128)(2,1)S(1)} collective-permute-done((bf16[2,192,256]{2,1,0:T(8,128)(2,1)S(1)}, bf16[2,192,256]{2,1,0:T(8,128)(2,1)S(1)}, u32[]{:S(2)}, u32[]{:S(2)}) %collective-permute-start.1) | collective-permute-done | bytes 196640 | tf_op jit(solution)/shard_map/ppermute | solution.py:258
  36.0 1.9 %collective-permute-start.2 = (bf16[4,192,256]{2,1,0:T(8,128)(2,1)S(1)}, bf16[4,192,256]{2,1,0:T(8,128)(2,1)S(1)}, u32[]{:S(2)}, u32[]{:S(2)}) collective-permute-start(bf16[4,192,256]{2,1,0:T(8,128)(2,1)S(1)} %constant_dynamic-update-slice_fusion.near_ref), channel_id=1, source_target_pairs={{0,1},{1,0},{2,3},{3,2},{4,5},{5,4},{6,7},{7,6},{8,9},{9,8},{10,11... | collective-permute-start | bytes 1179656 | tf_op jit(solution)/shard_map/ppermute | solution.py:263
  38.6 1.1 %collective-permute-done.2.far_ref = bf16[4,192,256]{2,1,0:T(8,128)(2,1)S(1)} collective-permute-done((bf16[4,192,256]{2,1,0:T(8,128)(2,1)S(1)}, bf16[4,192,256]{2,1,0:T(8,128)(2,1)S(1)}, u32[]{:S(2)}, u32[]{:S(2)}) %collective-permute-start.2) | collective-permute-done | bytes 393248 | tf_op jit(solution)/shard_map/ppermute | solution.py:263
  39.6 4.8 %all-to-all-done.kv_ref = bf16[64,24,256]{2,1,0:T(8,128)(2,1)S(1)} async-done(((bf16[64,24,256]{2,1,0:T(8,128)(2,1)}), bf16[64,24,256]{2,1,0:T(8,128)(2,1)S(1)}, u32[]{:S(2)}, u32[]{:S(2)}) %all-to-all-start) | async-done | bytes 786464 | tf_op jit(solution)/shard_map/all_to_all | solution.py:253
  44.5 6.0 %attention_stats.1 = (f32[3,1536]{1,0:T(4,128)S(1)}, bf16[1536,256]{1,0:T(8,128)(2,1)S(1)}, bf16[2,768,128]{2,1,0:T(8,128)(2,1)S(1)}, bf16[2,768,128]{2,1,0:T(8,128)(2,1)S(1)}, bf16[1536,1536]{1,0:T(8,128)(2,1)S(1)}) custom-call(s32[64]{0:T(128)S(1)} %convert_reduce_fusion.slots_ref, s32[4]{0:T(128)S(1)} %reshape.172.tiles_ref, ...), custom_call_target="tpu_custom_call" | custom-call | tf_op jit(solution)/shard_map/attention_stats/pallas_call | solution.py:204
  50.5 8.4 %all_to_all.15.all_ref = f32[8,2,1536]{2,1,0:T(2,128)S(1)} all-to-all(f32[8,2,1536]{2,1,0:T(2,128)S(1)} %broadcast_in_dim.13), channel_id=1, replica_groups=mesh['ctx'=64,'head'=8] {'head'}, dimensions={0} | all-to-all | bytes 196608 | tf_op jit(solution)/shard_map/all_to_all | solution.py:253
  58.9 8.2 %attention_grads.1 = (bf16[4,24,2048]{2,1,0:T(8,128)(2,1)S(1)}, bf16[4,24,2048]{2,1,0:T(8,128)(2,1)S(1)}, bf16[64,24,256]{2,1,0:T(8,128)(2,1)}) custom-call(s32[64]{0:T(128)S(1)} %convert_reduce_fusion.slots_ref, s32[4]{0:T(128)S(1)} %reshape.172.tiles_ref, s32[8]{0:T(128)S(1)} %pad_add_fusion.1.order_ref, f32[3,1536]{1,0:T(4,128)S(1)} %get-tuple-element.16.stat_ref, ...), custom_call_target="tpu_custom_call" | custom-call | tf_op jit(solution)/shard_map/attention_grads/pallas_call | solution.py:229
  67.1 1.9 %collective-permute-start.3 = (bf16[4,24,2048]{2,1,0:T(8,128)(2,1)S(1)}, bf16[4,24,2048]{2,1,0:T(8,128)(2,1)S(1)}, u32[]{:S(2)}, u32[]{:S(2)}) collective-permute-start(bf16[4,24,2048]{2,1,0:T(8,128)(2,1)S(1)} %get-tuple-element.22), channel_id=1, source_target_pairs={{0,1},{1,0},{2,3},{3,2},{4,5},{5,4},{6,7},{7,6},{8,9},{9,8},{10,11... | collective-permute-start | bytes 1179656 | tf_op jit(solution)/shard_map/ppermute | solution.py:263
  69.0 6.9 %all-to-all-start.2 = ((bf16[64,24,256]{2,1,0:T(8,128)(2,1)}), bf16[64,24,256]{2,1,0:T(8,128)(2,1)S(1)}, u32[]{:S(2)}, u32[]{:S(2)}) async-start(bf16[64,24,256]{2,1,0:T(8,128)(2,1)} %get-tuple-element.23), calls=%async_computation.2 | async-start | bytes 1572864 | tf_op jit(solution)/shard_map/all_to_all | solution.py:253
  76.1 2.5 %collective-permute-start.4 = (bf16[2,24,2048]{2,1,0:T(8,128)(2,1)S(1)}, bf16[2,24,2048]{2,1,0:T(8,128)(2,1)S(1)}, u32[]{:S(2)}, u32[]{:S(2)}) collective-permute-start(bf16[2,24,2048]{2,1,0:T(8,128)(2,1)S(1)} %slice.54), channel_id=1, source_target_pairs={{0,6},{1,7},{2,4},{3,5},{4,2},{5,3},{6,0},{7,1},{8,14},{9,15},{10,... | collective-permute-start | bytes 589832 | tf_op jit(solution)/shard_map/ppermute | solution.py:258
  78.5 7.4 %collective-permute-done.4 = bf16[2,24,2048]{2,1,0:T(8,128)(2,1)S(1)} collective-permute-done((bf16[2,24,2048]{2,1,0:T(8,128)(2,1)S(1)}, bf16[2,24,2048]{2,1,0:T(8,128)(2,1)S(1)}, u32[]{:S(2)}, u32[]{:S(2)}) %collective-permute-start.4) | collective-permute-done | bytes 196640 | tf_op jit(solution)/shard_map/ppermute | solution.py:258
  86.0 1.9 %collective-permute-start.5 = (bf16[1,24,2048]{2,1,0:T(8,128)(2,1)S(1)}, bf16[1,24,2048]{2,1,0:T(8,128)(2,1)S(1)}, u32[]{:S(2)}, u32[]{:S(2)}) collective-permute-start(bf16[1,24,2048]{2,1,0:T(8,128)(2,1)S(1)} %slice.55), channel_id=1, source_target_pairs={{0,2},{1,3},{2,0},{3,1},{4,6},{5,7},{6,4},{7,5},{8,10},{9,11},{10,... | collective-permute-start | bytes 294920 | tf_op jit(solution)/shard_map/ppermute | solution.py:258
  87.9 4.6 %collective-permute-done.5 = bf16[1,24,2048]{2,1,0:T(8,128)(2,1)S(1)} collective-permute-done((bf16[1,24,2048]{2,1,0:T(8,128)(2,1)S(1)}, bf16[1,24,2048]{2,1,0:T(8,128)(2,1)S(1)}, u32[]{:S(2)}, u32[]{:S(2)}) %collective-permute-start.5) | collective-permute-done | bytes 98336 | tf_op jit(solution)/shard_map/ppermute | solution.py:258
  92.5 0.6 fusion.5
  93.1 8.4 %all-to-all-done.2 = bf16[64,24,256]{2,1,0:T(8,128)(2,1)S(1)} async-done(((bf16[64,24,256]{2,1,0:T(8,128)(2,1)}), bf16[64,24,256]{2,1,0:T(8,128)(2,1)S(1)}, u32[]{:S(2)}, u32[]{:S(2)}) %all-to-all-start.2) | async-done | bytes 786464 | tf_op jit(solution)/shard_map/all_to_all | solution.py:253
  (28 shorter events, 2.4 us)
Async XLA Ops:
  3.1 41.4 %all-to-all-start = ((bf16[64,24,256]{2,1,0:T(8,128)(2,1)}), bf16[64,24,256]{2,1,0:T(8,128)(2,1)S(1)}, u32[]{:S(2)}, u32[]{:S(2)}) async-start(bf16[64,24,256]{2,1,0:T(8,128)(2,1)} %get-tuple-element.15), calls=%async_computation | async-start | bytes 1572864 | tf_op jit(solution)/shard_map/all_to_all | solution.py:253
  19.6 6.7 %collective-permute-start = (bf16[1,192,256]{2,1,0:T(8,128)(2,1)}, bf16[1,192,256]{2,1,0:T(8,128)(2,1)S(1)}, u32[]{:S(2)}, u32[]{:S(2)}) collective-permute-start(bf16[1,192,256]{2,1,0:T(8,128)(2,1)} %get-tuple-element.14), channel_id=1, source_target_pairs={{0,2},{1,3},{2,0},{3,1},{4,6},{5,7},{6,4},{7,5},{8,10},{9,11},{10,... | collective-permute-start | bytes 294920 | tf_op jit(solution)/shard_map/ppermute | solution.py:258
  27.2 8.8 %collective-permute-start.1 = (bf16[2,192,256]{2,1,0:T(8,128)(2,1)S(1)}, bf16[2,192,256]{2,1,0:T(8,128)(2,1)S(1)}, u32[]{:S(2)}, u32[]{:S(2)}) collective-permute-start(bf16[2,192,256]{2,1,0:T(8,128)(2,1)S(1)} %pad_maximum_fusion), channel_id=1, source_target_pairs={{0,6},{1,7},{2,4},{3,5},{4,2},{5,3},{6,0},{7,1},{8,14},{9,15},{10,... | collective-permute-start | bytes 589832 | tf_op jit(solution)/shard_map/ppermute | solution.py:258
  36.0 3.6 %collective-permute-start.2 = (bf16[4,192,256]{2,1,0:T(8,128)(2,1)S(1)}, bf16[4,192,256]{2,1,0:T(8,128)(2,1)S(1)}, u32[]{:S(2)}, u32[]{:S(2)}) collective-permute-start(bf16[4,192,256]{2,1,0:T(8,128)(2,1)S(1)} %constant_dynamic-update-slice_fusion.near_ref), channel_id=1, source_target_pairs={{0,1},{1,0},{2,3},{3,2},{4,5},{5,4},{6,7},{7,6},{8,9},{9,8},{10,11... | collective-permute-start | bytes 1179656 | tf_op jit(solution)/shard_map/ppermute | solution.py:263
  67.1 8.8 %collective-permute-start.3 = (bf16[4,24,2048]{2,1,0:T(8,128)(2,1)S(1)}, bf16[4,24,2048]{2,1,0:T(8,128)(2,1)S(1)}, u32[]{:S(2)}, u32[]{:S(2)}) collective-permute-start(bf16[4,24,2048]{2,1,0:T(8,128)(2,1)S(1)} %get-tuple-element.22), channel_id=1, source_target_pairs={{0,1},{1,0},{2,3},{3,2},{4,5},{5,4},{6,7},{7,6},{8,9},{9,8},{10,11... | collective-permute-start | bytes 1179656 | tf_op jit(solution)/shard_map/ppermute | solution.py:263
  69.0 32.5 %all-to-all-start.2 = ((bf16[64,24,256]{2,1,0:T(8,128)(2,1)}), bf16[64,24,256]{2,1,0:T(8,128)(2,1)S(1)}, u32[]{:S(2)}, u32[]{:S(2)}) async-start(bf16[64,24,256]{2,1,0:T(8,128)(2,1)} %get-tuple-element.23), calls=%async_computation.2 | async-start | bytes 1572864 | tf_op jit(solution)/shard_map/all_to_all | solution.py:253
  76.1 9.8 %collective-permute-start.4 = (bf16[2,24,2048]{2,1,0:T(8,128)(2,1)S(1)}, bf16[2,24,2048]{2,1,0:T(8,128)(2,1)S(1)}, u32[]{:S(2)}, u32[]{:S(2)}) collective-permute-start(bf16[2,24,2048]{2,1,0:T(8,128)(2,1)S(1)} %slice.54), channel_id=1, source_target_pairs={{0,6},{1,7},{2,4},{3,5},{4,2},{5,3},{6,0},{7,1},{8,14},{9,15},{10,... | collective-permute-start | bytes 589832 | tf_op jit(solution)/shard_map/ppermute | solution.py:258
  86.0 6.5 %collective-permute-start.5 = (bf16[1,24,2048]{2,1,0:T(8,128)(2,1)S(1)}, bf16[1,24,2048]{2,1,0:T(8,128)(2,1)S(1)}, u32[]{:S(2)}, u32[]{:S(2)}) collective-permute-start(bf16[1,24,2048]{2,1,0:T(8,128)(2,1)S(1)} %slice.55), channel_id=1, source_target_pairs={{0,2},{1,3},{2,0},{3,1},{4,6},{5,7},{6,4},{7,5},{8,10},{9,11},{10,... | collective-permute-start | bytes 294920 | tf_op jit(solution)/shard_map/ppermute | solution.py:258

commit v6 on v5

--- a/solution.py
+++ b/solution.py
@@ -15,11 +15,27 @@
 NT = (((1,), (1,)), ((), ()))
 
 
-def stage_rows(order_ref, sources, q_ref, d_ref, span, hd):
+def flips(mesh_x):
+    masks = [2 ** (bit + 1) - 1 for bit in range(mesh_x.bit_length() - 1)]
+    offsets = [0]
+    for mask in masks:
+        offsets = offsets + [mask ^ offset for offset in offsets]
+    return masks, offsets
+
+
+def partner(number, heads):
+    mesh_x = heads // 2
+    head = lax.axis_index("head")
+    _, offsets = flips(mesh_x)
+    change = 2 * offsets[number % mesh_x] + number // mesh_x
+    return jnp.bitwise_xor(head, jnp.int32(change))
+
+
+def stage_rows(sources, q_ref, d_ref, heads, span, hd):
     number = 0
     for src_ref in sources:
         for piece in range(src_ref.shape[0]):
-            at = pl.ds(pl.multiple_of(order_ref[number] * span, span), span)
+            at = pl.ds(pl.multiple_of(partner(number, heads) * span, span), span)
             for half in range(2):
                 rows = src_ref[piece, half * span : (half + 1) * span, :]
                 q_ref[half, at, :] = rows[:, :hd]
@@ -33,7 +49,7 @@
 
 
 def stats_kernel(
-    dims, slots_ref, tiles_ref, order_ref, kpos_ref, qpos_ref, near_ref, far_ref, kv_ref,
+    dims, slots_ref, full_ref, count_ref, kpos_ref, qpos_ref, near_ref, far_ref, kv_ref,
     stat_ref, kvs_ref, q_ref, d_ref, p_ref, s_s, sort_s,
 ):
     heads, span, hd, chunks, kc, tk, rc = dims
@@ -41,15 +57,17 @@
     half_rows = heads * span
     parts = range(half_rows // rc)
 
+    part = lax.axis_index("head") // (span // kc)
+
     def place(c, _):
-        start = pl.multiple_of(slots_ref[c] * kc, kc)
+        start = pl.multiple_of(slots_ref[2 * c + part] * kc, kc)
         sort_s[pl.ds(start, kc), :] = kv_ref[c].astype(F32)
         return 0
 
     lax.fori_loop(0, chunks, place, 0, unroll=4)
     for t in range(chunks * kc // tk):
         kvs_ref[t * tk : (t + 1) * tk, :] = sort_s[t * tk : (t + 1) * tk, :].astype(BF16)
-    stage_rows(order_ref, (near_ref, far_ref), q_ref, d_ref, span, hd)
+    stage_rows((near_ref, far_ref), q_ref, d_ref, heads, span, hd)
 
     for half in range(2):
 
@@ -67,7 +85,7 @@
                 new.append(jnp.maximum(tops[r], jnp.max(s.reshape(tk // 8, 8, rc), axis=0)))
             return tuple(new)
 
-        full, count = tiles_ref[2 * half], tiles_ref[2 * half + 1]
+        full, count = full_ref[half], count_ref[half]
         tops = tuple(jnp.full((8, rc), LOW, F32) for _ in parts)
         tops = lax.fori_loop(0, full, functools.partial(score, False), tops)
         tops = lax.fori_loop(full, count, functools.partial(score, True), tops)
@@ -100,7 +118,7 @@
 
 
 def grad_kernel(
-    dims, slots_ref, tiles_ref, order_ref, stat_ref, all_ref, q_ref, d_ref, kvs_ref, p_ref,
+    dims, slots_ref, full_ref, count_ref, stat_ref, all_ref, q_ref, d_ref, kvs_ref, p_ref,
     keep_ref, send_ref, dkv_ref, acc_s, o_s, dq_s, kvt_s, w_s, delta_s, flat_s,
 ):
     heads, span, hd, chunks, kc, tk, rc = dims
@@ -142,10 +160,12 @@
             acc_s[keys, hd:] += dv
             return 0
 
-        lax.fori_loop(0, tiles_ref[2 * half + 1], tile, 0)
+        lax.fori_loop(0, count_ref[half], tile, 0)
+
+    part = lax.axis_index("head") // (span // kc)
 
     def place(c, _):
-        start = pl.multiple_of(slots_ref[c] * kc, kc)
+        start = pl.multiple_of(slots_ref[2 * c + part] * kc, kc)
         rows = acc_s[pl.ds(start, kc), :]
         dkv_ref[c, :, :hd] = (rows[:, :hd] * scaling).astype(BF16)
         dkv_ref[c, :, hd:] = rows[:, hd:].astype(BF16)
@@ -157,7 +177,7 @@
     for which, (src, scale) in enumerate(((o_s, 1.0), (dq_s, scaling))):
         flat_s[...] = (src[...] * scale).T
         for number in range(heads):
-            target = order_ref[number]
+            target = partner(number, heads)
             half, block = target // blocks, target % blocks
             out_ref = keep_ref if number < per_core else send_ref
             for h in range(heads):
@@ -196,7 +216,7 @@
     )(query, dout, key, value)
 
 
-def run_stats(dims, slots, tiles, order, kpos, qpos, near, far, kv_all):
+def run_stats(dims, slots, full, count, kpos, qpos, near, far, kv_all):
     heads, span, hd, chunks, kc, _, _ = dims
     half_rows, n_keys = heads * span, chunks * kc
     smem = pl.BlockSpec(memory_space=pltpu.SMEM)
@@ -218,10 +238,10 @@
         ],
         compiler_params=pltpu.CompilerParams(vmem_limit_bytes=32 * 1024 * 1024),
         name="attention_stats",
-    )(slots, tiles, order, kpos, qpos, near, far, kv_all)
-
-
-def run_grads(dims, slots, tiles, order, stat, stat_all, q, d, kvs, probs):
+    )(slots, full, count, kpos, qpos, near, far, kv_all)
+
+
+def run_grads(dims, slots, full, count, stat, stat_all, q, d, kvs, probs):
     heads, span, hd, chunks, kc, _, _ = dims
     rows, n_keys = 2 * heads * span, chunks * kc
     smem = pl.BlockSpec(memory_space=pltpu.SMEM)
@@ -246,7 +266,7 @@
         ],
         compiler_params=pltpu.CompilerParams(vmem_limit_bytes=32 * 1024 * 1024),
         name="attention_grads",
-    )(slots, tiles, order, stat, stat_all, q, d, kvs, probs)
+    )(slots, full, count, stat, stat_all, q, d, kvs, probs)
 
 
 def exchange(x, axis):
@@ -279,41 +299,40 @@
     head = lax.axis_index("head")
 
     mesh_x = heads // 2
-    at_x, core = head // 2, head % 2
-    masks = [2 ** (bit + 1) - 1 for bit in range(mesh_x.bit_length() - 1)]
-    offsets = [0]
-    for mask in masks:
-        offsets = offsets + [mask ^ offset for offset in offsets]
-    origin = jnp.bitwise_xor(at_x, jnp.array(offsets, jnp.int32)) * 2
-    order = jnp.concatenate([origin + core, origin + 1 - core]).astype(jnp.int32)
-
-    spans = span_of.reshape(shards, 2)
-    key_span = lax.dynamic_index_in_dim(spans, head // blocks, 1, keepdims=False)
-    own = lax.dynamic_index_in_dim(spans, ctx, 0, keepdims=False)
-    rank = jnp.sum((key_span[None, :] < key_span[:, None]).astype(jnp.int32), axis=1)
-    place = jnp.arange(shards, dtype=jnp.int32)
-    ordered = jnp.sum(jnp.where(rank[None, :] == place[:, None], key_span[None, :], 0), axis=1)
+    part = head // blocks
+    own = lax.dynamic_slice_in_dim(span_of, 2 * ctx, 2)
+    block = jnp.arange(2 * shards, dtype=jnp.int32)
+    mine = block % 2 == part
+    below = mine[None, :] & (span_of[None, :] < span_of[:, None])
+    rank = jnp.sum(below.astype(jnp.int32), axis=1)
+    slot = jnp.arange(shards, dtype=jnp.int32)
+    here = mine[None, :] & (rank[None, :] == slot[:, None])
+    ordered = jnp.sum(jnp.where(here, span_of[None, :], 0), axis=1)
     kpos = (
         ordered[:, None] * span
         + (head % blocks) * kc
         + jnp.arange(kc, dtype=jnp.int32)[None, :]
     ).reshape(n_keys, 1)
     qpos = own[:, None] * span + jnp.tile(jnp.arange(span, dtype=jnp.int32), heads)[None, :]
-    before = jnp.sum((key_span[None, :] < own[:, None]).astype(jnp.int32), axis=1) * kc
-    seen = jnp.sum((key_span[None, :] <= own[:, None]).astype(jnp.int32), axis=1) * kc
-    tiles = jnp.stack([before // tk, (seen + tk - 1) // tk], axis=1).reshape(4)
+    before = mine[None, :] & (span_of[None, :] < own[:, None])
+    seen = mine[None, :] & (span_of[None, :] <= own[:, None])
+    before = jnp.sum(before.astype(jnp.int32), axis=1) * kc
+    seen = jnp.sum(seen.astype(jnp.int32), axis=1) * kc
+    full = before // tk
+    count = (seen + tk - 1) // tk
 
     near, kv_all = run_pack(shards, query_in, grad_out, key_in, value_in)
     kv_all = exchange(kv_all, "ctx")
+    masks, _ = flips(mesh_x)
     for mask in masks:
         near = jnp.concatenate([near, flip_x(near, mesh_x, mask)])
     far = swap_cores(near, mesh_x)
 
-    stat, kvs, q, d, probs = run_stats(dims, rank, tiles, order, kpos, qpos, near, far, kv_all)
+    stat, kvs, q, d, probs = run_stats(dims, rank, full, count, kpos, qpos, near, far, kv_all)
     rows = 2 * heads * span
     stat_all = exchange(jnp.broadcast_to(stat[None, :2], (heads, 2, rows)), "head")
     keep, send, key_parts = run_grads(
-        dims, rank, tiles, order, stat, stat_all, q, d, kvs, probs
+        dims, rank, full, count, stat, stat_all, q, d, kvs, probs
     )
     key_parts = exchange(key_parts, "ctx")
 

time: 103 us -> 103 us (level)
  Pallas kernels: 16.7 us -> 14.1 us
  other arithmetic: 2.6 us -> 4.63 us
  blocking collectives: 8.37 us -> 9.89 us
  local copies, waits for them, and re-layouts: 3.72 us -> 2.59 us
    reduce_sum x3, other arithmetic: 0.47 us -> 2.54 us  [the longest x1 0.9 us: local(): rank = jnp.sum(below.astype(jnp.int32), axis=1)]
    pallas_call x1, Pallas kernels: 8.24 us -> 6.69 us  [run_grads(): pl.pallas_call(functools.partial(grad_kernel, dims), out_shape=(jax.Shape...]
    all_to_all x1, blocking collectives: 8.37 us -> 9.89 us  [exchange(): return lax.all_to_all(x, axis, split_axis=0, concat_axis=0, tiled=True)]
    all_to_all x2, starting transfers between devices: 23.4 us -> 24.5 us  [exchange(): return lax.all_to_all(x, axis, split_axis=0, concat_axis=0, tiled=True)]
    pallas_call x1, Pallas kernels: 6 us -> 4.92 us  [run_stats(): pl.pallas_call(functools.partial(stats_kernel, dims), out_shape=(jax.Shap...]
  transfers between devices with their start and end apart: 8 -> 8, of which waited for: 7 -> 6; matrix products, arithmetic and copies ran while one was open for 5% -> 6% of each run, Pallas kernels for 0% -> 0%
where the time goes in v6:
time: 103 us; the launch traced here: 102 us
  starting transfers between devices  39.7 us (39%)
  waiting for transfers between devices  30.5 us (30%)
  Pallas kernels  14.1 us (14%)
  blocking collectives  9.89 us (10%)
  other arithmetic  4.63 us (4%)
  local copies, waits for them, and re-layouts  2.59 us (3%)
    all_to_all x2, starting transfers between devices, exchange(): return lax.all_to_all(x, axis, split_axis=0, concat_axis=0, tiled=True)  24.5 us
    ppermute x4, waiting for transfers between devices, flip_x(): return lax.ppermute(x, 'head', pairs)  16.3 us
    all_to_all x2, waiting for transfers between devices, exchange(): return lax.all_to_all(x, axis, split_axis=0, concat_axis=0, tiled=True)  12.6 us
    ppermute x4, starting transfers between devices, flip_x(): return lax.ppermute(x, 'head', pairs)  11.4 us
    all_to_all x1, blocking collectives, exchange(): return lax.all_to_all(x, axis, split_axis=0, concat_axis=0, tiled=True)  9.89 us
    pallas_call x1, Pallas kernels, run_grads(): pl.pallas_call(functools.partial(grad_kernel, dims), out_shape=(jax.Shape...  6.69 us
    pallas_call x1, Pallas kernels, run_stats(): pl.pallas_call(functools.partial(stats_kernel, dims), out_shape=(jax.Shap...  4.92 us
    ppermute x2, starting transfers between devices, swap_cores(): return lax.ppermute(x, 'head', pairs)  3.83 us
  transfers between devices with their start and end apart: 8, of which 6 were waited for; matrix products, arithmetic and copies ran while one was open for 6% of the time, Pallas kernels for 0%

profile of v6, /device:TPU:16, one launch (start us, length us, event | category | flops | bytes accessed | tf_op | source)
XLA Modules:
  0.0 102.3 jit_solution(14420851328591256533)
XLA Ops:
  0.6 2.5 %attention_pack.1 = (bf16[1,192,256]{2,1,0:T(8,128)(2,1)}, bf16[64,24,256]{2,1,0:T(8,128)(2,1)}) custom-call(bf16[192,128]{1,0:T(8,128)(2,1)} %q_ref.1, bf16[192,128]{1,0:T(8,128)(2,1)} %d_ref.1, bf16[24,128]{1,0:T(8,128)(2,1)} %k_ref.1, bf16[24,128]{1,0:T(8,128)(2,1)} %v_ref.1), custom_call_target="tpu_custom_call" | custom-call | tf_op jit(solution)/shard_map/attention_pack/pallas_call | solution.py:205
  3.1 16.5 %all-to-all-start = ((bf16[64,24,256]{2,1,0:T(8,128)(2,1)}), bf16[64,24,256]{2,1,0:T(8,128)(2,1)S(1)}, u32[]{:S(2)}, u32[]{:S(2)}) async-start(bf16[64,24,256]{2,1,0:T(8,128)(2,1)} %get-tuple-element.15), calls=%async_computation | async-start | bytes 1572864 | tf_op jit(solution)/shard_map/all_to_all | solution.py:273
  19.6 3.4 %collective-permute-start = (bf16[1,192,256]{2,1,0:T(8,128)(2,1)}, bf16[1,192,256]{2,1,0:T(8,128)(2,1)S(1)}, u32[]{:S(2)}, u32[]{:S(2)}) collective-permute-start(bf16[1,192,256]{2,1,0:T(8,128)(2,1)} %get-tuple-element.14), channel_id=1, source_target_pairs={{0,2},{1,3},{2,0},{3,1},{4,6},{5,7},{6,4},{7,5},{8,10},{9,11},{10,... | collective-permute-start | bytes 294920 | tf_op jit(solution)/shard_map/ppermute | solution.py:278
  23.0 0.9 convert_reduce_fusion.slots_ref
  23.9 0.8 select_reduce_fusion
  25.2 0.9 constant_dynamic-update-slice_fusion.2
  26.1 0.7 broadcast_multiply_fusion
  26.8 0.9 pad_maximum_fusion
  27.7 4.2 %collective-permute-start.1 = (bf16[2,192,256]{2,1,0:T(8,128)(2,1)S(1)}, bf16[2,192,256]{2,1,0:T(8,128)(2,1)S(1)}, u32[]{:S(2)}, u32[]{:S(2)}) collective-permute-start(bf16[2,192,256]{2,1,0:T(8,128)(2,1)S(1)} %pad_maximum_fusion), channel_id=1, source_target_pairs={{0,6},{1,7},{2,4},{3,5},{4,2},{5,3},{6,0},{7,1},{8,14},{9,15},{10,... | collective-permute-start | bytes 589832 | tf_op jit(solution)/shard_map/ppermute | solution.py:278
  31.9 0.9 fusion.4
  32.8 3.8 %collective-permute-done.1 = bf16[2,192,256]{2,1,0:T(8,128)(2,1)S(1)} collective-permute-done((bf16[2,192,256]{2,1,0:T(8,128)(2,1)S(1)}, bf16[2,192,256]{2,1,0:T(8,128)(2,1)S(1)}, u32[]{:S(2)}, u32[]{:S(2)}) %collective-permute-start.1) | collective-permute-done | bytes 196640 | tf_op jit(solution)/shard_map/ppermute | solution.py:278
  36.6 1.9 %collective-permute-start.2 = (bf16[4,192,256]{2,1,0:T(8,128)(2,1)S(1)}, bf16[4,192,256]{2,1,0:T(8,128)(2,1)S(1)}, u32[]{:S(2)}, u32[]{:S(2)}) collective-permute-start(bf16[4,192,256]{2,1,0:T(8,128)(2,1)S(1)} %constant_dynamic-update-slice_fusion.near_ref), channel_id=1, source_target_pairs={{0,1},{1,0},{2,3},{3,2},{4,5},{5,4},{6,7},{7,6},{8,9},{9,8},{10,11... | collective-permute-start | bytes 1179656 | tf_op jit(solution)/shard_map/ppermute | solution.py:283
  38.7 1.6 %collective-permute-done.2.far_ref = bf16[4,192,256]{2,1,0:T(8,128)(2,1)S(1)} collective-permute-done((bf16[4,192,256]{2,1,0:T(8,128)(2,1)S(1)}, bf16[4,192,256]{2,1,0:T(8,128)(2,1)S(1)}, u32[]{:S(2)}, u32[]{:S(2)}) %collective-permute-start.2) | collective-permute-done | bytes 393248 | tf_op jit(solution)/shard_map/ppermute | solution.py:283
  40.3 4.2 %all-to-all-done.kv_ref = bf16[64,24,256]{2,1,0:T(8,128)(2,1)S(1)} async-done(((bf16[64,24,256]{2,1,0:T(8,128)(2,1)}), bf16[64,24,256]{2,1,0:T(8,128)(2,1)S(1)}, u32[]{:S(2)}, u32[]{:S(2)}) %all-to-all-start) | async-done | bytes 786464 | tf_op jit(solution)/shard_map/all_to_all | solution.py:273
  44.5 4.9 %attention_stats.1 = (f32[3,1536]{1,0:T(4,128)S(1)}, bf16[1536,256]{1,0:T(8,128)(2,1)S(1)}, bf16[2,768,128]{2,1,0:T(8,128)(2,1)S(1)}, bf16[2,768,128]{2,1,0:T(8,128)(2,1)S(1)}, bf16[1536,1536]{1,0:T(8,128)(2,1)S(1)}) custom-call(s32[128]{0:T(128)S(1)} %convert_reduce_fusion.slots_ref, s32[2]{0:T(128)S(1)} %get-tuple-element.33.full_ref, ...), custom_call_target="tpu_custom_call" | custom-call | tf_op jit(solution)/shard_map/attention_stats/pallas_call | solution.py:224
  49.4 9.9 %all_to_all.15.all_ref = f32[8,2,1536]{2,1,0:T(2,128)S(1)} all-to-all(f32[8,2,1536]{2,1,0:T(2,128)S(1)} %broadcast_in_dim.16), channel_id=1, replica_groups=mesh['ctx'=64,'head'=8] {'head'}, dimensions={0} | all-to-all | bytes 196608 | tf_op jit(solution)/shard_map/all_to_all | solution.py:273
  59.3 6.7 %attention_grads.1 = (bf16[4,24,2048]{2,1,0:T(8,128)(2,1)S(1)}, bf16[4,24,2048]{2,1,0:T(8,128)(2,1)S(1)}, bf16[64,24,256]{2,1,0:T(8,128)(2,1)}) custom-call(s32[128]{0:T(128)S(1)} %convert_reduce_fusion.slots_ref, s32[2]{0:T(128)S(1)} %get-tuple-element.33.full_ref, s32[2]{0:T(128)S(1)} %get-tuple-element.32.count_ref, ...), custom_call_target="tpu_custom_call" | custom-call | tf_op jit(solution)/shard_map/attention_grads/pallas_call | solution.py:249
  66.0 1.9 %collective-permute-start.3 = (bf16[4,24,2048]{2,1,0:T(8,128)(2,1)S(1)}, bf16[4,24,2048]{2,1,0:T(8,128)(2,1)S(1)}, u32[]{:S(2)}, u32[]{:S(2)}) collective-permute-start(bf16[4,24,2048]{2,1,0:T(8,128)(2,1)S(1)} %get-tuple-element.22), channel_id=1, source_target_pairs={{0,1},{1,0},{2,3},{3,2},{4,5},{5,4},{6,7},{7,6},{8,9},{9,8},{10,11... | collective-permute-start | bytes 1179656 | tf_op jit(solution)/shard_map/ppermute | solution.py:283
  67.9 8.0 %all-to-all-start.2 = ((bf16[64,24,256]{2,1,0:T(8,128)(2,1)}), bf16[64,24,256]{2,1,0:T(8,128)(2,1)S(1)}, u32[]{:S(2)}, u32[]{:S(2)}) async-start(bf16[64,24,256]{2,1,0:T(8,128)(2,1)} %get-tuple-element.23), calls=%async_computation.2 | async-start | bytes 1572864 | tf_op jit(solution)/shard_map/all_to_all | solution.py:273
  76.1 1.9 %collective-permute-start.4 = (bf16[2,24,2048]{2,1,0:T(8,128)(2,1)S(1)}, bf16[2,24,2048]{2,1,0:T(8,128)(2,1)S(1)}, u32[]{:S(2)}, u32[]{:S(2)}) collective-permute-start(bf16[2,24,2048]{2,1,0:T(8,128)(2,1)S(1)} %slice.54), channel_id=1, source_target_pairs={{0,6},{1,7},{2,4},{3,5},{4,2},{5,3},{6,0},{7,1},{8,14},{9,15},{10,... | collective-permute-start | bytes 589832 | tf_op jit(solution)/shard_map/ppermute | solution.py:278
  78.0 7.9 %collective-permute-done.4 = bf16[2,24,2048]{2,1,0:T(8,128)(2,1)S(1)} collective-permute-done((bf16[2,24,2048]{2,1,0:T(8,128)(2,1)S(1)}, bf16[2,24,2048]{2,1,0:T(8,128)(2,1)S(1)}, u32[]{:S(2)}, u32[]{:S(2)}) %collective-permute-start.4) | collective-permute-done | bytes 196640 | tf_op jit(solution)/shard_map/ppermute | solution.py:278
  86.0 1.9 %collective-permute-start.5 = (bf16[1,24,2048]{2,1,0:T(8,128)(2,1)S(1)}, bf16[1,24,2048]{2,1,0:T(8,128)(2,1)S(1)}, u32[]{:S(2)}, u32[]{:S(2)}) collective-permute-start(bf16[1,24,2048]{2,1,0:T(8,128)(2,1)S(1)} %slice.55), channel_id=1, source_target_pairs={{0,2},{1,3},{2,0},{3,1},{4,6},{5,7},{6,4},{7,5},{8,10},{9,11},{10,... | collective-permute-start | bytes 294920 | tf_op jit(solution)/shard_map/ppermute | solution.py:278
  87.9 4.6 %collective-permute-done.5 = bf16[1,24,2048]{2,1,0:T(8,128)(2,1)S(1)} collective-permute-done((bf16[1,24,2048]{2,1,0:T(8,128)(2,1)S(1)}, bf16[1,24,2048]{2,1,0:T(8,128)(2,1)S(1)}, u32[]{:S(2)}, u32[]{:S(2)}) %collective-permute-start.5) | collective-permute-done | bytes 98336 | tf_op jit(solution)/shard_map/ppermute | solution.py:278
  93.2 8.4 %all-to-all-done.2 = bf16[64,24,256]{2,1,0:T(8,128)(2,1)S(1)} async-done(((bf16[64,24,256]{2,1,0:T(8,128)(2,1)}), bf16[64,24,256]{2,1,0:T(8,128)(2,1)S(1)}, u32[]{:S(2)}, u32[]{:S(2)}) %all-to-all-start.2) | async-done | bytes 786464 | tf_op jit(solution)/shard_map/all_to_all | solution.py:273
  (22 shorter events, 2.1 us)
Async XLA Ops:
  3.1 41.4 %all-to-all-start = ((bf16[64,24,256]{2,1,0:T(8,128)(2,1)}), bf16[64,24,256]{2,1,0:T(8,128)(2,1)S(1)}, u32[]{:S(2)}, u32[]{:S(2)}) async-start(bf16[64,24,256]{2,1,0:T(8,128)(2,1)} %get-tuple-element.15), calls=%async_computation | async-start | bytes 1572864 | tf_op jit(solution)/shard_map/all_to_all | solution.py:273
  19.6 7.2 %collective-permute-start = (bf16[1,192,256]{2,1,0:T(8,128)(2,1)}, bf16[1,192,256]{2,1,0:T(8,128)(2,1)S(1)}, u32[]{:S(2)}, u32[]{:S(2)}) collective-permute-start(bf16[1,192,256]{2,1,0:T(8,128)(2,1)} %get-tuple-element.14), channel_id=1, source_target_pairs={{0,2},{1,3},{2,0},{3,1},{4,6},{5,7},{6,4},{7,5},{8,10},{9,11},{10,... | collective-permute-start | bytes 294920 | tf_op jit(solution)/shard_map/ppermute | solution.py:278
  27.7 8.9 %collective-permute-start.1 = (bf16[2,192,256]{2,1,0:T(8,128)(2,1)S(1)}, bf16[2,192,256]{2,1,0:T(8,128)(2,1)S(1)}, u32[]{:S(2)}, u32[]{:S(2)}) collective-permute-start(bf16[2,192,256]{2,1,0:T(8,128)(2,1)S(1)} %pad_maximum_fusion), channel_id=1, source_target_pairs={{0,6},{1,7},{2,4},{3,5},{4,2},{5,3},{6,0},{7,1},{8,14},{9,15},{10,... | collective-permute-start | bytes 589832 | tf_op jit(solution)/shard_map/ppermute | solution.py:278
  36.6 3.6 %collective-permute-start.2 = (bf16[4,192,256]{2,1,0:T(8,128)(2,1)S(1)}, bf16[4,192,256]{2,1,0:T(8,128)(2,1)S(1)}, u32[]{:S(2)}, u32[]{:S(2)}) collective-permute-start(bf16[4,192,256]{2,1,0:T(8,128)(2,1)S(1)} %constant_dynamic-update-slice_fusion.near_ref), channel_id=1, source_target_pairs={{0,1},{1,0},{2,3},{3,2},{4,5},{5,4},{6,7},{7,6},{8,9},{9,8},{10,11... | collective-permute-start | bytes 1179656 | tf_op jit(solution)/shard_map/ppermute | solution.py:283
  66.0 9.9 %collective-permute-start.3 = (bf16[4,24,2048]{2,1,0:T(8,128)(2,1)S(1)}, bf16[4,24,2048]{2,1,0:T(8,128)(2,1)S(1)}, u32[]{:S(2)}, u32[]{:S(2)}) collective-permute-start(bf16[4,24,2048]{2,1,0:T(8,128)(2,1)S(1)} %get-tuple-element.22), channel_id=1, source_target_pairs={{0,1},{1,0},{2,3},{3,2},{4,5},{5,4},{6,7},{7,6},{8,9},{9,8},{10,11... | collective-permute-start | bytes 1179656 | tf_op jit(solution)/shard_map/ppermute | solution.py:283
  67.9 33.6 %all-to-all-start.2 = ((bf16[64,24,256]{2,1,0:T(8,128)(2,1)}), bf16[64,24,256]{2,1,0:T(8,128)(2,1)S(1)}, u32[]{:S(2)}, u32[]{:S(2)}) async-start(bf16[64,24,256]{2,1,0:T(8,128)(2,1)} %get-tuple-element.23), calls=%async_computation.2 | async-start | bytes 1572864 | tf_op jit(solution)/shard_map/all_to_all | solution.py:273
  76.1 9.8 %collective-permute-start.4 = (bf16[2,24,2048]{2,1,0:T(8,128)(2,1)S(1)}, bf16[2,24,2048]{2,1,0:T(8,128)(2,1)S(1)}, u32[]{:S(2)}, u32[]{:S(2)}) collective-permute-start(bf16[2,24,2048]{2,1,0:T(8,128)(2,1)S(1)} %slice.54), channel_id=1, source_target_pairs={{0,6},{1,7},{2,4},{3,5},{4,2},{5,3},{6,0},{7,1},{8,14},{9,15},{10,... | collective-permute-start | bytes 589832 | tf_op jit(solution)/shard_map/ppermute | solution.py:278
  86.0 6.5 %collective-permute-start.5 = (bf16[1,24,2048]{2,1,0:T(8,128)(2,1)S(1)}, bf16[1,24,2048]{2,1,0:T(8,128)(2,1)S(1)}, u32[]{:S(2)}, u32[]{:S(2)}) collective-permute-start(bf16[1,24,2048]{2,1,0:T(8,128)(2,1)S(1)} %slice.55), channel_id=1, source_target_pairs={{0,2},{1,3},{2,0},{3,1},{4,6},{5,7},{6,4},{7,5},{8,10},{9,11},{10,... | collective-permute-start | bytes 294920 | tf_op jit(solution)/shard_map/ppermute | solution.py:278
